TPU v7x, 32 devices: a whole 2x2x4 slice. The times are simulated.
32 devices in a mesh: pb: 8 (over y, x, core), ka: 4 (over z).
Axes of the slice: x: 2, y: 2, z: 4, core: 2. Of those that a mesh axis runs over, the one named last changes fastest.
Arguments:
- queries: bfloat16 [4096, 4096], P('pb'), may hold values from -6 to 6
- key_rows: bfloat16 [4096, 512], P(('pb', 'ka')), may hold values from -6 to 6
- values: bfloat16 [4096, 512], P(('pb', 'ka')), may hold values from -6 to 6
- attn_out: bfloat16 [4096, 4096], P(('pb', 'ka')), may hold values from -6 to 6
- grad_out: bfloat16 [4096, 4096], P('pb'), may hold values from -6 to 6
- log_sums: float32 [32, 4096], P(None, ('pb', 'ka')), may hold values from 3 to 7
- key_gain: float32 [512], replicated, may hold values from 0.25 to 1.75
- value_gain: float32 [512], replicated, may hold values from 0.25 to 1.75
- doc_ids: int32 [32], replicated, may hold values from 0 to 3, never falling along the last dimension, each value on 1 to 16 neighbouring positions
- tile_mask: int32 [32, 32], replicated, may hold values 0 or 1
- block_order: int32 [32], replicated, may hold values from 0 to 31, each once
Outputs:
- grad_queries: bfloat16 [4096, 4096], P(('pb', 'ka'))
- grad_keys: bfloat16 [4096, 512], P(('pb', 'ka'))
- grad_values: bfloat16 [4096, 512], P(('pb', 'ka'))
- grad_key_gain: float32 [512], replicated
- grad_value_gain: float32 [512], replicated
Inputs may be any that keep to these rules, and one draw needn't show every extreme that they name: `doc_ids`: documents are numbered in sequence order; each spans 1 to 16 tiles, one exactly that many. `block_order`: each sequence tile once.
All inputs are finite; a program needn't handle non-finite values.
Results may differ from a plain program's by a relative error of at most 0.015.
Values may be sent and summed in bfloat16 or wider, within the bound.
No kernel may reach another device: no remote copies, remote signals or barrier semaphores. Data moves between devices by JAX's collectives and lax.ppermute only.
A program may use at most 192 MiB of HBM per device.

v0:
```python
import functools

import jax
import jax.numpy as jnp
from jax import lax
from jax.experimental import pallas as pl
from jax.experimental.pallas import tpu as pltpu
from jax.sharding import PartitionSpec as P

HEAD_DIM = 128
TILE = 128
SPARE = 16
LOG2E = 1.4426950408889634
VMEM = pltpu.VMEM
SMEM = pltpu.SMEM
F32 = jnp.float32
BF16 = jnp.bfloat16


def split_three(x):
    high = x.astype(BF16).astype(F32)
    rest = x - high
    middle = rest.astype(BF16).astype(F32)
    low = (rest - middle).astype(BF16).astype(F32)
    return high, middle, low


def head_rows(heads_dev):
    return -(-heads_dev // 8) * 8


def extra_rows(heads_dev):
    return -(-3 * head_rows(heads_dev) // 16) * 16


def prepare_kernel(dims, place_ref, key_ref, value_ref, attn_ref, grad_ref, lse_ref, *rest):
    count_ka, heads, heads_dev, share = dims
    outs, (lse_pad, delta_pad) = rest[:count_ka], rest[count_ka:]
    place_ka = place_ref[1]
    rows8 = head_rows(heads_dev)
    lanes = lax.broadcasted_iota(jnp.int32, (TILE, TILE), 1)
    columns = jnp.zeros((TILE, TILE), F32)
    for head in range(heads):
        part = pl.ds(head * HEAD_DIM, HEAD_DIM)
        products = grad_ref[:, part].astype(F32) * attn_ref[:, part].astype(F32)
        total = jnp.sum(products, axis=1, keepdims=True)
        columns = jnp.where(lanes == head, total, columns)
    delta_pad[...] = jnp.zeros_like(delta_pad)
    lse_pad[...] = jnp.zeros_like(lse_pad)
    delta_pad[:heads, :] = columns.T[:heads, :]
    lse_pad[:heads, :] = lse_ref[...]
    filler = extra_rows(heads_dev) - 3 * rows8
    for step in range(count_ka):
        target = lax.rem(place_ka + step, count_ka)
        kv_at = pl.ds(pl.multiple_of(target // share * HEAD_DIM, HEAD_DIM), HEAD_DIM)
        outs[step][:TILE, :HEAD_DIM] = key_ref[:, kv_at]
        outs[step][:TILE, HEAD_DIM:] = value_ref[:, kv_at]
        head_at = pl.ds(target * heads_dev, rows8)
        both = jnp.concatenate([lse_pad[head_at, :], delta_pad[head_at, :]], axis=1)
        terms = list(split_three(both))
        if filler:
            terms.append(jnp.zeros((filler, 2 * HEAD_DIM), F32))
        outs[step][TILE:, :] = jnp.concatenate(terms, axis=0).astype(BF16)


def own_heads_kernel(place_ref, queries_ref, grads_ref, out_ref):
    for number, ref in enumerate((queries_ref, grads_ref)):
        for head in range(ref.shape[1] // HEAD_DIM):
            part = pl.ds(head * HEAD_DIM, HEAD_DIM)
            tile = ref[:, part]
            out_ref[number, 0, part, :] = tile
            out_ref[2 + number, 0, part, :] = tile.T


def attention_kernel(dims, place_ref, order_ref, doc_ref, mask_ref, *rest):
    count_chip, count_ka, heads_dev, share, stage, steps = dims
    key_tiles = count_chip * count_ka
    if stage == 0:
        (key_gain_ref, value_gain_ref), rest = rest[:2], rest[2:]
    (heads_ref, stats_ref), rest = rest[:2], rest[2:]
    if stage != 1:
        blocks, rest = rest[:count_chip], rest[count_chip:]
    if stage == 0:
        (dq_out, keys, values, keys_t, key_sum, value_sum), rest = rest[:6], rest[6:]
    else:
        (keys, values, keys_t, key_start, value_start), rest = rest[:5], rest[5:]
    if stage == 1:
        dq_outs, rest = rest[:len(steps)], rest[len(steps):]
        (key_sum, value_sum), rest = rest[:2], rest[2:]
    if stage == 2:
        dq_back, rest = rest[0], rest[1:]
        dq_outs, rest = rest[:len(steps)], rest[len(steps):]
        kv_outs, rest = rest[:count_chip], rest[count_chip:]
        (key_sum, value_sum), rest = rest[:2], rest[2:]
    (lse_delta, weights_low, dscores_low, dq_turn, live_list, limit_list) = rest
    place_pb, place_ka = place_ref[0], place_ref[1]
    query_pb = place_pb if stage else place_pb ^ 1
    rows8 = head_rows(heads_dev)
    spare = extra_rows(heads_dev)
    score_scale = HEAD_DIM ** -0.5

    if stage == 0:
        kv_at = pl.ds(pl.multiple_of(place_ka // share * HEAD_DIM, HEAD_DIM), HEAD_DIM)
        key_gain = key_gain_ref[:, kv_at]
        value_gain = value_gain_ref[:, kv_at]
        for number in range(count_chip):
            for step in range(count_ka):
                part = pl.ds(step * TILE, TILE)
                local = number * count_ka + step
                key_tile = (blocks[number][part, :HEAD_DIM].astype(F32) * key_gain).astype(BF16)
                value_tile = (blocks[number][part, HEAD_DIM:].astype(F32) * value_gain).astype(BF16)
                keys[local] = key_tile
                values[local] = value_tile
                keys_t[local] = key_tile.T
        key_sum[...] = jnp.zeros_like(key_sum)
        value_sum[...] = jnp.zeros_like(value_sum)
    else:
        key_sum[...] = key_start[...]
        value_sum[...] = value_start[...]

    reach = (lax.broadcasted_iota(jnp.int32, (TILE, TILE), 1)
             - lax.broadcasted_iota(jnp.int32, (TILE, TILE), 0))
    reach = jnp.concatenate([reach, reach], axis=0)
    reach = jnp.concatenate([reach, reach], axis=1)
    lower = lax.broadcasted_iota(jnp.int32, (2 * TILE, 2 * TILE), 0) < TILE

    def query_step(turn_q, carry):
        step_q = jnp.int32(steps[0])
        for number, step in enumerate(steps):
            step_q = jnp.where(turn_q == number, step, step_q)
        tile_at = lax.rem(place_ka + step_q, count_ka)
        seq_q = order_ref[query_pb * count_ka + tile_at]
        doc_q = doc_ref[seq_q]

        def collect(local, count):
            number = local // count_ka
            step = lax.rem(local, count_ka)
            stored = ((place_pb ^ (2 * number)) * count_ka
                      + lax.rem(place_ka - step + count_ka, count_ka))
            seq_k = order_ref[stored]
            live = (mask_ref[seq_q, seq_k] == 1) & (doc_ref[seq_k] == doc_q) & (seq_q >= seq_k)
            live_list[count] = local
            limit_list[count] = jnp.where(seq_q == seq_k, 0, -TILE)
            return count + live.astype(jnp.int32)

        live_count = lax.fori_loop(0, key_tiles, collect, jnp.int32(0))
        live_list[live_count] = 0
        limit_list[live_count] = TILE

        slot = lax.rem(place_ka - tile_at + count_ka, count_ka)
        packed = stats_ref[pl.ds(pl.multiple_of(slot * spare, spare), spare), :].astype(F32)
        lse_delta[...] = (packed[:rows8] + packed[rows8:2 * rows8]) + packed[2 * rows8:3 * rows8]
        dq_turn[...] = jnp.zeros_like(dq_turn)

        def pair_step(at, carry):
            first, second = live_list[2 * at], live_list[2 * at + 1]
            limits = jnp.where(lower, limit_list[2 * at], limit_list[2 * at + 1])
            allowed = reach >= limits
            key_pair = jnp.concatenate([keys[first], keys[second]], axis=0)
            value_pair = jnp.concatenate([values[first], values[second]], axis=0)
            key_turn = jnp.concatenate([keys_t[first], keys_t[second]], axis=1)
            for head in range(0, heads_dev, 2):
                part = pl.ds(head * HEAD_DIM, 2 * HEAD_DIM)
                q_turn, o_turn = [
                    jnp.concatenate(
                        [heads_ref[kind, tile_at, pl.ds(at * HEAD_DIM, HEAD_DIM), :] for at in (head, head + 1)],
                        axis=1,
                    )
                    for kind in (2, 3)
                ]
                scores = jnp.dot(key_pair, q_turn, preferred_element_type=F32)
                dweights = jnp.dot(value_pair, o_turn, preferred_element_type=F32)
                lse_row = jnp.concatenate([lse_delta[at:at + 1, :TILE] for at in (head, head + 1)], axis=1)
                delta_row = jnp.concatenate([lse_delta[at:at + 1, TILE:] for at in (head, head + 1)], axis=1)
                weights = jnp.exp2(scores * (score_scale * LOG2E) - lse_row * LOG2E)
                weights = jnp.where(allowed, weights, 0.0)
                weights_low[:, part] = weights.astype(BF16)
                dscores_low[:, part] = (weights * (dweights - delta_row)).astype(BF16)
            value_term = jnp.dot(weights_low[...], heads_ref[1, tile_at], preferred_element_type=F32)
            key_term = jnp.dot(dscores_low[...], heads_ref[0, tile_at], preferred_element_type=F32)
            dq_turn[...] += jnp.dot(key_turn, dscores_low[...], preferred_element_type=F32)
            key_sum[first] += key_term[:TILE]
            value_sum[first] += value_term[:TILE]
            key_sum[second] += key_term[TILE:]
            value_sum[second] += value_term[TILE:]
            return carry

        lax.fori_loop(0, (live_count + 1) // 2, pair_step, 0)
        tile_grad = dq_turn[...] * score_scale
        if stage == 0:
            dq_out[tile_at] = tile_grad.astype(BF16)
            return carry
        if stage == 2:
            tile_grad = tile_grad + dq_back[tile_at].astype(F32)
        for number in range(len(steps)):
            @pl.when(turn_q == number)
            def _():
                dq_outs[number][...] = tile_grad.astype(dq_outs[number].dtype)
        return carry

    lax.fori_loop(0, len(steps), query_step, 0)
    if stage != 2:
        return

    key_gains = jnp.zeros((8, HEAD_DIM), F32)
    value_gains = jnp.zeros((8, HEAD_DIM), F32)
    for number in range(count_chip):
        for step in range(count_ka):
            part = pl.ds(step * TILE, TILE)
            local = number * count_ka + step
            key_total = key_sum[local] * score_scale
            value_total = value_sum[local]
            kv_outs[number][part, :HEAD_DIM] = key_total.astype(kv_outs[number].dtype)
            kv_outs[number][part, HEAD_DIM:] = value_total.astype(kv_outs[number].dtype)
            key_raw = blocks[number][part, :HEAD_DIM].astype(F32)
            value_raw = blocks[number][part, HEAD_DIM:].astype(F32)
            key_gains += jnp.sum((key_total * key_raw).reshape(TILE // 8, 8, HEAD_DIM), axis=0)
            value_gains += jnp.sum((value_total * value_raw).reshape(TILE // 8, 8, HEAD_DIM), axis=0)
    gains = jnp.concatenate([jnp.sum(key_gains, axis=0, keepdims=True),
                             jnp.sum(value_gains, axis=0, keepdims=True)], axis=1)
    packed = pack_gains(gains)
    for number in range(count_chip):
        kv_outs[number][count_ka * TILE:, :] = packed.astype(kv_outs[number].dtype)


def pack_gains(gains):
    rows = lax.broadcasted_iota(jnp.int32, (SPARE, gains.shape[1]), 0)
    high, middle, low = split_three(gains)
    packed = jnp.where(rows == 0, high, jnp.where(rows == 1, middle, low))
    return jnp.where(rows < 3, packed, 0.0)


def add_kernel(dims, place_ref, other_ref, *rest):
    count_ka, steps = dims
    parts, outs = rest[:len(steps)], rest[len(steps):]
    for number, step in enumerate(steps):
        tile_at = lax.rem(place_ref[1] + step, count_ka)
        outs[number][...] = (parts[number][...] + other_ref[tile_at].astype(F32)).astype(BF16)


def collect_kernel(dims, place_ref, key_gain_ref, value_gain_ref, *rest):
    count_chip, count_ka, share = dims
    parts, outs = rest[:count_chip], rest[count_chip:]
    kv_at = pl.ds(pl.multiple_of(place_ref[1] // share * HEAD_DIM, HEAD_DIM), HEAD_DIM)
    gain = jnp.concatenate([key_gain_ref[:, kv_at], value_gain_ref[:, kv_at]], axis=1)
    for step in range(count_ka):
        rows = pl.ds(step * TILE, TILE)
        total = parts[0][rows, :]
        for number in range(1, count_chip):
            total = total + parts[number][rows, :].astype(F32)
        if share == 1:
            total = total * gain
        outs[step][:TILE, :] = total.astype(outs[step].dtype)
    spare = pl.ds(count_ka * TILE, SPARE)
    total = parts[0][spare, :]
    for number in range(1, count_chip):
        total = total + parts[number][spare, :].astype(F32)
    packed = pack_gains(jnp.sum(total, axis=0, keepdims=True))
    for step in range(count_ka):
        outs[step][TILE:, :] = packed.astype(outs[step].dtype)


def turn_kernel(*refs):
    half = len(refs) // 2
    for source, target in zip(refs[:half], refs[half:]):
        for head in range(source.shape[1] // HEAD_DIM):
            part = pl.ds(head * HEAD_DIM, HEAD_DIM)
            target[:, part] = source[:, part].T


def place_kernel(dims, place_ref, *rest):
    count_ka, heads_dev, late = dims
    dq_parts, rest = rest[:count_ka], rest[count_ka:]
    dq_out, rest = rest[0], rest[1:]
    turned, sems = rest[:-1], rest[-1]
    width = heads_dev * HEAD_DIM
    copies = []
    for step in tuple(at for at in range(count_ka) if at not in late) + late:
        source = lax.rem(place_ref[1] - step + count_ka, count_ka)
        columns = pl.ds(pl.multiple_of(source * width, HEAD_DIM), width)
        piece = dq_parts[step]
        if step in late:
            turn_kernel(piece, turned[late.index(step)])
            piece = turned[late.index(step)]
        copies.append(pltpu.make_async_copy(piece, dq_out.at[:, columns], sems.at[step]))
        copies[-1].start()
    for copy in copies:
        copy.wait()


def finish_kernel(dims, place_ref, key_gain_ref, value_gain_ref, *rest):
    count_ka, share = dims
    pieces, rest = rest[:count_ka], rest[count_ka:]
    dk_out, dv_out, gains_out, sums = rest
    place_ka = place_ref[1]
    sums[...] = jnp.zeros_like(sums)
    for step in range(count_ka):
        source = lax.rem(place_ka + step, count_ka)
        sums[source // share] += pieces[step][...].astype(F32)
    for head in range(count_ka // share):
        part = pl.ds(head * HEAD_DIM, HEAD_DIM)
        key_total = sums[head, :TILE, :HEAD_DIM]
        value_total = sums[head, :TILE, HEAD_DIM:]
        if share > 1:
            key_total = key_total * key_gain_ref[:, part]
            value_total = value_total * value_gain_ref[:, part]
        dk_out[:, part] = key_total.astype(BF16)
        dv_out[:, part] = value_total.astype(BF16)
        gains = jnp.sum(sums[head, TILE:, :], axis=0, keepdims=True)
        gains_out[0:1, part] = gains[:, :HEAD_DIM]
        gains_out[1:2, part] = gains[:, HEAD_DIM:]


def in_vmem(count):
    return [pl.BlockSpec(memory_space=VMEM)] * count


def in_smem(count):
    return [pl.BlockSpec(memory_space=SMEM)] * count


def anywhere(count):
    return [pl.BlockSpec(memory_space=pl.ANY)] * count


def params(mib):
    return pltpu.CompilerParams(vmem_limit_bytes=mib * 1024 * 1024)


def shards(
    queries,
    key_rows,
    values,
    attn_out,
    grad_out,
    log_sums,
    key_gain,
    value_gain,
    doc_ids,
    tile_mask,
    block_order,
):
    count_pb = lax.axis_size("pb")
    count_ka = lax.axis_size("ka")
    place_pb = lax.axis_index("pb")
    place_ka = lax.axis_index("ka")
    rows_dev = key_rows.shape[0]
    query_rows = queries.shape[0]
    heads = log_sums.shape[0]
    feat_width = queries.shape[1]
    kv_heads = key_rows.shape[1] // HEAD_DIM
    heads_dev = heads // count_ka
    share = count_ka // kv_heads
    assert rows_dev == TILE and share * kv_heads == count_ka and count_pb & (count_pb - 1) == 0
    width = heads_dev * HEAD_DIM
    place = jnp.stack([place_pb, place_ka]).astype(jnp.int32)
    key_gain = key_gain.reshape(1, -1)
    value_gain = value_gain.reshape(1, -1)

    spare = extra_rows(heads_dev)
    count_chip = count_pb // 2

    def swap(array, number):
        return lax.ppermute(array, "pb", [(at, at ^ number) for at in range(count_pb)])

    def turn(array, step):
        return lax.ppermute(array, "ka", [(at, (at + step) % count_ka) for at in range(count_ka)])

    sends = pl.pallas_call(
        functools.partial(prepare_kernel, (count_ka, heads, heads_dev, share)),
        grid_spec=pltpu.PrefetchScalarGridSpec(
            num_scalar_prefetch=1,
            grid=(1,),
            in_specs=[
                pl.BlockSpec((rows_dev, key_rows.shape[1]), lambda i, s: (0, 0)),
                pl.BlockSpec((rows_dev, key_rows.shape[1]), lambda i, s: (0, 0)),
                pl.BlockSpec((rows_dev, feat_width), lambda i, s: (0, 0)),
                pl.BlockSpec((rows_dev, feat_width), lambda i, s: (s[1], 0)),
                pl.BlockSpec((heads, rows_dev), lambda i, s: (0, 0)),
            ],
            out_specs=[pl.BlockSpec((TILE + spare, 2 * HEAD_DIM), lambda i, s: (0, 0))] * count_ka,
            scratch_shapes=[VMEM((heads + 8, TILE), F32)] * 2,
        ),
        out_shape=[jax.ShapeDtypeStruct((TILE + spare, 2 * HEAD_DIM), BF16)] * count_ka,
        compiler_params=params(57),
        name="prepare",
    )(place, key_rows, values, attn_out, grad_out, log_sums)
    messages = [sends[0]] + [turn(sends[step], step) for step in range(1, count_ka)]

    later_place, _ = lax.optimization_barrier((place, sends[0]))
    own_queries = pl.pallas_call(
        own_heads_kernel,
        grid_spec=pltpu.PrefetchScalarGridSpec(
            num_scalar_prefetch=1,
            grid=(count_ka,),
            in_specs=[pl.BlockSpec((TILE, width), lambda i, s: (i, s[1]))] * 2,
            out_specs=pl.BlockSpec((4, 1, width, HEAD_DIM), lambda i, s: (0, i, 0, 0)),
        ),
        out_shape=jax.ShapeDtypeStruct((4, count_ka, width, HEAD_DIM), BF16),
        compiler_params=params(60),
        cost_estimate=pl.CostEstimate(flops=0, bytes_accessed=12 * query_rows * width, transcendentals=0),
        name="own_heads",
    )(later_place, queries, grad_out)
    messages, own_queries = lax.optimization_barrier((messages, own_queries))
    own_block = jnp.concatenate([message[:TILE] for message in messages], axis=0)
    own_stats = jnp.concatenate([message[TILE:] for message in messages], axis=0)
    blocks = [own_block] + [swap(own_block, 2 * number) for number in range(1, count_chip)]
    other_stats = swap(own_stats, 1)
    other_queries = swap(own_queries, 1)

    key_tiles = count_chip * count_ka
    sum_shape = jax.ShapeDtypeStruct((key_tiles, TILE, HEAD_DIM), F32)
    key_shape = jax.ShapeDtypeStruct((key_tiles, TILE, HEAD_DIM), BF16)
    kv_shape = (query_rows + SPARE, 2 * HEAD_DIM)
    work = [
        VMEM((head_rows(heads_dev), 2 * TILE), F32),
        VMEM((2 * TILE, width), BF16),
        VMEM((2 * TILE, width), BF16),
        VMEM((HEAD_DIM, width), F32),
        SMEM((key_tiles + 2,), jnp.int32),
        SMEM((key_tiles + 2,), jnp.int32),
    ]
    half = count_ka // 2
    early = (half, 0)
    late = tuple(step for step in range(1, count_ka) if step != half)
    scalars = (place, block_order, doc_ids, tile_mask)

    def attend(stage, steps, outs, scratch, *operands):
        dims = (count_chip, count_ka, heads_dev, share, stage, steps)
        pairs = len(steps) * key_tiles
        return pl.pallas_call(
            functools.partial(attention_kernel, dims),
            in_specs=in_smem(4) + in_vmem(len(operands)),
            out_specs=in_vmem(len(outs)),
            out_shape=outs,
            scratch_shapes=scratch + work,
            compiler_params=params(14 + key_tiles // 2),
            cost_estimate=pl.CostEstimate(
                flops=10 * pairs * TILE * TILE * width, bytes_accessed=1 << 22, transcendentals=0
            ),
            name=("attention_other", "attention_early", "attention_late")[stage],
        )(*scalars, *operands)

    part_shape = jax.ShapeDtypeStruct((HEAD_DIM, width), F32)
    full_shape = jax.ShapeDtypeStruct((HEAD_DIM, width), BF16)
    dq_other, *state = attend(
        0, tuple(range(count_ka)),
        [jax.ShapeDtypeStruct((count_ka, HEAD_DIM, width), BF16)] + [key_shape] * 3 + [sum_shape] * 2,
        [], key_gain, value_gain, other_queries, other_stats, *blocks,
    )
    dq_back = swap(dq_other, 1)
    keys, sums = state[:3], state[3:]
    *dq_early, key_sum, value_sum = attend(
        1, early, [part_shape] * len(early) + [sum_shape] * 2, [],
        own_queries, own_stats, *keys, *sums,
    )
    added = pl.pallas_call(
        functools.partial(add_kernel, (count_ka, early)),
        in_specs=in_smem(1) + in_vmem(1 + len(early)),
        out_specs=in_vmem(len(early)),
        out_shape=[full_shape] * len(early),
        compiler_params=params(16),
        name="add_queries",
    )(place, dq_back, *dq_early)
    dq_parts = [None] * count_ka
    added = list(added)
    late_stats, added[-1] = lax.optimization_barrier((own_stats, added[-1]))
    dq_parts[half], dq_parts[0] = turn(added[0], half), added[1]
    results = attend(
        2, late,
        [full_shape] * len(late) + [jax.ShapeDtypeStruct(kv_shape, F32)]
        + [jax.ShapeDtypeStruct(kv_shape, BF16)] * (count_chip - 1),
        [VMEM(sum_shape.shape, F32)] * 2,
        own_queries, late_stats, *blocks, *keys, key_sum, value_sum, dq_back,
    )
    dq_late, kv_own = results[:len(late)], results[len(late):]
    kv_own = list(kv_own)
    kv_own[-1], dq_parts[half] = lax.optimization_barrier((kv_own[-1], dq_parts[half]))
    kv_parts = [kv_own[0]] + [swap(kv_own[number], 2 * number) for number in range(1, count_chip)]
    for number, step in enumerate(late):
        dq_parts[step] = turn(dq_late[number], step)

    piece_type = BF16 if share == 1 else F32
    piece_shape = (TILE + SPARE, 2 * HEAD_DIM)
    totals = pl.pallas_call(
        functools.partial(collect_kernel, (count_chip, count_ka, share)),
        in_specs=in_smem(1) + in_vmem(2 + count_chip),
        out_specs=in_vmem(count_ka),
        out_shape=[jax.ShapeDtypeStruct(piece_shape, piece_type)] * count_ka,
        compiler_params=params(24),
        name="collect",
    )(place, key_gain, value_gain, *kv_parts)
    pieces = [totals[0]] + [turn(totals[step], -step) for step in range(1, count_ka)]

    grad_keys, grad_values, gains = pl.pallas_call(
        functools.partial(finish_kernel, (count_ka, share)),
        in_specs=in_smem(1) + in_vmem(2 + count_ka),
        out_specs=in_vmem(3),
        out_shape=[
            jax.ShapeDtypeStruct(key_rows.shape, BF16),
            jax.ShapeDtypeStruct(key_rows.shape, BF16),
            jax.ShapeDtypeStruct((2, key_rows.shape[1]), F32),
        ],
        scratch_shapes=[VMEM((kv_heads, TILE + SPARE, 2 * HEAD_DIM), F32)],
        compiler_params=params(16),
        name="finish",
    )(place, key_gain, value_gain, *pieces)
    gains = gains + swap(gains, 1)
    first = (0, half)
    turned = pl.pallas_call(
        turn_kernel,
        in_specs=in_vmem(len(first)),
        out_specs=in_vmem(len(first)),
        out_shape=[full_shape] * len(first),
        compiler_params=params(8),
        cost_estimate=pl.CostEstimate(flops=0, bytes_accessed=1 << 22, transcendentals=0),
        name="turn_queries",
    )(*[dq_parts[step] for step in first])
    for number, step in enumerate(first):
        dq_parts[step] = turned[number]
    grad_queries = pl.pallas_call(
        functools.partial(place_kernel, (count_ka, heads_dev, late)),
        in_specs=in_smem(1) + in_vmem(count_ka),
        out_specs=pl.BlockSpec(memory_space=pl.ANY),
        out_shape=jax.ShapeDtypeStruct((rows_dev, feat_width), BF16),
        scratch_shapes=[VMEM((TILE, width), BF16)] * len(late) + [pltpu.SemaphoreType.DMA((count_ka,))],
        compiler_params=params(16),
        cost_estimate=pl.CostEstimate(flops=0, bytes_accessed=4 * rows_dev * feat_width, transcendentals=0),
        name="place_queries",
    )(place, *dq_parts)
    return grad_queries, grad_keys, grad_values, gains[0], gains[1]


def solution(mesh):
    placed = (
        P("pb", None),
        P(("pb", "ka"), None),
        P(("pb", "ka"), None),
        P(("pb", "ka"), None),
        P("pb", None),
        P(None, ("pb", "ka")),
        P(),
        P(),
        P(),
        P(),
        P(),
    )
    return jax.shard_map(
        shards,
        mesh=mesh,
        in_specs=placed,
        out_specs=(P(("pb", "ka"), None), P(("pb", "ka"), None), P(("pb", "ka"), None), P(), P()),
        check_vma=False,
    )
```

profile of v0, /device:TPU:0, one launch (start us, length us, event | category | flops | bytes accessed | tf_op | source)
XLA Modules:
  0.0 90.3 jit_solution(17456653157010145373)
XLA Ops:
  0.6 0.7 pad_add_fusion.place_ref
  1.3 3.7 %prepare.1 = (bf16[160,256]{1,0:T(8,128)(2,1)}, bf16[160,256]{1,0:T(8,128)(2,1)}, bf16[160,256]{1,0:T(8,128)(2,1)}, bf16[160,256]{1,0:T(8,128)(2,1)}) custom-call(s32[2]{0:T(128)} %pad_add_fusion.place_ref, bf16[128,512]{1,0:T(8,128)(2,1)} %key_ref.1, bf16[128,512]{1,0:T(8,128)(2,1)} %value_ref.1, bf16[128,4096]{1,0:T(8,128)(2,1)} %attn_ref.1, ...), custom_call_target="tpu_custom_call" | custom-call | tf_op jit(solution)/shard_map/prepare/pallas_call | solution.py:369
  5.0 3.0 %collective-permute-start = (bf16[160,256]{1,0:T(8,128)(2,1)}, bf16[160,256]{1,0:T(8,128)(2,1)S(1)}, u32[]{:S(2)}, u32[]{:S(2)}) collective-permute-start(bf16[160,256]{1,0:T(8,128)(2,1)} %get-tuple-element.47), channel_id=1, source_target_pairs={{0,1},{1,2},{2,3},{3,0},{4,5},{5,6},{6,7},{7,4},{8,9},{9,10},{10,1... | collective-permute-start | bytes 245768 | tf_op jit(solution)/shard_map/ppermute | solution.py:367
  8.1 2.6 %collective-permute-start.1 = (bf16[160,256]{1,0:T(8,128)(2,1)}, bf16[160,256]{1,0:T(8,128)(2,1)S(1)}, u32[]{:S(2)}, u32[]{:S(2)}) collective-permute-start(bf16[160,256]{1,0:T(8,128)(2,1)} %get-tuple-element.48), channel_id=1, source_target_pairs={{0,2},{1,3},{2,0},{3,1},{4,6},{5,7},{6,4},{7,5},{8,10},{9,11},{10,... | collective-permute-start | bytes 245768 | tf_op jit(solution)/shard_map/ppermute | solution.py:367
  10.7 1.3 %collective-permute-start.2 = (bf16[160,256]{1,0:T(8,128)(2,1)}, bf16[160,256]{1,0:T(8,128)(2,1)S(1)}, u32[]{:S(2)}, u32[]{:S(2)}) collective-permute-start(bf16[160,256]{1,0:T(8,128)(2,1)} %get-tuple-element.49), channel_id=1, source_target_pairs={{0,3},{1,0},{2,1},{3,2},{4,7},{5,4},{6,5},{7,6},{8,11},{9,8},{10,9... | collective-permute-start | bytes 245768 | tf_op jit(solution)/shard_map/ppermute | solution.py:367
  12.0 0.0 copy-start.7
  12.0 0.0 copy-start.1
  12.0 0.0 copy-start.4
  12.0 0.0 copy-start.5
  12.0 0.0 copy-start.6
  12.0 5.3 %own_heads.1.rest_0_ = bf16[4,4,1024,128]{3,2,1,0:T(8,128)(2,1)} custom-call(s32[2]{0:T(128)} %pad_add_fusion.place_ref, bf16[512,4096]{1,0:T(8,128)(2,1)} %queries_ref.1, bf16[512,4096]{1,0:T(8,128)(2,1)} %grads_ref.1), custom_call_target="tpu_custom_call" | custom-call | bytes 6291456 | tf_op jit(solution)/shard_map/own_heads/pallas_call | solution.py:391
  17.4 0.0 collective-permute-done
  17.4 0.0 collective-permute-done.1
  17.4 0.0 collective-permute-done.2
  17.4 0.1 collective-permute-start.3
  17.5 0.0 copy-done.7
  17.6 2.5 %collective-permute-start.7 = (bf16[512,256]{1,0:T(8,128)(2,1)S(1)}, bf16[512,256]{1,0:T(8,128)(2,1)S(1)}, u32[]{:S(2)}, u32[]{:S(2)}) collective-permute-start(bf16[512,256]{1,0:T(8,128)(2,1)S(1)} %pad_maximum_fusion.rest_4_.rest_2_), channel_id=1, source_target_pairs={{0,24},{4,28},{8,16},{12,20},{16,8},{20,12},{24,0},{28,4},{1,25},{... | collective-permute-start | bytes 786440 | tf_op jit(solution)/shard_map/ppermute | solution.py:364
  20.1 0.5 collective-permute-start.6
  20.6 0.5 collective-permute-start.5
  21.2 0.1 collective-permute-start.4
  21.2 3.5 %collective-permute-done.4.rest_3_ = bf16[128,256]{1,0:T(8,128)(2,1)S(1)} collective-permute-done((bf16[128,256]{1,0:T(8,128)(2,1)S(1)}, bf16[128,256]{1,0:T(8,128)(2,1)S(1)}, u32[]{:S(2)}, u32[]{:S(2)}) %collective-permute-start.4) | collective-permute-done | bytes 65568 | tf_op jit(solution)/shard_map/ppermute | solution.py:364
  24.7 3.0 %collective-permute-done.7.rest_7_.rest_5_ = bf16[512,256]{1,0:T(8,128)(2,1)S(1)} collective-permute-done((bf16[512,256]{1,0:T(8,128)(2,1)S(1)}, bf16[512,256]{1,0:T(8,128)(2,1)S(1)}, u32[]{:S(2)}, u32[]{:S(2)}) %collective-permute-start.7) | collective-permute-done | bytes 262176 | tf_op jit(solution)/shard_map/ppermute | solution.py:364
  27.7 5.2 %collective-permute-done.6.rest_6_.rest_4_ = bf16[512,256]{1,0:T(8,128)(2,1)S(1)} collective-permute-done((bf16[512,256]{1,0:T(8,128)(2,1)S(1)}, bf16[512,256]{1,0:T(8,128)(2,1)S(1)}, u32[]{:S(2)}, u32[]{:S(2)}) %collective-permute-start.6) | collective-permute-done | bytes 262176 | tf_op jit(solution)/shard_map/ppermute | solution.py:364
  32.9 0.1 collective-permute-done.5.rest_5_.rest_3_
  33.0 0.0 collective-permute-done.3.rest_2_
  33.0 0.0 copy-done.1
  33.0 0.0 copy-done.2
  33.0 0.0 copy-done.3
  33.0 0.0 copy-done.4
  33.0 0.0 copy-done.5
  33.0 0.0 copy-done.6
  33.0 0.0 copy-start
  33.0 7.1 %attention_other.1 = (bf16[4,128,1024]{2,1,0:T(8,128)(2,1)S(1)}, bf16[16,128,128]{2,1,0:T(8,128)(2,1)S(1)}, bf16[16,128,128]{2,1,0:T(8,128)(2,1)S(1)}, bf16[16,1...) custom-call(s32[2]{0:T(128)S(1)} %copy-done.1, s32[32]{0:T(128)S(1)} %copy-done.5, ...), custom_call_target="tpu_custom_call" | custom-call | flops 10737418240 | bytes 4194304 | tf_op jit(solution)/shard_map/attention_other/pallas_call | solution.py:431
  40.1 5.6 %collective-permute-start.8 = (bf16[4,128,1024]{2,1,0:T(8,128)(2,1)S(1)}, bf16[4,128,1024]{2,1,0:T(8,128)(2,1)S(1)}, u32[]{:S(2)}, u32[]{:S(2)}) collective-permute-start(bf16[4,128,1024]{2,1,0:T(8,128)(2,1)S(1)} %get-tuple-element.56), channel_id=1, source_target_pairs={{0,4},{4,0},{8,12},{12,8},{16,20},{20,16},{24,28},{28,24},{1,5},{5... | collective-permute-start | bytes 3145736 | tf_op jit(solution)/shard_map/ppermute | solution.py:364
  45.7 0.0 copy-done
  45.7 4.4 %attention_early.1 = (f32[128,1024]{1,0:T(8,128)S(1)}, f32[128,1024]{1,0:T(8,128)S(1)}, f32[16,128,128]{2,1,0:T(8,128)S(1)}, f32[16,128,128]{2,1,0:T(8,128)S(1)}) custom-call(s32[2]{0:T(128)S(1)} %copy-done.1, s32[32]{0:T(128)S(1)} %copy-done.5, s32[32]{0:T(128)S(1)} %copy-done.6, s32[32,32]{1,0:T(8,128)S(1)} %copy-done.4, ...), custom_call_target="tpu_custom_call" | custom-call | flops 5368709120 | bytes 4194304 | tf_op jit(solution)/shard_map/attention_early/pallas_call | solution.py:431
  50.1 0.0 collective-permute-done.8.other_ref.rest_11_
  50.1 0.6 add_queries.1
  50.7 0.6 collective-permute-start.9
  51.3 7.1 %attention_late.1 = (bf16[128,1024]{1,0:T(8,128)(2,1)S(1)}, bf16[128,1024]{1,0:T(8,128)(2,1)S(1)}, f32[528,256]{1,0:T(8,128)S(1)}, bf16[528,256]{1,0:T(8,128)(2,...) custom-call(s32[2]{0:T(128)S(1)} %copy-done.1, s32[32]{0:T(128)S(1)} %copy-done.5, s32[32]{0:T(128)S(1)} %copy-done.6, ...), custom_call_target="tpu_custom_call" | custom-call | flops 5368709120 | bytes 4194304 | tf_op jit(solution)/shard_map/attention_late/pallas_call | solution.py:431
  58.5 0.1 collective-permute-start.12
  58.6 0.1 collective-permute-start.13
  58.6 7.4 %collective-permute-done.9.refs_1_ = bf16[128,1024]{1,0:T(8,128)(2,1)S(1)} collective-permute-done((bf16[128,1024]{1,0:T(8,128)(2,1)S(1)}, bf16[128,1024]{1,0:T(8,128)(2,1)S(1)}, u32[]{:S(2)}, u32[]{:S(2)}) %collective-permute-start.9) | collective-permute-done | bytes 262176 | tf_op jit(solution)/shard_map/ppermute | solution.py:367
  66.0 0.0 collective-permute-start.14
  66.0 0.0 collective-permute-start.10
  66.0 3.8 %collective-permute-start.11 = (bf16[128,1024]{1,0:T(8,128)(2,1)S(1)}, bf16[128,1024]{1,0:T(8,128)(2,1)S(1)}, u32[]{:S(2)}, u32[]{:S(2)}) collective-permute-start(bf16[128,1024]{1,0:T(8,128)(2,1)S(1)} %get-tuple-element.75), channel_id=1, source_target_pairs={{0,3},{1,0},{2,1},{3,2},{4,7},{5,4},{6,5},{7,6},{8,11},{9,8},{10,9... | collective-permute-start | bytes 786440 | tf_op jit(solution)/shard_map/ppermute | solution.py:367
  69.8 0.0 collective-permute-done.12.rest_1_
  69.8 0.0 collective-permute-done.13.rest_2_
  69.8 5.6 %collective-permute-done.14.rest_3_ = bf16[528,256]{1,0:T(8,128)(2,1)S(1)} collective-permute-done((bf16[528,256]{1,0:T(8,128)(2,1)S(1)}, bf16[528,256]{1,0:T(8,128)(2,1)S(1)}, u32[]{:S(2)}, u32[]{:S(2)}) %collective-permute-start.14) | collective-permute-done | bytes 270368 | tf_op jit(solution)/shard_map/ppermute | solution.py:364
  75.4 0.7 collect.1
  76.1 1.8 %collective-permute-start.15 = (bf16[144,256]{1,0:T(8,128)(2,1)S(1)}, bf16[144,256]{1,0:T(8,128)(2,1)S(1)}, u32[]{:S(2)}, u32[]{:S(2)}) collective-permute-start(bf16[144,256]{1,0:T(8,128)(2,1)S(1)} %get-tuple-element.81), channel_id=1, source_target_pairs={{0,3},{1,0},{2,1},{3,2},{4,7},{5,4},{6,5},{7,6},{8,11},{9,8},{10,9... | collective-permute-start | bytes 221192 | tf_op jit(solution)/shard_map/ppermute | solution.py:367
  77.9 0.0 collective-permute-start.16
  77.9 0.6 collective-permute-start.17
  78.5 3.8 %collective-permute-done.15.rest_1_ = bf16[144,256]{1,0:T(8,128)(2,1)S(1)} collective-permute-done((bf16[144,256]{1,0:T(8,128)(2,1)S(1)}, bf16[144,256]{1,0:T(8,128)(2,1)S(1)}, u32[]{:S(2)}, u32[]{:S(2)}) %collective-permute-start.15) | collective-permute-done | bytes 73760 | tf_op jit(solution)/shard_map/ppermute | solution.py:367
  82.3 1.9 %collective-permute-done.16.rest_2_ = bf16[144,256]{1,0:T(8,128)(2,1)S(1)} collective-permute-done((bf16[144,256]{1,0:T(8,128)(2,1)S(1)}, bf16[144,256]{1,0:T(8,128)(2,1)S(1)}, u32[]{:S(2)}, u32[]{:S(2)}) %collective-permute-start.16) | collective-permute-done | bytes 73760 | tf_op jit(solution)/shard_map/ppermute | solution.py:367
  84.2 2.4 %collective-permute-done.17.rest_3_ = bf16[144,256]{1,0:T(8,128)(2,1)S(1)} collective-permute-done((bf16[144,256]{1,0:T(8,128)(2,1)S(1)}, bf16[144,256]{1,0:T(8,128)(2,1)S(1)}, u32[]{:S(2)}, u32[]{:S(2)}) %collective-permute-start.17) | collective-permute-done | bytes 73760 | tf_op jit(solution)/shard_map/ppermute | solution.py:367
  86.5 1.4 %finish.1 = (bf16[128,512]{1,0:T(8,128)(2,1)}, bf16[128,512]{1,0:T(8,128)(2,1)}, f32[2,512]{1,0:T(2,128)S(1)}) custom-call(s32[2]{0:T(128)S(1)} %copy-done.1, f32[1,512]{1,0:T(1,128)S(1)} %bitcast.8, f32[1,512]{1,0:T(1,128)S(1)} %bitcast.11, bf16[144,256]{1,0:T(8,128)(2,1)S(1)} %get-tuple-element.80.rest_0_, ...), custom_call_target="tpu_custom_call" | custom-call | tf_op jit(solution)/shard_map/finish/pallas_call | solution.py:495
  87.9 0.0 collective-permute-start.18
  87.9 0.2 turn_queries.1
  88.1 0.0 collective-permute-done.10.rest_1_
  88.1 0.0 collective-permute-done.11.rest_3_
  88.1 1.6 %place_queries.1 = bf16[128,4096]{1,0:T(8,128)(2,1)} custom-call(s32[2]{0:T(128)S(1)} %copy-done.1, bf16[128,1024]{1,0:T(8,128)(2,1)S(1)} %get-tuple-element.72.rest_0_, bf16[128,1024]{1,0:T(8,128)(2,1)S(1)} %collective-permute-done.10.rest_1_, bf16[128,1024]{1,0:T(8,128)(2,1)S(1)} %get-tuple-element.74.rest_2_, ...), custom_call_target="tpu_custom_call" | custom-call | bytes 2097152 | tf_op jit(solution)/shard_map/place_queries/pallas_call | solution.py:521
  89.7 0.0 collective-permute-done.18
  89.7 0.6 fusion
  (13 shorter events, 0.1 us)
Async XLA Ops:
  5.0 12.4 %collective-permute-start = (bf16[160,256]{1,0:T(8,128)(2,1)}, bf16[160,256]{1,0:T(8,128)(2,1)S(1)}, u32[]{:S(2)}, u32[]{:S(2)}) collective-permute-start(bf16[160,256]{1,0:T(8,128)(2,1)} %get-tuple-element.47), channel_id=1, source_target_pairs={{0,1},{1,2},{2,3},{3,0},{4,5},{5,6},{6,7},{7,4},{8,9},{9,10},{10,1... | collective-permute-start | bytes 245768 | tf_op jit(solution)/shard_map/ppermute | solution.py:367
  8.1 9.3 %collective-permute-start.1 = (bf16[160,256]{1,0:T(8,128)(2,1)}, bf16[160,256]{1,0:T(8,128)(2,1)S(1)}, u32[]{:S(2)}, u32[]{:S(2)}) collective-permute-start(bf16[160,256]{1,0:T(8,128)(2,1)} %get-tuple-element.48), channel_id=1, source_target_pairs={{0,2},{1,3},{2,0},{3,1},{4,6},{5,7},{6,4},{7,5},{8,10},{9,11},{10,... | collective-permute-start | bytes 245768 | tf_op jit(solution)/shard_map/ppermute | solution.py:367
  10.7 6.8 %collective-permute-start.2 = (bf16[160,256]{1,0:T(8,128)(2,1)}, bf16[160,256]{1,0:T(8,128)(2,1)S(1)}, u32[]{:S(2)}, u32[]{:S(2)}) collective-permute-start(bf16[160,256]{1,0:T(8,128)(2,1)} %get-tuple-element.49), channel_id=1, source_target_pairs={{0,3},{1,0},{2,1},{3,2},{4,7},{5,4},{6,5},{7,6},{8,11},{9,8},{10,9... | collective-permute-start | bytes 245768 | tf_op jit(solution)/shard_map/ppermute | solution.py:367
  12.0 5.5 %copy-start.7 = (bf16[160,256]{1,0:T(8,128)(2,1)S(1)}, bf16[160,256]{1,0:T(8,128)(2,1)}, u32[]{:S(2)}) copy-start(bf16[160,256]{1,0:T(8,128)(2,1)} %get-tuple-element.51) | copy-start | bytes 245764
  12.0 21.0 %copy-start.1 = (s32[2]{0:T(128)S(1)}, s32[2]{0:T(128)}, u32[]{:S(2)}) copy-start(s32[2]{0:T(128)} %pad_add_fusion.place_ref) | copy-start | bytes 28
  12.0 21.0 %copy-start.2 = (f32[512]{0:T(512)S(1)}, f32[512]{0:T(512)}, u32[]{:S(2)}) copy-start(f32[512]{0:T(512)} %param.17) | copy-start | bytes 6148
  12.0 21.0 %copy-start.3 = (f32[512]{0:T(512)S(1)}, f32[512]{0:T(512)}, u32[]{:S(2)}) copy-start(f32[512]{0:T(512)} %param.18) | copy-start | bytes 6148
  12.0 21.0 %copy-start.4 = (s32[32,32]{1,0:T(8,128)S(1)}, s32[32,32]{1,0:T(8,128)}, u32[]{:S(2)}) copy-start(s32[32,32]{1,0:T(8,128)} %mask_ref.5) | copy-start | bytes 12292
  12.0 21.0 %copy-start.5 = (s32[32]{0:T(128)S(1)}, s32[32]{0:T(128)}, u32[]{:S(2)}) copy-start(s32[32]{0:T(128)} %order_ref.5) | copy-start | bytes 388
  12.0 21.0 %copy-start.6 = (s32[32]{0:T(128)S(1)}, s32[32]{0:T(128)}, u32[]{:S(2)}) copy-start(s32[32]{0:T(128)} %doc_ref.5) | copy-start | bytes 388
  17.4 15.6 %collective-permute-start.3 = (bf16[4,4,1024,128]{3,2,1,0:T(8,128)(2,1)}, bf16[4,4,1024,128]{3,2,1,0:T(8,128)(2,1)S(1)}, u32[]{:S(2)}, u32[]{:S(2)}) collective-permute-start(bf16[4,4,1024,128]{3,2,1,0:T(8,128)(2,1)} %own_heads.1.rest_0_), channel_id=1, source_target_pairs={{0,4},{4,0},{8,12},{12,8},{16,20},{20,16},{24,28},{28,24},{1,5},{5... | collective-permute-start | bytes 12582920 | tf_op jit(solution)/shard_map/ppermute | solution.py:364
  17.6 10.1 %collective-permute-start.7 = (bf16[512,256]{1,0:T(8,128)(2,1)S(1)}, bf16[512,256]{1,0:T(8,128)(2,1)S(1)}, u32[]{:S(2)}, u32[]{:S(2)}) collective-permute-start(bf16[512,256]{1,0:T(8,128)(2,1)S(1)} %pad_maximum_fusion.rest_4_.rest_2_), channel_id=1, source_target_pairs={{0,24},{4,28},{8,16},{12,20},{16,8},{20,12},{24,0},{28,4},{1,25},{... | collective-permute-start | bytes 786440 | tf_op jit(solution)/shard_map/ppermute | solution.py:364
  20.1 12.8 %collective-permute-start.6 = (bf16[512,256]{1,0:T(8,128)(2,1)S(1)}, bf16[512,256]{1,0:T(8,128)(2,1)S(1)}, u32[]{:S(2)}, u32[]{:S(2)}) collective-permute-start(bf16[512,256]{1,0:T(8,128)(2,1)S(1)} %pad_maximum_fusion.rest_4_.rest_2_), channel_id=1, source_target_pairs={{0,16},{4,20},{8,24},{12,28},{16,0},{20,4},{24,8},{28,12},{1,17},{... | collective-permute-start | bytes 786440 | tf_op jit(solution)/shard_map/ppermute | solution.py:364
  20.6 12.4 %collective-permute-start.5 = (bf16[512,256]{1,0:T(8,128)(2,1)S(1)}, bf16[512,256]{1,0:T(8,128)(2,1)S(1)}, u32[]{:S(2)}, u32[]{:S(2)}) collective-permute-start(bf16[512,256]{1,0:T(8,128)(2,1)S(1)} %pad_maximum_fusion.rest_4_.rest_2_), channel_id=1, source_target_pairs={{0,8},{4,12},{8,0},{12,4},{16,24},{20,28},{24,16},{28,20},{1,9},{5... | collective-permute-start | bytes 786440 | tf_op jit(solution)/shard_map/ppermute | solution.py:364
  21.2 3.6 %collective-permute-start.4 = (bf16[128,256]{1,0:T(8,128)(2,1)S(1)}, bf16[128,256]{1,0:T(8,128)(2,1)S(1)}, u32[]{:S(2)}, u32[]{:S(2)}) collective-permute-start(bf16[128,256]{1,0:T(8,128)(2,1)S(1)} %pad_maximum_fusion.1.rest_1_), channel_id=1, source_target_pairs={{0,4},{4,0},{8,12},{12,8},{16,20},{20,16},{24,28},{28,24},{1,5},{5... | collective-permute-start | bytes 196616 | tf_op jit(solution)/shard_map/ppermute | solution.py:364
  33.0 12.7 %copy-start = (bf16[4,4,1024,128]{3,2,1,0:T(8,128)(2,1)S(1)}, bf16[4,4,1024,128]{3,2,1,0:T(8,128)(2,1)}, u32[]{:S(2)}) copy-start(bf16[4,4,1024,128]{3,2,1,0:T(8,128)(2,1)} %own_heads.1.rest_0_) | copy-start | bytes 12582916
  40.1 10.0 %collective-permute-start.8 = (bf16[4,128,1024]{2,1,0:T(8,128)(2,1)S(1)}, bf16[4,128,1024]{2,1,0:T(8,128)(2,1)S(1)}, u32[]{:S(2)}, u32[]{:S(2)}) collective-permute-start(bf16[4,128,1024]{2,1,0:T(8,128)(2,1)S(1)} %get-tuple-element.56), channel_id=1, source_target_pairs={{0,4},{4,0},{8,12},{12,8},{16,20},{20,16},{24,28},{28,24},{1,5},{5... | collective-permute-start | bytes 3145736 | tf_op jit(solution)/shard_map/ppermute | solution.py:364
  50.7 15.3 %collective-permute-start.9 = (bf16[128,1024]{1,0:T(8,128)(2,1)S(1)}, bf16[128,1024]{1,0:T(8,128)(2,1)S(1)}, u32[]{:S(2)}, u32[]{:S(2)}) collective-permute-start(bf16[128,1024]{1,0:T(8,128)(2,1)S(1)} %get-tuple-element.70), channel_id=1, source_target_pairs={{0,2},{1,3},{2,0},{3,1},{4,6},{5,7},{6,4},{7,5},{8,10},{9,11},{10,... | collective-permute-start | bytes 786440 | tf_op jit(solution)/shard_map/ppermute | solution.py:367
  58.5 11.3 %collective-permute-start.12 = (bf16[528,256]{1,0:T(8,128)(2,1)S(1)}, bf16[528,256]{1,0:T(8,128)(2,1)S(1)}, u32[]{:S(2)}, u32[]{:S(2)}) collective-permute-start(bf16[528,256]{1,0:T(8,128)(2,1)S(1)} %get-tuple-element.77), channel_id=1, source_target_pairs={{0,8},{4,12},{8,0},{12,4},{16,24},{20,28},{24,16},{28,20},{1,9},{5... | collective-permute-start | bytes 811016 | tf_op jit(solution)/shard_map/ppermute | solution.py:364
  58.6 11.3 %collective-permute-start.13 = (bf16[528,256]{1,0:T(8,128)(2,1)S(1)}, bf16[528,256]{1,0:T(8,128)(2,1)S(1)}, u32[]{:S(2)}, u32[]{:S(2)}) collective-permute-start(bf16[528,256]{1,0:T(8,128)(2,1)S(1)} %get-tuple-element.78), channel_id=1, source_target_pairs={{0,16},{4,20},{8,24},{12,28},{16,0},{20,4},{24,8},{28,12},{1,17},{... | collective-permute-start | bytes 811016 | tf_op jit(solution)/shard_map/ppermute | solution.py:364
  66.0 9.4 %collective-permute-start.14 = (bf16[528,256]{1,0:T(8,128)(2,1)S(1)}, bf16[528,256]{1,0:T(8,128)(2,1)S(1)}, u32[]{:S(2)}, u32[]{:S(2)}) collective-permute-start(bf16[528,256]{1,0:T(8,128)(2,1)S(1)} %get-tuple-element.79), channel_id=1, source_target_pairs={{0,24},{4,28},{8,16},{12,20},{16,8},{20,12},{24,0},{28,4},{1,25},{... | collective-permute-start | bytes 811016 | tf_op jit(solution)/shard_map/ppermute | solution.py:364
  66.0 22.1 %collective-permute-start.10 = (bf16[128,1024]{1,0:T(8,128)(2,1)S(1)}, bf16[128,1024]{1,0:T(8,128)(2,1)S(1)}, u32[]{:S(2)}, u32[]{:S(2)}) collective-permute-start(bf16[128,1024]{1,0:T(8,128)(2,1)S(1)} %get-tuple-element.73), channel_id=1, source_target_pairs={{0,1},{1,2},{2,3},{3,0},{4,5},{5,6},{6,7},{7,4},{8,9},{9,10},{10,1... | collective-permute-start | bytes 786440 | tf_op jit(solution)/shard_map/ppermute | solution.py:367
  66.0 22.1 %collective-permute-start.11 = (bf16[128,1024]{1,0:T(8,128)(2,1)S(1)}, bf16[128,1024]{1,0:T(8,128)(2,1)S(1)}, u32[]{:S(2)}, u32[]{:S(2)}) collective-permute-start(bf16[128,1024]{1,0:T(8,128)(2,1)S(1)} %get-tuple-element.75), channel_id=1, source_target_pairs={{0,3},{1,0},{2,1},{3,2},{4,7},{5,4},{6,5},{7,6},{8,11},{9,8},{10,9... | collective-permute-start | bytes 786440 | tf_op jit(solution)/shard_map/ppermute | solution.py:367
  76.1 6.2 %collective-permute-start.15 = (bf16[144,256]{1,0:T(8,128)(2,1)S(1)}, bf16[144,256]{1,0:T(8,128)(2,1)S(1)}, u32[]{:S(2)}, u32[]{:S(2)}) collective-permute-start(bf16[144,256]{1,0:T(8,128)(2,1)S(1)} %get-tuple-element.81), channel_id=1, source_target_pairs={{0,3},{1,0},{2,1},{3,2},{4,7},{5,4},{6,5},{7,6},{8,11},{9,8},{10,9... | collective-permute-start | bytes 221192 | tf_op jit(solution)/shard_map/ppermute | solution.py:367
  77.9 6.3 %collective-permute-start.16 = (bf16[144,256]{1,0:T(8,128)(2,1)S(1)}, bf16[144,256]{1,0:T(8,128)(2,1)S(1)}, u32[]{:S(2)}, u32[]{:S(2)}) collective-permute-start(bf16[144,256]{1,0:T(8,128)(2,1)S(1)} %get-tuple-element.82), channel_id=1, source_target_pairs={{0,2},{1,3},{2,0},{3,1},{4,6},{5,7},{6,4},{7,5},{8,10},{9,11},{10,... | collective-permute-start | bytes 221192 | tf_op jit(solution)/shard_map/ppermute | solution.py:367
  77.9 8.6 %collective-permute-start.17 = (bf16[144,256]{1,0:T(8,128)(2,1)S(1)}, bf16[144,256]{1,0:T(8,128)(2,1)S(1)}, u32[]{:S(2)}, u32[]{:S(2)}) collective-permute-start(bf16[144,256]{1,0:T(8,128)(2,1)S(1)} %get-tuple-element.83), channel_id=1, source_target_pairs={{0,1},{1,2},{2,3},{3,0},{4,5},{5,6},{6,7},{7,4},{8,9},{9,10},{10,1... | collective-permute-start | bytes 221192 | tf_op jit(solution)/shard_map/ppermute | solution.py:367
  87.9 1.8 %collective-permute-start.18 = (f32[2,512]{1,0:T(2,128)S(1)}, f32[2,512]{1,0:T(2,128)S(1)}, u32[]{:S(2)}, u32[]{:S(2)}) collective-permute-start(f32[2,512]{1,0:T(2,128)S(1)} %get-tuple-element.86), channel_id=1, source_target_pairs={{0,4},{4,0},{8,12},{12,8},{16,20},{20,16},{24,28},{28,24},{1,5},{5... | collective-permute-start | bytes 12296 | tf_op jit(solution)/shard_map/ppermute | solution.py:364
where the time goes:
time: 89.5 us; the launch traced here: 90.3 us
  waiting for transfers between devices  32.6 us (36%)
  Pallas kernels  32.1 us (36%)
  starting transfers between devices  23.3 us (26%)
  between operations  0.9 us (1%)
    pallas_call x3, Pallas kernels, attend(): pl.pallas_call(functools.partial(attention_kernel, dims), in_specs=in_sme...  18.5 us
    ppermute x10, waiting for transfers between devices, swap(): lax.ppermute(array, 'pb', [(at, at ^ number) for at in range(count_pb)])  17.3 us
    ppermute x9, waiting for transfers between devices, turn(): lax.ppermute(array, 'ka', [(at, (at + step) % count_ka) for at in range(c...  15.4 us
    ppermute x9, starting transfers between devices, turn(): lax.ppermute(array, 'ka', [(at, (at + step) % count_ka) for at in range(c...  13.8 us
    ppermute x10, starting transfers between devices, swap(): lax.ppermute(array, 'pb', [(at, at ^ number) for at in range(count_pb)])  9.47 us
    pallas_call x1, Pallas kernels, shards(): pl.pallas_call(own_heads_kernel, grid_spec=pltpu.PrefetchScalarGridSpec(n...  5.35 us
    pallas_call x1, Pallas kernels, shards(): pl.pallas_call(functools.partial(prepare_kernel, (count_ka, heads, heads_...  3.74 us
  transfers between devices with their start and end apart: 19, of which 9 were waited for; matrix products, arithmetic and copies ran while one was open for 0% of the time, Pallas kernels for 23%

commit v1 on v0

--- a/solution.py
+++ b/solution.py
@@ -11,6 +11,8 @@
 TILE = 128
 SPARE = 16
 LOG2E = 1.4426950408889634
+ENTRY = 8
+LAST_DIMS = (((1,), (1,)), ((), ()))
 VMEM = pltpu.VMEM
 SMEM = pltpu.SMEM
 F32 = jnp.float32
@@ -67,14 +69,64 @@
     for number, ref in enumerate((queries_ref, grads_ref)):
         for head in range(ref.shape[1] // HEAD_DIM):
             part = pl.ds(head * HEAD_DIM, HEAD_DIM)
-            tile = ref[:, part]
-            out_ref[number, 0, part, :] = tile
-            out_ref[2 + number, 0, part, :] = tile.T
-
-
-def attention_kernel(dims, place_ref, order_ref, doc_ref, mask_ref, *rest):
+            out_ref[number, 0, part, :] = ref[:, part]
+
+
+def places():
+    return lax.axis_index("pb"), lax.axis_index("ka")
+
+
+def plan_kernel(dims, order_ref, doc_ref, mask_ref, *rest):
+    count_chip, count_ka, stages = dims
+    tables, (live_list, limit_list) = rest[:len(stages)], rest[len(stages):]
+    key_tiles = count_chip * count_ka
+    place_pb, place_ka = places()
+    for table, (other, steps) in zip(tables, stages):
+        query_pb = place_pb ^ other
+
+        def query_step(turn_q, chunks, table=table, query_pb=query_pb, steps=steps):
+            step_q = jnp.int32(steps[0])
+            for number, step in enumerate(steps):
+                step_q = jnp.where(turn_q == number, step, step_q)
+            tile_at = lax.rem(place_ka + step_q, count_ka)
+            seq_q = order_ref[query_pb * count_ka + tile_at]
+            doc_q = doc_ref[seq_q]
+
+            def collect(number, count):
+                for step in range(count_ka):
+                    stored = (place_pb ^ (2 * number)) * count_ka + lax.rem(
+                        place_ka - step + count_ka, count_ka
+                    )
+                    seq_k = order_ref[stored]
+                    live = (mask_ref[seq_q, seq_k] == 1) & (doc_ref[seq_k] == doc_q) & (seq_q >= seq_k)
+                    live_list[count] = number * count_ka + step
+                    limit_list[count] = jnp.where(seq_q == seq_k, 0, -TILE)
+                    count = count + live.astype(jnp.int32)
+                return count
+
+            count = lax.fori_loop(0, count_chip, collect, jnp.int32(0))
+            live_list[count] = 0
+            limit_list[count] = TILE
+            pairs = (count + 1) // 2
+
+            def write(at, carry):
+                base = ENTRY * (chunks + at + 1)
+                table[base] = turn_q
+                table[base + 1] = tile_at
+                table[base + 2] = live_list[2 * at]
+                table[base + 3] = live_list[2 * at + 1]
+                table[base + 4] = limit_list[2 * at]
+                table[base + 5] = limit_list[2 * at + 1]
+                return carry
+
+            lax.fori_loop(0, pairs, write, 0)
+            return chunks + pairs
+
+        table[0] = lax.fori_loop(0, len(steps), query_step, jnp.int32(0))
+
+
+def attention_kernel(dims, table_ref, *rest):
     count_chip, count_ka, heads_dev, share, stage, steps = dims
-    key_tiles = count_chip * count_ka
     if stage == 0:
         (key_gain_ref, value_gain_ref), rest = rest[:2], rest[2:]
     (heads_ref, stats_ref), rest = rest[:2], rest[2:]
@@ -92,9 +144,8 @@
         dq_outs, rest = rest[:len(steps)], rest[len(steps):]
         kv_outs, rest = rest[:count_chip], rest[count_chip:]
         (key_sum, value_sum), rest = rest[:2], rest[2:]
-    (lse_delta, weights_low, dscores_low, dq_turn, live_list, limit_list) = rest
-    place_pb, place_ka = place_ref[0], place_ref[1]
-    query_pb = place_pb if stage else place_pb ^ 1
+    lse_delta, weights_low, dscores_low, dq_sum = rest
+    _, place_ka = places()
     rows8 = head_rows(heads_dev)
     spare = extra_rows(heads_dev)
     score_scale = HEAD_DIM ** -0.5
@@ -124,81 +175,58 @@
     reach = jnp.concatenate([reach, reach], axis=1)
     lower = lax.broadcasted_iota(jnp.int32, (2 * TILE, 2 * TILE), 0) < TILE
 
-    def query_step(turn_q, carry):
-        step_q = jnp.int32(steps[0])
-        for number, step in enumerate(steps):
-            step_q = jnp.where(turn_q == number, step, step_q)
-        tile_at = lax.rem(place_ka + step_q, count_ka)
-        seq_q = order_ref[query_pb * count_ka + tile_at]
-        doc_q = doc_ref[seq_q]
-
-        def collect(local, count):
-            number = local // count_ka
-            step = lax.rem(local, count_ka)
-            stored = ((place_pb ^ (2 * number)) * count_ka
-                      + lax.rem(place_ka - step + count_ka, count_ka))
-            seq_k = order_ref[stored]
-            live = (mask_ref[seq_q, seq_k] == 1) & (doc_ref[seq_k] == doc_q) & (seq_q >= seq_k)
-            live_list[count] = local
-            limit_list[count] = jnp.where(seq_q == seq_k, 0, -TILE)
-            return count + live.astype(jnp.int32)
-
-        live_count = lax.fori_loop(0, key_tiles, collect, jnp.int32(0))
-        live_list[live_count] = 0
-        limit_list[live_count] = TILE
-
-        slot = lax.rem(place_ka - tile_at + count_ka, count_ka)
-        packed = stats_ref[pl.ds(pl.multiple_of(slot * spare, spare), spare), :].astype(F32)
-        lse_delta[...] = (packed[:rows8] + packed[rows8:2 * rows8]) + packed[2 * rows8:3 * rows8]
-        dq_turn[...] = jnp.zeros_like(dq_turn)
-
-        def pair_step(at, carry):
-            first, second = live_list[2 * at], live_list[2 * at + 1]
-            limits = jnp.where(lower, limit_list[2 * at], limit_list[2 * at + 1])
-            allowed = reach >= limits
-            key_pair = jnp.concatenate([keys[first], keys[second]], axis=0)
-            value_pair = jnp.concatenate([values[first], values[second]], axis=0)
-            key_turn = jnp.concatenate([keys_t[first], keys_t[second]], axis=1)
-            for head in range(0, heads_dev, 2):
-                part = pl.ds(head * HEAD_DIM, 2 * HEAD_DIM)
-                q_turn, o_turn = [
-                    jnp.concatenate(
-                        [heads_ref[kind, tile_at, pl.ds(at * HEAD_DIM, HEAD_DIM), :] for at in (head, head + 1)],
-                        axis=1,
-                    )
-                    for kind in (2, 3)
-                ]
-                scores = jnp.dot(key_pair, q_turn, preferred_element_type=F32)
-                dweights = jnp.dot(value_pair, o_turn, preferred_element_type=F32)
-                lse_row = jnp.concatenate([lse_delta[at:at + 1, :TILE] for at in (head, head + 1)], axis=1)
-                delta_row = jnp.concatenate([lse_delta[at:at + 1, TILE:] for at in (head, head + 1)], axis=1)
-                weights = jnp.exp2(scores * (score_scale * LOG2E) - lse_row * LOG2E)
-                weights = jnp.where(allowed, weights, 0.0)
-                weights_low[:, part] = weights.astype(BF16)
-                dscores_low[:, part] = (weights * (dweights - delta_row)).astype(BF16)
-            value_term = jnp.dot(weights_low[...], heads_ref[1, tile_at], preferred_element_type=F32)
-            key_term = jnp.dot(dscores_low[...], heads_ref[0, tile_at], preferred_element_type=F32)
-            dq_turn[...] += jnp.dot(key_turn, dscores_low[...], preferred_element_type=F32)
-            key_sum[first] += key_term[:TILE]
-            value_sum[first] += value_term[:TILE]
-            key_sum[second] += key_term[TILE:]
-            value_sum[second] += value_term[TILE:]
-            return carry
-
-        lax.fori_loop(0, (live_count + 1) // 2, pair_step, 0)
-        tile_grad = dq_turn[...] * score_scale
+    tiles = [lax.rem(place_ka + step, count_ka) for step in steps]
+    for number, step in enumerate(steps):
+        slot = count_ka - step if step else 0
+        packed = stats_ref[pl.ds(slot * spare, spare), :].astype(F32)
+        lse_delta[number] = (packed[:rows8] + packed[rows8:2 * rows8]) + packed[2 * rows8:3 * rows8]
+    dq_sum[...] = jnp.zeros_like(dq_sum)
+
+    def chunk_step(at, carry):
+        base = ENTRY * (at + 1)
+        turn_q, tile_at = table_ref[base], table_ref[base + 1]
+        first, second = table_ref[base + 2], table_ref[base + 3]
+        limits = jnp.where(lower, table_ref[base + 4], table_ref[base + 5])
+        allowed = reach >= limits
+        key_pair = jnp.concatenate([keys[first], keys[second]], axis=0)
+        value_pair = jnp.concatenate([values[first], values[second]], axis=0)
+        key_turn = jnp.concatenate([keys_t[first], keys_t[second]], axis=1)
+        for head in range(0, heads_dev, 2):
+            part = pl.ds(head * HEAD_DIM, 2 * HEAD_DIM)
+            scores = lax.dot_general(
+                key_pair, heads_ref[0, tile_at, part, :], LAST_DIMS, preferred_element_type=F32
+            )
+            dweights = lax.dot_general(
+                value_pair, heads_ref[1, tile_at, part, :], LAST_DIMS, preferred_element_type=F32
+            )
+            lse_row, delta_row = [
+                jnp.concatenate(
+                    [lse_delta[turn_q, at_head:at_head + 1, lanes] for at_head in (head, head + 1)], axis=1
+                )
+                for lanes in (slice(0, TILE), slice(TILE, 2 * TILE))
+            ]
+            weights = jnp.exp2(scores * (score_scale * LOG2E) - lse_row * LOG2E)
+            weights = jnp.where(allowed, weights, 0.0)
+            weights_low[:, part] = weights.astype(BF16)
+            dscores_low[:, part] = (weights * (dweights - delta_row)).astype(BF16)
+        value_term = jnp.dot(weights_low[...], heads_ref[1, tile_at], preferred_element_type=F32)
+        key_term = jnp.dot(dscores_low[...], heads_ref[0, tile_at], preferred_element_type=F32)
+        dq_sum[turn_q] += jnp.dot(key_turn, dscores_low[...], preferred_element_type=F32)
+        key_sum[first] += key_term[:TILE]
+        value_sum[first] += value_term[:TILE]
+        key_sum[second] += key_term[TILE:]
+        value_sum[second] += value_term[TILE:]
+        return carry
+
+    lax.fori_loop(0, table_ref[0], chunk_step, 0)
+    for number, tile_at in enumerate(tiles):
+        tile_grad = dq_sum[number] * score_scale
         if stage == 0:
             dq_out[tile_at] = tile_grad.astype(BF16)
-            return carry
-        if stage == 2:
-            tile_grad = tile_grad + dq_back[tile_at].astype(F32)
-        for number in range(len(steps)):
-            @pl.when(turn_q == number)
-            def _():
-                dq_outs[number][...] = tile_grad.astype(dq_outs[number].dtype)
-        return carry
-
-    lax.fori_loop(0, len(steps), query_step, 0)
+        else:
+            if stage == 2:
+                tile_grad = tile_grad + dq_back[tile_at].astype(F32)
+            dq_outs[number][...] = tile_grad.astype(dq_outs[number].dtype)
     if stage != 2:
         return
 
@@ -230,18 +258,18 @@
     return jnp.where(rows < 3, packed, 0.0)
 
 
-def add_kernel(dims, place_ref, other_ref, *rest):
+def add_kernel(dims, other_ref, *rest):
     count_ka, steps = dims
     parts, outs = rest[:len(steps)], rest[len(steps):]
     for number, step in enumerate(steps):
-        tile_at = lax.rem(place_ref[1] + step, count_ka)
+        tile_at = lax.rem(places()[1] + step, count_ka)
         outs[number][...] = (parts[number][...] + other_ref[tile_at].astype(F32)).astype(BF16)
 
 
-def collect_kernel(dims, place_ref, key_gain_ref, value_gain_ref, *rest):
+def collect_kernel(dims, key_gain_ref, value_gain_ref, *rest):
     count_chip, count_ka, share = dims
     parts, outs = rest[:count_chip], rest[count_chip:]
-    kv_at = pl.ds(pl.multiple_of(place_ref[1] // share * HEAD_DIM, HEAD_DIM), HEAD_DIM)
+    kv_at = pl.ds(pl.multiple_of(places()[1] // share * HEAD_DIM, HEAD_DIM), HEAD_DIM)
     gain = jnp.concatenate([key_gain_ref[:, kv_at], value_gain_ref[:, kv_at]], axis=1)
     for step in range(count_ka):
         rows = pl.ds(step * TILE, TILE)
@@ -268,7 +296,7 @@
             target[:, part] = source[:, part].T
 
 
-def place_kernel(dims, place_ref, *rest):
+def place_kernel(dims, *rest):
     count_ka, heads_dev, late = dims
     dq_parts, rest = rest[:count_ka], rest[count_ka:]
     dq_out, rest = rest[0], rest[1:]
@@ -276,7 +304,7 @@
     width = heads_dev * HEAD_DIM
     copies = []
     for step in tuple(at for at in range(count_ka) if at not in late) + late:
-        source = lax.rem(place_ref[1] - step + count_ka, count_ka)
+        source = lax.rem(places()[1] - step + count_ka, count_ka)
         columns = pl.ds(pl.multiple_of(source * width, HEAD_DIM), width)
         piece = dq_parts[step]
         if step in late:
@@ -288,11 +316,11 @@
         copy.wait()
 
 
-def finish_kernel(dims, place_ref, key_gain_ref, value_gain_ref, *rest):
+def finish_kernel(dims, key_gain_ref, value_gain_ref, *rest):
     count_ka, share = dims
     pieces, rest = rest[:count_ka], rest[count_ka:]
     dk_out, dv_out, gains_out, sums = rest
-    place_ka = place_ref[1]
+    _, place_ka = places()
     sums[...] = jnp.zeros_like(sums)
     for step in range(count_ka):
         source = lax.rem(place_ka + step, count_ka)
@@ -394,11 +422,11 @@
             num_scalar_prefetch=1,
             grid=(count_ka,),
             in_specs=[pl.BlockSpec((TILE, width), lambda i, s: (i, s[1]))] * 2,
-            out_specs=pl.BlockSpec((4, 1, width, HEAD_DIM), lambda i, s: (0, i, 0, 0)),
+            out_specs=pl.BlockSpec((2, 1, width, HEAD_DIM), lambda i, s: (0, i, 0, 0)),
         ),
-        out_shape=jax.ShapeDtypeStruct((4, count_ka, width, HEAD_DIM), BF16),
+        out_shape=jax.ShapeDtypeStruct((2, count_ka, width, HEAD_DIM), BF16),
         compiler_params=params(60),
-        cost_estimate=pl.CostEstimate(flops=0, bytes_accessed=12 * query_rows * width, transcendentals=0),
+        cost_estimate=pl.CostEstimate(flops=0, bytes_accessed=8 * query_rows * width, transcendentals=0),
         name="own_heads",
     )(later_place, queries, grad_out)
     messages, own_queries = lax.optimization_barrier((messages, own_queries))
@@ -406,68 +434,79 @@
     own_stats = jnp.concatenate([message[TILE:] for message in messages], axis=0)
     blocks = [own_block] + [swap(own_block, 2 * number) for number in range(1, count_chip)]
     other_stats = swap(own_stats, 1)
+    later_order, _ = lax.optimization_barrier((block_order, own_block))
     other_queries = swap(own_queries, 1)
 
     key_tiles = count_chip * count_ka
     sum_shape = jax.ShapeDtypeStruct((key_tiles, TILE, HEAD_DIM), F32)
     key_shape = jax.ShapeDtypeStruct((key_tiles, TILE, HEAD_DIM), BF16)
     kv_shape = (query_rows + SPARE, 2 * HEAD_DIM)
-    work = [
-        VMEM((head_rows(heads_dev), 2 * TILE), F32),
-        VMEM((2 * TILE, width), BF16),
-        VMEM((2 * TILE, width), BF16),
-        VMEM((HEAD_DIM, width), F32),
-        SMEM((key_tiles + 2,), jnp.int32),
-        SMEM((key_tiles + 2,), jnp.int32),
-    ]
     half = count_ka // 2
     early = (half, 0)
     late = tuple(step for step in range(1, count_ka) if step != half)
-    scalars = (place, block_order, doc_ids, tile_mask)
-
-    def attend(stage, steps, outs, scratch, *operands):
+    stages = ((1, tuple(range(count_ka))), (0, early), (0, late))
+    tables = pl.pallas_call(
+        functools.partial(plan_kernel, (count_chip, count_ka, stages)),
+        in_specs=in_smem(3),
+        out_specs=in_smem(len(stages)),
+        out_shape=[
+            jax.ShapeDtypeStruct((ENTRY * (1 + len(steps) * (key_tiles + 1) // 2),), jnp.int32)
+            for _, steps in stages
+        ],
+        scratch_shapes=[SMEM((key_tiles + 2,), jnp.int32)] * 2,
+        cost_estimate=pl.CostEstimate(flops=0, bytes_accessed=1 << 22, transcendentals=0),
+        name="plan",
+    )(later_order, doc_ids, tile_mask)
+
+    def attend(stage, outs, scratch, *operands):
+        steps = stages[stage][1]
         dims = (count_chip, count_ka, heads_dev, share, stage, steps)
         pairs = len(steps) * key_tiles
         return pl.pallas_call(
             functools.partial(attention_kernel, dims),
-            in_specs=in_smem(4) + in_vmem(len(operands)),
+            in_specs=in_smem(1) + in_vmem(len(operands)),
             out_specs=in_vmem(len(outs)),
             out_shape=outs,
-            scratch_shapes=scratch + work,
+            scratch_shapes=scratch + [
+                VMEM((len(steps), head_rows(heads_dev), 2 * TILE), F32),
+                VMEM((2 * TILE, width), BF16),
+                VMEM((2 * TILE, width), BF16),
+                VMEM((len(steps), HEAD_DIM, width), F32),
+            ],
             compiler_params=params(14 + key_tiles // 2),
             cost_estimate=pl.CostEstimate(
                 flops=10 * pairs * TILE * TILE * width, bytes_accessed=1 << 22, transcendentals=0
             ),
             name=("attention_other", "attention_early", "attention_late")[stage],
-        )(*scalars, *operands)
+        )(tables[stage], *operands)
 
     part_shape = jax.ShapeDtypeStruct((HEAD_DIM, width), F32)
     full_shape = jax.ShapeDtypeStruct((HEAD_DIM, width), BF16)
     dq_other, *state = attend(
-        0, tuple(range(count_ka)),
+        0,
         [jax.ShapeDtypeStruct((count_ka, HEAD_DIM, width), BF16)] + [key_shape] * 3 + [sum_shape] * 2,
         [], key_gain, value_gain, other_queries, other_stats, *blocks,
     )
     dq_back = swap(dq_other, 1)
     keys, sums = state[:3], state[3:]
     *dq_early, key_sum, value_sum = attend(
-        1, early, [part_shape] * len(early) + [sum_shape] * 2, [],
+        1, [part_shape] * len(early) + [sum_shape] * 2, [],
         own_queries, own_stats, *keys, *sums,
     )
     added = pl.pallas_call(
         functools.partial(add_kernel, (count_ka, early)),
-        in_specs=in_smem(1) + in_vmem(1 + len(early)),
+        in_specs=in_vmem(1 + len(early)),
         out_specs=in_vmem(len(early)),
         out_shape=[full_shape] * len(early),
         compiler_params=params(16),
         name="add_queries",
-    )(place, dq_back, *dq_early)
+    )(dq_back, *dq_early)
     dq_parts = [None] * count_ka
     added = list(added)
     late_stats, added[-1] = lax.optimization_barrier((own_stats, added[-1]))
     dq_parts[half], dq_parts[0] = turn(added[0], half), added[1]
     results = attend(
-        2, late,
+        2,
         [full_shape] * len(late) + [jax.ShapeDtypeStruct(kv_shape, F32)]
         + [jax.ShapeDtypeStruct(kv_shape, BF16)] * (count_chip - 1),
         [VMEM(sum_shape.shape, F32)] * 2,
@@ -475,7 +514,7 @@
     )
     dq_late, kv_own = results[:len(late)], results[len(late):]
     kv_own = list(kv_own)
-    kv_own[-1], dq_parts[half] = lax.optimization_barrier((kv_own[-1], dq_parts[half]))
+    kv_own[2], dq_parts[half] = lax.optimization_barrier((kv_own[2], dq_parts[half]))
     kv_parts = [kv_own[0]] + [swap(kv_own[number], 2 * number) for number in range(1, count_chip)]
     for number, step in enumerate(late):
         dq_parts[step] = turn(dq_late[number], step)
@@ -484,17 +523,17 @@
     piece_shape = (TILE + SPARE, 2 * HEAD_DIM)
     totals = pl.pallas_call(
         functools.partial(collect_kernel, (count_chip, count_ka, share)),
-        in_specs=in_smem(1) + in_vmem(2 + count_chip),
+        in_specs=in_vmem(2 + count_chip),
         out_specs=in_vmem(count_ka),
         out_shape=[jax.ShapeDtypeStruct(piece_shape, piece_type)] * count_ka,
         compiler_params=params(24),
         name="collect",
-    )(place, key_gain, value_gain, *kv_parts)
+    )(key_gain, value_gain, *kv_parts)
     pieces = [totals[0]] + [turn(totals[step], -step) for step in range(1, count_ka)]
 
     grad_keys, grad_values, gains = pl.pallas_call(
         functools.partial(finish_kernel, (count_ka, share)),
-        in_specs=in_smem(1) + in_vmem(2 + count_ka),
+        in_specs=in_vmem(2 + count_ka),
         out_specs=in_vmem(3),
         out_shape=[
             jax.ShapeDtypeStruct(key_rows.shape, BF16),
@@ -504,7 +543,7 @@
         scratch_shapes=[VMEM((kv_heads, TILE + SPARE, 2 * HEAD_DIM), F32)],
         compiler_params=params(16),
         name="finish",
-    )(place, key_gain, value_gain, *pieces)
+    )(key_gain, value_gain, *pieces)
     gains = gains + swap(gains, 1)
     first = (0, half)
     turned = pl.pallas_call(
@@ -520,14 +559,14 @@
         dq_parts[step] = turned[number]
     grad_queries = pl.pallas_call(
         functools.partial(place_kernel, (count_ka, heads_dev, late)),
-        in_specs=in_smem(1) + in_vmem(count_ka),
+        in_specs=in_vmem(count_ka),
         out_specs=pl.BlockSpec(memory_space=pl.ANY),
         out_shape=jax.ShapeDtypeStruct((rows_dev, feat_width), BF16),
         scratch_shapes=[VMEM((TILE, width), BF16)] * len(late) + [pltpu.SemaphoreType.DMA((count_ka,))],
         compiler_params=params(16),
         cost_estimate=pl.CostEstimate(flops=0, bytes_accessed=4 * rows_dev * feat_width, transcendentals=0),
         name="place_queries",
-    )(place, *dq_parts)
+    )(*dq_parts)
     return grad_queries, grad_keys, grad_values, gains[0], gains[1]
 
 

time: 89.5 us -> 83.9 us (0.937); the launches traced: 90.3 us -> 83 us
  waiting for transfers between devices: 32.6 us -> 27.8 us
  Pallas kernels: 32.1 us -> 27.6 us
  starting transfers between devices: 23.3 us -> 24.7 us
    pallas_call x3, Pallas kernels: 18.5 us -> 13.8 us  [attend(): pl.pallas_call(functools.partial(attention_kernel, dims), in_specs=in_sme...]
    ppermute x10, waiting for transfers between devices: 17.3 us -> 13.4 us  [swap(): lax.ppermute(array, 'pb', [(at, at ^ number) for at in range(count_pb)])]
    pallas_call x0 -> x1, Pallas kernels: none -> 3.07 us  [shards(): pl.pallas_call(functools.partial(plan_kernel, (count_chip, count_ka, stag...]
    ppermute x9, starting transfers between devices: 13.8 us -> 16 us  [turn(): lax.ppermute(array, 'ka', [(at, (at + step) % count_ka) for at in range(c...]
    ppermute x9, waiting for transfers between devices: 15.4 us -> 14.4 us  [turn(): lax.ppermute(array, 'ka', [(at, (at + step) % count_ka) for at in range(c...]
  transfers between devices with their start and end apart: 19 -> 19, of which waited for: 9 -> 7; matrix products, arithmetic and copies ran while one was open for 0% -> 0% of each run, Pallas kernels for 23% -> 24%
where the time goes in v1:
time: 83.9 us; the launch traced here: 83 us
  waiting for transfers between devices  27.8 us (33%)
  Pallas kernels  27.6 us (33%)
  starting transfers between devices  24.7 us (29%)
  local copies, waits for them, and re-layouts  1.32 us (2%)
  between operations  0.87 us (1%)
    ppermute x9, starting transfers between devices, turn(): lax.ppermute(array, 'ka', [(at, (at + step) % count_ka) for at in range(c...  16 us
    ppermute x9, waiting for transfers between devices, turn(): lax.ppermute(array, 'ka', [(at, (at + step) % count_ka) for at in range(c...  14.4 us
    pallas_call x3, Pallas kernels, attend(): pl.pallas_call(functools.partial(attention_kernel, dims), in_specs=in_sme...  13.8 us
    ppermute x10, waiting for transfers between devices, swap(): lax.ppermute(array, 'pb', [(at, at ^ number) for at in range(count_pb)])  13.4 us
    ppermute x10, starting transfers between devices, swap(): lax.ppermute(array, 'pb', [(at, at ^ number) for at in range(count_pb)])  8.73 us
    pallas_call x1, Pallas kernels, shards(): pl.pallas_call(own_heads_kernel, grid_spec=pltpu.PrefetchScalarGridSpec(n...  4.67 us
    pallas_call x1, Pallas kernels, shards(): pl.pallas_call(functools.partial(prepare_kernel, (count_ka, heads, heads_...  3.73 us
    pallas_call x1, Pallas kernels, shards(): pl.pallas_call(functools.partial(plan_kernel, (count_chip, count_ka, stag...  3.07 us
  transfers between devices with their start and end apart: 19, of which 7 were waited for; matrix products, arithmetic and copies ran while one was open for 0% of the time, Pallas kernels for 24%

profile of v1, /device:TPU:0, one launch (start us, length us, event | category | flops | bytes accessed | tf_op | source)
XLA Modules:
  0.0 83.0 jit_solution(9195737916992939416)
XLA Ops:
  0.6 0.6 pad_add_fusion.place_ref
  1.2 3.7 %prepare.1 = (bf16[160,256]{1,0:T(8,128)(2,1)}, bf16[160,256]{1,0:T(8,128)(2,1)}, bf16[160,256]{1,0:T(8,128)(2,1)}, bf16[160,256]{1,0:T(8,128)(2,1)}) custom-call(s32[2]{0:T(128)} %pad_add_fusion.place_ref, bf16[128,512]{1,0:T(8,128)(2,1)} %key_ref.1, bf16[128,512]{1,0:T(8,128)(2,1)} %value_ref.1, bf16[128,4096]{1,0:T(8,128)(2,1)} %attn_ref.1, ...), custom_call_target="tpu_custom_call" | custom-call | tf_op jit(solution)/shard_map/prepare/pallas_call | solution.py:397
  5.0 3.0 %collective-permute-start = (bf16[160,256]{1,0:T(8,128)(2,1)}, bf16[160,256]{1,0:T(8,128)(2,1)S(1)}, u32[]{:S(2)}, u32[]{:S(2)}) collective-permute-start(bf16[160,256]{1,0:T(8,128)(2,1)} %get-tuple-element.51), channel_id=1, source_target_pairs={{0,1},{1,2},{2,3},{3,0},{4,5},{5,6},{6,7},{7,4},{8,9},{9,10},{10,1... | collective-permute-start | bytes 245768 | tf_op jit(solution)/shard_map/ppermute | solution.py:395
  8.0 2.6 %collective-permute-start.1 = (bf16[160,256]{1,0:T(8,128)(2,1)}, bf16[160,256]{1,0:T(8,128)(2,1)S(1)}, u32[]{:S(2)}, u32[]{:S(2)}) collective-permute-start(bf16[160,256]{1,0:T(8,128)(2,1)} %get-tuple-element.52), channel_id=1, source_target_pairs={{0,2},{1,3},{2,0},{3,1},{4,6},{5,7},{6,4},{7,5},{8,10},{9,11},{10,... | collective-permute-start | bytes 245768 | tf_op jit(solution)/shard_map/ppermute | solution.py:395
  10.6 1.3 %collective-permute-start.2 = (bf16[160,256]{1,0:T(8,128)(2,1)}, bf16[160,256]{1,0:T(8,128)(2,1)S(1)}, u32[]{:S(2)}, u32[]{:S(2)}) collective-permute-start(bf16[160,256]{1,0:T(8,128)(2,1)} %get-tuple-element.53), channel_id=1, source_target_pairs={{0,3},{1,0},{2,1},{3,2},{4,7},{5,4},{6,5},{7,6},{8,11},{9,8},{10,9... | collective-permute-start | bytes 245768 | tf_op jit(solution)/shard_map/ppermute | solution.py:395
  11.9 0.0 copy-start.6
  11.9 0.0 copy-start.1
  11.9 0.0 copy-start.2
  11.9 4.7 %own_heads.1.rest_0_ = bf16[2,4,1024,128]{3,2,1,0:T(8,128)(2,1)} custom-call(s32[2]{0:T(128)} %pad_add_fusion.place_ref, bf16[512,4096]{1,0:T(8,128)(2,1)} %queries_ref.1, bf16[512,4096]{1,0:T(8,128)(2,1)} %grads_ref.1), custom_call_target="tpu_custom_call" | custom-call | bytes 4194304 | tf_op jit(solution)/shard_map/own_heads/pallas_call | solution.py:419
  16.6 0.0 collective-permute-done
  16.6 0.0 collective-permute-done.1
  16.6 0.0 collective-permute-done.2
  16.6 0.1 collective-permute-start.3
  16.7 0.0 copy-done.6
  16.8 2.5 %collective-permute-start.7 = (bf16[512,256]{1,0:T(8,128)(2,1)S(1)}, bf16[512,256]{1,0:T(8,128)(2,1)S(1)}, u32[]{:S(2)}, u32[]{:S(2)}) collective-permute-start(bf16[512,256]{1,0:T(8,128)(2,1)S(1)} %pad_maximum_fusion.rest_4_.rest_2_), channel_id=1, source_target_pairs={{0,24},{4,28},{8,16},{12,20},{16,8},{20,12},{24,0},{28,4},{1,25},{... | collective-permute-start | bytes 786440 | tf_op jit(solution)/shard_map/ppermute | solution.py:392
  19.3 0.5 collective-permute-start.6
  19.8 0.5 collective-permute-start.5
  20.4 0.1 collective-permute-start.4
  20.5 3.1 %plan.1 = (s32[280]{0:T(512)}, s32[144]{0:T(256)}, s32[144]{0:T(256)}) custom-call(s32[32]{0:T(128)} %order_ref, s32[32]{0:T(128)} %doc_ref.1, s32[32,32]{1,0:T(8,128)} %mask_ref.1), custom_call_target="tpu_custom_call" | custom-call | bytes 4194304 | tf_op jit(solution)/shard_map/plan/pallas_call | solution.py:448
  23.5 0.0 collective-permute-done.4.rest_3_
  23.5 3.4 %collective-permute-done.7.rest_7_.rest_5_ = bf16[512,256]{1,0:T(8,128)(2,1)S(1)} collective-permute-done((bf16[512,256]{1,0:T(8,128)(2,1)S(1)}, bf16[512,256]{1,0:T(8,128)(2,1)S(1)}, u32[]{:S(2)}, u32[]{:S(2)}) %collective-permute-start.7) | collective-permute-done | bytes 262176 | tf_op jit(solution)/shard_map/ppermute | solution.py:392
  26.9 5.2 %collective-permute-done.6.rest_6_.rest_4_ = bf16[512,256]{1,0:T(8,128)(2,1)S(1)} collective-permute-done((bf16[512,256]{1,0:T(8,128)(2,1)S(1)}, bf16[512,256]{1,0:T(8,128)(2,1)S(1)}, u32[]{:S(2)}, u32[]{:S(2)}) %collective-permute-start.6) | collective-permute-done | bytes 262176 | tf_op jit(solution)/shard_map/ppermute | solution.py:392
  32.1 0.1 collective-permute-done.5.rest_5_.rest_3_
  32.2 0.0 collective-permute-done.3.rest_2_
  32.2 0.0 copy-done.1
  32.2 0.0 copy-done.2
  32.2 0.0 copy-start.3
  32.2 0.7 copy-done.3
  32.9 0.0 copy-start
  32.9 0.0 copy-start.5
  32.9 3.7 %attention_other.1 = (bf16[4,128,1024]{2,1,0:T(8,128)(2,1)S(1)}, bf16[16,128,128]{2,1,0:T(8,128)(2,1)S(1)}, bf16[16,128,128]{2,1,0:T(8,128)(2,1)S(1)}, bf16[16,1...) custom-call(s32[280]{0:T(512)S(1)} %copy-done.3, f32[1,512]{1,0:T(1,128)S(1)} %bitcast.6, ...), custom_call_target="tpu_custom_call" | custom-call | flops 10737418240 | bytes 4194304 | tf_op jit(solution)/shard_map/attention_other/pallas_call | solution.py:465
  36.6 4.9 %collective-permute-start.8 = (bf16[4,128,1024]{2,1,0:T(8,128)(2,1)S(1)}, bf16[4,128,1024]{2,1,0:T(8,128)(2,1)S(1)}, u32[]{:S(2)}, u32[]{:S(2)}) collective-permute-start(bf16[4,128,1024]{2,1,0:T(8,128)(2,1)S(1)} %get-tuple-element.62), channel_id=1, source_target_pairs={{0,4},{4,0},{8,12},{12,8},{16,20},{20,16},{24,28},{28,24},{1,5},{5... | collective-permute-start | bytes 3145736 | tf_op jit(solution)/shard_map/ppermute | solution.py:392
  41.4 0.0 copy-done
  41.4 0.0 copy-done.5
  41.4 4.1 %attention_early.1 = (f32[128,1024]{1,0:T(8,128)S(1)}, f32[128,1024]{1,0:T(8,128)S(1)}, f32[16,128,128]{2,1,0:T(8,128)S(1)}, f32[16,128,128]{2,1,0:T(8,128)S(1)}) custom-call(s32[144]{0:T(256)S(1)} %copy-done.5, bf16[2,4,1024,128]{3,2,1,0:T(8,128)(2,1)S(1)} %copy-done, bf16[128,256]{1,0:T(8,128)(2,1)S(1)} %pad_maximum_fusion.1.rest_1_, ...), custom_call_target="tpu_custom_call" | custom-call | flops 5368709120 | bytes 4194304 | tf_op jit(solution)/shard_map/attention_early/pallas_call | solution.py:465
  45.5 0.0 collective-permute-done.8.other_ref.rest_11_
  45.5 0.1 add_queries.1
  45.6 1.3 %collective-permute-start.9 = (bf16[128,1024]{1,0:T(8,128)(2,1)S(1)}, bf16[128,1024]{1,0:T(8,128)(2,1)S(1)}, u32[]{:S(2)}, u32[]{:S(2)}) collective-permute-start(bf16[128,1024]{1,0:T(8,128)(2,1)S(1)} %get-tuple-element.78), channel_id=1, source_target_pairs={{0,2},{1,3},{2,0},{3,1},{4,6},{5,7},{6,4},{7,5},{8,10},{9,11},{10,... | collective-permute-start | bytes 786440 | tf_op jit(solution)/shard_map/ppermute | solution.py:395
  47.0 0.0 copy-done.4
  47.0 6.1 %attention_late.1 = (bf16[128,1024]{1,0:T(8,128)(2,1)S(1)}, bf16[128,1024]{1,0:T(8,128)(2,1)S(1)}, f32[528,256]{1,0:T(8,128)S(1)}, bf16[528,256]{1,0:T(8,128)(2,...) custom-call(s32[144]{0:T(256)S(1)} %copy-done.4, bf16[2,4,1024,128]{3,2,1,0:T(8,128)(2,1)S(1)} %copy-done, ...), custom_call_target="tpu_custom_call" | custom-call | flops 5368709120 | bytes 4194304 | tf_op jit(solution)/shard_map/attention_late/pallas_call | solution.py:465
  53.0 0.1 collective-permute-start.12
  53.1 0.1 collective-permute-start.14
  53.2 6.5 %collective-permute-done.9.refs_1_ = bf16[128,1024]{1,0:T(8,128)(2,1)S(1)} collective-permute-done((bf16[128,1024]{1,0:T(8,128)(2,1)S(1)}, bf16[128,1024]{1,0:T(8,128)(2,1)S(1)}, u32[]{:S(2)}, u32[]{:S(2)}) %collective-permute-start.9) | collective-permute-done | bytes 262176 | tf_op jit(solution)/shard_map/ppermute | solution.py:395
  59.7 0.0 collective-permute-start.13
  59.7 0.0 collective-permute-start.10
  59.7 3.8 %collective-permute-start.11 = (bf16[128,1024]{1,0:T(8,128)(2,1)S(1)}, bf16[128,1024]{1,0:T(8,128)(2,1)S(1)}, u32[]{:S(2)}, u32[]{:S(2)}) collective-permute-start(bf16[128,1024]{1,0:T(8,128)(2,1)S(1)} %get-tuple-element.83), channel_id=1, source_target_pairs={{0,3},{1,0},{2,1},{3,2},{4,7},{5,4},{6,5},{7,6},{8,11},{9,8},{10,9... | collective-permute-start | bytes 786440 | tf_op jit(solution)/shard_map/ppermute | solution.py:395
  63.5 0.0 collective-permute-done.12.rest_1_
  63.5 0.0 collective-permute-done.14.rest_3_
  63.5 4.8 %collective-permute-done.13.rest_2_ = bf16[528,256]{1,0:T(8,128)(2,1)S(1)} collective-permute-done((bf16[528,256]{1,0:T(8,128)(2,1)S(1)}, bf16[528,256]{1,0:T(8,128)(2,1)S(1)}, u32[]{:S(2)}, u32[]{:S(2)}) %collective-permute-start.13) | collective-permute-done | bytes 270368 | tf_op jit(solution)/shard_map/ppermute | solution.py:392
  68.3 0.2 collect.1
  68.4 3.0 %collective-permute-start.15 = (bf16[144,256]{1,0:T(8,128)(2,1)S(1)}, bf16[144,256]{1,0:T(8,128)(2,1)S(1)}, u32[]{:S(2)}, u32[]{:S(2)}) collective-permute-start(bf16[144,256]{1,0:T(8,128)(2,1)S(1)} %get-tuple-element.89), channel_id=1, source_target_pairs={{0,3},{1,0},{2,1},{3,2},{4,7},{5,4},{6,5},{7,6},{8,11},{9,8},{10,9... | collective-permute-start | bytes 221192 | tf_op jit(solution)/shard_map/ppermute | solution.py:395
  71.4 0.8 %collective-permute-start.16 = (bf16[144,256]{1,0:T(8,128)(2,1)S(1)}, bf16[144,256]{1,0:T(8,128)(2,1)S(1)}, u32[]{:S(2)}, u32[]{:S(2)}) collective-permute-start(bf16[144,256]{1,0:T(8,128)(2,1)S(1)} %get-tuple-element.90), channel_id=1, source_target_pairs={{0,2},{1,3},{2,0},{3,1},{4,6},{5,7},{6,4},{7,5},{8,10},{9,11},{10,... | collective-permute-start | bytes 221192 | tf_op jit(solution)/shard_map/ppermute | solution.py:395
  72.3 0.0 collective-permute-start.17
  72.3 1.9 %collective-permute-done.15.rest_1_ = bf16[144,256]{1,0:T(8,128)(2,1)S(1)} collective-permute-done((bf16[144,256]{1,0:T(8,128)(2,1)S(1)}, bf16[144,256]{1,0:T(8,128)(2,1)S(1)}, u32[]{:S(2)}, u32[]{:S(2)}) %collective-permute-start.15) | collective-permute-done | bytes 73760 | tf_op jit(solution)/shard_map/ppermute | solution.py:395
  74.2 6.1 %collective-permute-done.16.rest_2_ = bf16[144,256]{1,0:T(8,128)(2,1)S(1)} collective-permute-done((bf16[144,256]{1,0:T(8,128)(2,1)S(1)}, bf16[144,256]{1,0:T(8,128)(2,1)S(1)}, u32[]{:S(2)}, u32[]{:S(2)}) %collective-permute-start.16) | collective-permute-done | bytes 73760 | tf_op jit(solution)/shard_map/ppermute | solution.py:395
  80.2 0.0 collective-permute-done.17.rest_3_
  80.2 0.8 %finish.1 = (bf16[128,512]{1,0:T(8,128)(2,1)}, bf16[128,512]{1,0:T(8,128)(2,1)}, f32[2,512]{1,0:T(2,128)S(1)}) custom-call(f32[1,512]{1,0:T(1,128)S(1)} %bitcast.8, f32[1,512]{1,0:T(1,128)S(1)} %bitcast.11, bf16[144,256]{1,0:T(8,128)(2,1)S(1)} %get-tuple-element.88.rest_0_, bf16[144,256]{1,0:T(8,128)(2,1)S(1)} %collective-permute-done.15.rest_1_, ...), custom_call_target="tpu_custom_call" | custom-call | tf_op jit(solution)/shard_map/finish/pallas_call | solution.py:534
  81.1 0.0 collective-permute-start.18
  81.1 0.2 turn_queries.1
  81.3 0.0 collective-permute-done.10.rest_1_
  81.3 0.0 collective-permute-done.11.rest_3_
  81.3 1.0 %place_queries.1 = bf16[128,4096]{1,0:T(8,128)(2,1)} custom-call(bf16[128,1024]{1,0:T(8,128)(2,1)S(1)} %get-tuple-element.80.rest_0_, bf16[128,1024]{1,0:T(8,128)(2,1)S(1)} %collective-permute-done.10.rest_1_, bf16[128,1024]{1,0:T(8,128)(2,1)S(1)} %get-tuple-element.82.rest_2_, bf16[128,1024]{1,0:T(8,128)(2,1)S(1)} %collective-permute-done.11.rest_3_), custom_call_target="tpu_custom_call" | custom-call | bytes 2097152 | tf_op jit(solution)/shard_map/place_queries/pallas_call | solution.py:560
  82.4 0.0 collective-permute-done.18
  82.4 0.6 fusion
  (12 shorter events, 0.1 us)
Async XLA Ops:
  5.0 11.6 %collective-permute-start = (bf16[160,256]{1,0:T(8,128)(2,1)}, bf16[160,256]{1,0:T(8,128)(2,1)S(1)}, u32[]{:S(2)}, u32[]{:S(2)}) collective-permute-start(bf16[160,256]{1,0:T(8,128)(2,1)} %get-tuple-element.51), channel_id=1, source_target_pairs={{0,1},{1,2},{2,3},{3,0},{4,5},{5,6},{6,7},{7,4},{8,9},{9,10},{10,1... | collective-permute-start | bytes 245768 | tf_op jit(solution)/shard_map/ppermute | solution.py:395
  8.0 8.6 %collective-permute-start.1 = (bf16[160,256]{1,0:T(8,128)(2,1)}, bf16[160,256]{1,0:T(8,128)(2,1)S(1)}, u32[]{:S(2)}, u32[]{:S(2)}) collective-permute-start(bf16[160,256]{1,0:T(8,128)(2,1)} %get-tuple-element.52), channel_id=1, source_target_pairs={{0,2},{1,3},{2,0},{3,1},{4,6},{5,7},{6,4},{7,5},{8,10},{9,11},{10,... | collective-permute-start | bytes 245768 | tf_op jit(solution)/shard_map/ppermute | solution.py:395
  10.6 6.0 %collective-permute-start.2 = (bf16[160,256]{1,0:T(8,128)(2,1)}, bf16[160,256]{1,0:T(8,128)(2,1)S(1)}, u32[]{:S(2)}, u32[]{:S(2)}) collective-permute-start(bf16[160,256]{1,0:T(8,128)(2,1)} %get-tuple-element.53), channel_id=1, source_target_pairs={{0,3},{1,0},{2,1},{3,2},{4,7},{5,4},{6,5},{7,6},{8,11},{9,8},{10,9... | collective-permute-start | bytes 245768 | tf_op jit(solution)/shard_map/ppermute | solution.py:395
  11.9 4.8 %copy-start.6 = (bf16[160,256]{1,0:T(8,128)(2,1)S(1)}, bf16[160,256]{1,0:T(8,128)(2,1)}, u32[]{:S(2)}) copy-start(bf16[160,256]{1,0:T(8,128)(2,1)} %get-tuple-element.55) | copy-start | bytes 245764
  11.9 20.3 %copy-start.1 = (f32[512]{0:T(512)S(1)}, f32[512]{0:T(512)}, u32[]{:S(2)}) copy-start(f32[512]{0:T(512)} %param.17) | copy-start | bytes 6148
  11.9 20.3 %copy-start.2 = (f32[512]{0:T(512)S(1)}, f32[512]{0:T(512)}, u32[]{:S(2)}) copy-start(f32[512]{0:T(512)} %param.18) | copy-start | bytes 6148
  16.6 15.6 %collective-permute-start.3 = (bf16[2,4,1024,128]{3,2,1,0:T(8,128)(2,1)}, bf16[2,4,1024,128]{3,2,1,0:T(8,128)(2,1)S(1)}, u32[]{:S(2)}, u32[]{:S(2)}) collective-permute-start(bf16[2,4,1024,128]{3,2,1,0:T(8,128)(2,1)} %own_heads.1.rest_0_), channel_id=1, source_target_pairs={{0,4},{4,0},{8,12},{12,8},{16,20},{20,16},{24,28},{28,24},{1,5},{5... | collective-permute-start | bytes 6291464 | tf_op jit(solution)/shard_map/ppermute | solution.py:392
  16.8 10.1 %collective-permute-start.7 = (bf16[512,256]{1,0:T(8,128)(2,1)S(1)}, bf16[512,256]{1,0:T(8,128)(2,1)S(1)}, u32[]{:S(2)}, u32[]{:S(2)}) collective-permute-start(bf16[512,256]{1,0:T(8,128)(2,1)S(1)} %pad_maximum_fusion.rest_4_.rest_2_), channel_id=1, source_target_pairs={{0,24},{4,28},{8,16},{12,20},{16,8},{20,12},{24,0},{28,4},{1,25},{... | collective-permute-start | bytes 786440 | tf_op jit(solution)/shard_map/ppermute | solution.py:392
  19.3 12.8 %collective-permute-start.6 = (bf16[512,256]{1,0:T(8,128)(2,1)S(1)}, bf16[512,256]{1,0:T(8,128)(2,1)S(1)}, u32[]{:S(2)}, u32[]{:S(2)}) collective-permute-start(bf16[512,256]{1,0:T(8,128)(2,1)S(1)} %pad_maximum_fusion.rest_4_.rest_2_), channel_id=1, source_target_pairs={{0,16},{4,20},{8,24},{12,28},{16,0},{20,4},{24,8},{28,12},{1,17},{... | collective-permute-start | bytes 786440 | tf_op jit(solution)/shard_map/ppermute | solution.py:392
  19.8 12.4 %collective-permute-start.5 = (bf16[512,256]{1,0:T(8,128)(2,1)S(1)}, bf16[512,256]{1,0:T(8,128)(2,1)S(1)}, u32[]{:S(2)}, u32[]{:S(2)}) collective-permute-start(bf16[512,256]{1,0:T(8,128)(2,1)S(1)} %pad_maximum_fusion.rest_4_.rest_2_), channel_id=1, source_target_pairs={{0,8},{4,12},{8,0},{12,4},{16,24},{20,28},{24,16},{28,20},{1,9},{5... | collective-permute-start | bytes 786440 | tf_op jit(solution)/shard_map/ppermute | solution.py:392
  20.4 3.2 %collective-permute-start.4 = (bf16[128,256]{1,0:T(8,128)(2,1)S(1)}, bf16[128,256]{1,0:T(8,128)(2,1)S(1)}, u32[]{:S(2)}, u32[]{:S(2)}) collective-permute-start(bf16[128,256]{1,0:T(8,128)(2,1)S(1)} %pad_maximum_fusion.1.rest_1_), channel_id=1, source_target_pairs={{0,4},{4,0},{8,12},{12,8},{16,20},{20,16},{24,28},{28,24},{1,5},{5... | collective-permute-start | bytes 196616 | tf_op jit(solution)/shard_map/ppermute | solution.py:392
  32.2 0.7 copy-start.3
  32.9 8.6 %copy-start = (bf16[2,4,1024,128]{3,2,1,0:T(8,128)(2,1)S(1)}, bf16[2,4,1024,128]{3,2,1,0:T(8,128)(2,1)}, u32[]{:S(2)}) copy-start(bf16[2,4,1024,128]{3,2,1,0:T(8,128)(2,1)} %own_heads.1.rest_0_) | copy-start | bytes 6291460
  32.9 8.6 %copy-start.5 = (s32[144]{0:T(256)S(1)}, s32[144]{0:T(256)}, u32[]{:S(2)}) copy-start(s32[144]{0:T(256)} %get-tuple-element.63.table_ref) | copy-start | bytes 1732
  36.6 8.9 %collective-permute-start.8 = (bf16[4,128,1024]{2,1,0:T(8,128)(2,1)S(1)}, bf16[4,128,1024]{2,1,0:T(8,128)(2,1)S(1)}, u32[]{:S(2)}, u32[]{:S(2)}) collective-permute-start(bf16[4,128,1024]{2,1,0:T(8,128)(2,1)S(1)} %get-tuple-element.62), channel_id=1, source_target_pairs={{0,4},{4,0},{8,12},{12,8},{16,20},{20,16},{24,28},{28,24},{1,5},{5... | collective-permute-start | bytes 3145736 | tf_op jit(solution)/shard_map/ppermute | solution.py:392
  41.4 5.5 %copy-start.4 = (s32[144]{0:T(256)S(1)}, s32[144]{0:T(256)}, u32[]{:S(2)}) copy-start(s32[144]{0:T(256)} %get-tuple-element.73.table_ref) | copy-start | bytes 1732
  45.6 14.0 %collective-permute-start.9 = (bf16[128,1024]{1,0:T(8,128)(2,1)S(1)}, bf16[128,1024]{1,0:T(8,128)(2,1)S(1)}, u32[]{:S(2)}, u32[]{:S(2)}) collective-permute-start(bf16[128,1024]{1,0:T(8,128)(2,1)S(1)} %get-tuple-element.78), channel_id=1, source_target_pairs={{0,2},{1,3},{2,0},{3,1},{4,6},{5,7},{6,4},{7,5},{8,10},{9,11},{10,... | collective-permute-start | bytes 786440 | tf_op jit(solution)/shard_map/ppermute | solution.py:395
  53.0 10.4 %collective-permute-start.12 = (bf16[528,256]{1,0:T(8,128)(2,1)S(1)}, bf16[528,256]{1,0:T(8,128)(2,1)S(1)}, u32[]{:S(2)}, u32[]{:S(2)}) collective-permute-start(bf16[528,256]{1,0:T(8,128)(2,1)S(1)} %get-tuple-element.85), channel_id=1, source_target_pairs={{0,8},{4,12},{8,0},{12,4},{16,24},{20,28},{24,16},{28,20},{1,9},{5... | collective-permute-start | bytes 811016 | tf_op jit(solution)/shard_map/ppermute | solution.py:392
  53.1 10.4 %collective-permute-start.14 = (bf16[528,256]{1,0:T(8,128)(2,1)S(1)}, bf16[528,256]{1,0:T(8,128)(2,1)S(1)}, u32[]{:S(2)}, u32[]{:S(2)}) collective-permute-start(bf16[528,256]{1,0:T(8,128)(2,1)S(1)} %get-tuple-element.87), channel_id=1, source_target_pairs={{0,24},{4,28},{8,16},{12,20},{16,8},{20,12},{24,0},{28,4},{1,25},{... | collective-permute-start | bytes 811016 | tf_op jit(solution)/shard_map/ppermute | solution.py:392
  59.7 8.6 %collective-permute-start.13 = (bf16[528,256]{1,0:T(8,128)(2,1)S(1)}, bf16[528,256]{1,0:T(8,128)(2,1)S(1)}, u32[]{:S(2)}, u32[]{:S(2)}) collective-permute-start(bf16[528,256]{1,0:T(8,128)(2,1)S(1)} %get-tuple-element.86), channel_id=1, source_target_pairs={{0,16},{4,20},{8,24},{12,28},{16,0},{20,4},{24,8},{28,12},{1,17},{... | collective-permute-start | bytes 811016 | tf_op jit(solution)/shard_map/ppermute | solution.py:392
  59.7 21.6 %collective-permute-start.10 = (bf16[128,1024]{1,0:T(8,128)(2,1)S(1)}, bf16[128,1024]{1,0:T(8,128)(2,1)S(1)}, u32[]{:S(2)}, u32[]{:S(2)}) collective-permute-start(bf16[128,1024]{1,0:T(8,128)(2,1)S(1)} %get-tuple-element.81), channel_id=1, source_target_pairs={{0,1},{1,2},{2,3},{3,0},{4,5},{5,6},{6,7},{7,4},{8,9},{9,10},{10,1... | collective-permute-start | bytes 786440 | tf_op jit(solution)/shard_map/ppermute | solution.py:395
  59.7 21.6 %collective-permute-start.11 = (bf16[128,1024]{1,0:T(8,128)(2,1)S(1)}, bf16[128,1024]{1,0:T(8,128)(2,1)S(1)}, u32[]{:S(2)}, u32[]{:S(2)}) collective-permute-start(bf16[128,1024]{1,0:T(8,128)(2,1)S(1)} %get-tuple-element.83), channel_id=1, source_target_pairs={{0,3},{1,0},{2,1},{3,2},{4,7},{5,4},{6,5},{7,6},{8,11},{9,8},{10,9... | collective-permute-start | bytes 786440 | tf_op jit(solution)/shard_map/ppermute | solution.py:395
  68.4 5.7 %collective-permute-start.15 = (bf16[144,256]{1,0:T(8,128)(2,1)S(1)}, bf16[144,256]{1,0:T(8,128)(2,1)S(1)}, u32[]{:S(2)}, u32[]{:S(2)}) collective-permute-start(bf16[144,256]{1,0:T(8,128)(2,1)S(1)} %get-tuple-element.89), channel_id=1, source_target_pairs={{0,3},{1,0},{2,1},{3,2},{4,7},{5,4},{6,5},{7,6},{8,11},{9,8},{10,9... | collective-permute-start | bytes 221192 | tf_op jit(solution)/shard_map/ppermute | solution.py:395
  71.4 8.8 %collective-permute-start.16 = (bf16[144,256]{1,0:T(8,128)(2,1)S(1)}, bf16[144,256]{1,0:T(8,128)(2,1)S(1)}, u32[]{:S(2)}, u32[]{:S(2)}) collective-permute-start(bf16[144,256]{1,0:T(8,128)(2,1)S(1)} %get-tuple-element.90), channel_id=1, source_target_pairs={{0,2},{1,3},{2,0},{3,1},{4,6},{5,7},{6,4},{7,5},{8,10},{9,11},{10,... | collective-permute-start | bytes 221192 | tf_op jit(solution)/shard_map/ppermute | solution.py:395
  72.3 8.0 %collective-permute-start.17 = (bf16[144,256]{1,0:T(8,128)(2,1)S(1)}, bf16[144,256]{1,0:T(8,128)(2,1)S(1)}, u32[]{:S(2)}, u32[]{:S(2)}) collective-permute-start(bf16[144,256]{1,0:T(8,128)(2,1)S(1)} %get-tuple-element.91), channel_id=1, source_target_pairs={{0,1},{1,2},{2,3},{3,0},{4,5},{5,6},{6,7},{7,4},{8,9},{9,10},{10,1... | collective-permute-start | bytes 221192 | tf_op jit(solution)/shard_map/ppermute | solution.py:395
  81.1 1.3 %collective-permute-start.18 = (f32[2,512]{1,0:T(2,128)S(1)}, f32[2,512]{1,0:T(2,128)S(1)}, u32[]{:S(2)}, u32[]{:S(2)}) collective-permute-start(f32[2,512]{1,0:T(2,128)S(1)} %get-tuple-element.94), channel_id=1, source_target_pairs={{0,4},{4,0},{8,12},{12,8},{16,20},{20,16},{24,28},{28,24},{1,5},{5... | collective-permute-start | bytes 12296 | tf_op jit(solution)/shard_map/ppermute | solution.py:392

commit v2 on v1

v2 whole, which is shorter than its diff:
```python
import functools

import jax
import jax.numpy as jnp
from jax import lax
from jax.experimental import pallas as pl
from jax.experimental.pallas import tpu as pltpu
from jax.sharding import PartitionSpec as P

HEAD_DIM = 128
TILE = 128
SPARE = 16
LOG2E = 1.4426950408889634
ENTRY = 4
PARTS = 4
LAST_DIMS = (((1,), (1,)), ((), ()))
VMEM = pltpu.VMEM
SMEM = pltpu.SMEM
F32 = jnp.float32
BF16 = jnp.bfloat16


def split_three(x):
    high = x.astype(BF16).astype(F32)
    rest = x - high
    middle = rest.astype(BF16).astype(F32)
    low = (rest - middle).astype(BF16).astype(F32)
    return high, middle, low


def head_rows(heads_dev):
    return -(-heads_dev // 8) * 8


def extra_rows(heads_dev):
    return -(-3 * head_rows(heads_dev) // 16) * 16


def prepare_kernel(dims, key_ref, value_ref, attn_ref, grads_ref, lse_ref, *rest):
    count_ka, heads, heads_dev, share = dims
    outs, (attn, grad, lse_pad, delta_pad, sems) = rest[:count_ka], rest[count_ka:]
    _, place_ka = places()
    rows8 = head_rows(heads_dev)
    part_heads = heads // PARTS
    rows = pl.ds(pl.multiple_of(place_ka * TILE, TILE), TILE)
    copies = []
    for part in range(PARTS):
        columns = pl.ds(part * part_heads * HEAD_DIM, part_heads * HEAD_DIM)
        copies.append((
            pltpu.make_async_copy(attn_ref.at[:, columns], attn.at[part], sems.at[0, part]),
            pltpu.make_async_copy(grads_ref.at[rows, columns], grad.at[part], sems.at[1, part]),
        ))
        for copy in copies[-1]:
            copy.start()
    for step in range(count_ka):
        target = lax.rem(place_ka + step, count_ka)
        kv_at = pl.ds(pl.multiple_of(target // share * HEAD_DIM, HEAD_DIM), HEAD_DIM)
        outs[step][:TILE, :HEAD_DIM] = key_ref[:, kv_at]
        outs[step][:TILE, HEAD_DIM:] = value_ref[:, kv_at]
    lanes = lax.broadcasted_iota(jnp.int32, (TILE, TILE), 1)
    columns = jnp.zeros((TILE, TILE), F32)
    for part in range(PARTS):
        for copy in copies[part]:
            copy.wait()
        for head in range(part_heads):
            at = pl.ds(head * HEAD_DIM, HEAD_DIM)
            products = grad[part, :, at].astype(F32) * attn[part, :, at].astype(F32)
            total = jnp.sum(products, axis=1, keepdims=True)
            columns = jnp.where(lanes == part * part_heads + head, total, columns)
    delta_pad[...] = jnp.zeros_like(delta_pad)
    lse_pad[...] = jnp.zeros_like(lse_pad)
    delta_pad[:heads, :] = columns.T[:heads, :]
    lse_pad[:heads, :] = lse_ref[...]
    filler = extra_rows(heads_dev) - 3 * rows8
    for step in range(count_ka):
        target = lax.rem(place_ka + step, count_ka)
        head_at = pl.ds(target * heads_dev, rows8)
        both = jnp.concatenate([lse_pad[head_at, :], delta_pad[head_at, :]], axis=1)
        terms = list(split_three(both))
        if filler:
            terms.append(jnp.zeros((filler, 2 * HEAD_DIM), F32))
        outs[step][TILE:, :] = jnp.concatenate(terms, axis=0).astype(BF16)


def own_heads_kernel(dims, queries_ref, grads_ref, out_ref, sems):
    count_ka, heads_dev = dims
    _, place_ka = places()
    copies = []
    for number, ref in enumerate((queries_ref, grads_ref)):
        for head in range(heads_dev):
            columns = pl.ds(pl.multiple_of((place_ka * heads_dev + head) * HEAD_DIM, HEAD_DIM), HEAD_DIM)
            for tile in range(count_ka):
                copies.append(pltpu.make_async_copy(
                    ref.at[pl.ds(tile * TILE, TILE), columns],
                    out_ref.at[number, tile, pl.ds(head * HEAD_DIM, HEAD_DIM), :],
                    sems.at[number, head, tile],
                ))
                copies[-1].start()
    for copy in copies:
        copy.wait()


def places():
    return lax.axis_index("pb"), lax.axis_index("ka")


def plan_kernel(dims, order_ref, doc_ref, mask_ref, *tables):
    count_chip, count_ka, stages = dims
    place_pb, place_ka = places()
    for table, (other, steps) in zip(tables, stages):
        query_pb = place_pb ^ other

        def query_step(turn_q, units, table=table, query_pb=query_pb, steps=steps):
            step_q = jnp.int32(steps[0])
            for number, step in enumerate(steps):
                step_q = jnp.where(turn_q == number, step, step_q)
            tile_at = lax.rem(place_ka + step_q, count_ka)
            seq_q = order_ref[query_pb * count_ka + tile_at]
            doc_q = doc_ref[seq_q]

            def collect(number, units):
                for step in range(count_ka):
                    stored = (place_pb ^ (2 * number)) * count_ka + lax.rem(
                        place_ka - step + count_ka, count_ka
                    )
                    seq_k = order_ref[stored]
                    live = (mask_ref[seq_q, seq_k] == 1) & (doc_ref[seq_k] == doc_q) & (seq_q >= seq_k)
                    base = ENTRY * (units + 1)
                    table[base] = turn_q
                    table[base + 1] = tile_at
                    table[base + 2] = number * count_ka + step
                    table[base + 3] = jnp.where(seq_q == seq_k, 0, -TILE)
                    units = units + live.astype(jnp.int32)
                return units

            return lax.fori_loop(0, count_chip, collect, units)

        units = lax.fori_loop(0, len(steps), query_step, jnp.int32(0))
        table[0] = (units + 1) // 2
        base = ENTRY * (units + 1)
        table[base] = 0
        table[base + 1] = 0
        table[base + 2] = 0
        table[base + 3] = TILE


def attention_kernel(dims, table_ref, *rest):
    count_chip, count_ka, heads_dev, share, stage, steps = dims
    if stage == 0:
        (key_gain_ref, value_gain_ref), rest = rest[:2], rest[2:]
    (heads_ref, stats_ref), rest = rest[:2], rest[2:]
    if stage in (0, 3):
        blocks, rest = rest[:count_chip], rest[count_chip:]
    if stage == 0:
        (dq_out, keys, values, keys_t, key_sum, value_sum), rest = rest[:6], rest[6:]
    else:
        (keys, values, keys_t, key_start, value_start), rest = rest[:5], rest[5:]
        dq_out, rest = rest[0], rest[1:]
        if stage == 3:
            kv_outs, rest = rest[:count_chip], rest[count_chip:]
        (key_sum, value_sum), rest = rest[:2], rest[2:]
    lse_delta, weights_low, dscores_low, dq_sum = rest
    _, place_ka = places()
    rows8 = head_rows(heads_dev)
    spare = extra_rows(heads_dev)
    score_scale = HEAD_DIM ** -0.5

    if stage == 0:
        kv_at = pl.ds(pl.multiple_of(place_ka // share * HEAD_DIM, HEAD_DIM), HEAD_DIM)
        key_gain = key_gain_ref[:, kv_at]
        value_gain = value_gain_ref[:, kv_at]
        for number in range(count_chip):
            for step in range(count_ka):
                part = pl.ds(step * TILE, TILE)
                local = number * count_ka + step
                key_tile = (blocks[number][part, :HEAD_DIM].astype(F32) * key_gain).astype(BF16)
                value_tile = (blocks[number][part, HEAD_DIM:].astype(F32) * value_gain).astype(BF16)
                keys[local] = key_tile
                values[local] = value_tile
                keys_t[local] = key_tile.T
        key_sum[...] = jnp.zeros_like(key_sum)
        value_sum[...] = jnp.zeros_like(value_sum)
    else:
        key_sum[...] = key_start[...]
        value_sum[...] = value_start[...]

    reach = (lax.broadcasted_iota(jnp.int32, (TILE, TILE), 1)
             - lax.broadcasted_iota(jnp.int32, (TILE, TILE), 0))
    reach = jnp.concatenate([reach, reach], axis=1)

    for number, step in enumerate(steps):
        slot = count_ka - step if step else 0
        packed = stats_ref[pl.ds(slot * spare, spare), :].astype(F32)
        lse_delta[number] = (packed[:rows8] + packed[rows8:2 * rows8]) + packed[2 * rows8:3 * rows8]
    dq_sum[...] = jnp.zeros_like(dq_sum)

    def unit_step(at, carry):
        terms = []
        for lane in range(2):
            base = ENTRY * (2 * at + lane + 1)
            turn_q, tile_at, key_at = table_ref[base], table_ref[base + 1], table_ref[base + 2]
            allowed = reach >= table_ref[base + 3]
            for head in range(0, heads_dev, 2):
                part = pl.ds(head * HEAD_DIM, 2 * HEAD_DIM)
                scores = lax.dot_general(
                    keys[key_at], heads_ref[0, tile_at, part, :], LAST_DIMS, preferred_element_type=F32
                )
                dweights = lax.dot_general(
                    values[key_at], heads_ref[1, tile_at, part, :], LAST_DIMS, preferred_element_type=F32
                )
                lse_row, delta_row = [
                    jnp.concatenate(
                        [lse_delta[turn_q, number:number + 1, lanes] for number in (head, head + 1)], axis=1
                    )
                    for lanes in (slice(0, TILE), slice(TILE, 2 * TILE))
                ]
                weights = jnp.exp2(scores * (score_scale * LOG2E) - lse_row * LOG2E)
                weights = jnp.where(allowed, weights, 0.0)
                weights_low[lane, :, part] = weights.astype(BF16)
                dscores_low[lane, :, part] = (weights * (dweights - delta_row)).astype(BF16)
            terms.append((
                turn_q,
                key_at,
                jnp.dot(weights_low[lane], heads_ref[1, tile_at], preferred_element_type=F32),
                jnp.dot(dscores_low[lane], heads_ref[0, tile_at], preferred_element_type=F32),
                jnp.dot(keys_t[key_at], dscores_low[lane], preferred_element_type=F32),
            ))
        for turn_q, key_at, value_term, key_term, dq_term in terms:
            value_sum[key_at] += value_term
            key_sum[key_at] += key_term
            dq_sum[turn_q] += dq_term
        return carry

    lax.fori_loop(0, table_ref[0], unit_step, 0)
    for number in range(len(steps)):
        dq_out[number] = (dq_sum[number] * score_scale).astype(dq_out.dtype)
    if stage != 3:
        return

    key_gains = jnp.zeros((8, HEAD_DIM), F32)
    value_gains = jnp.zeros((8, HEAD_DIM), F32)
    for number in range(count_chip):
        for step in range(count_ka):
            part = pl.ds(step * TILE, TILE)
            local = number * count_ka + step
            key_total = key_sum[local] * score_scale
            value_total = value_sum[local]
            kv_outs[number][part, :HEAD_DIM] = key_total.astype(kv_outs[number].dtype)
            kv_outs[number][part, HEAD_DIM:] = value_total.astype(kv_outs[number].dtype)
            key_raw = blocks[number][part, :HEAD_DIM].astype(F32)
            value_raw = blocks[number][part, HEAD_DIM:].astype(F32)
            key_gains += jnp.sum((key_total * key_raw).reshape(TILE // 8, 8, HEAD_DIM), axis=0)
            value_gains += jnp.sum((value_total * value_raw).reshape(TILE // 8, 8, HEAD_DIM), axis=0)
    gains = jnp.concatenate([jnp.sum(key_gains, axis=0, keepdims=True),
                             jnp.sum(value_gains, axis=0, keepdims=True)], axis=1)
    packed = pack_gains(gains)
    for number in range(count_chip):
        kv_outs[number][count_ka * TILE:, :] = packed.astype(kv_outs[number].dtype)


def pack_gains(gains):
    rows = lax.broadcasted_iota(jnp.int32, (SPARE, gains.shape[1]), 0)
    high, middle, low = split_three(gains)
    packed = jnp.where(rows == 0, high, jnp.where(rows == 1, middle, low))
    return jnp.where(rows < 3, packed, 0.0)


def add_kernel(part_ref, other_ref, *outs):
    width = part_ref.shape[2]
    tile, column = 0, 0
    for out_ref in outs:
        part = pl.ds(column, out_ref.shape[1])
        out_ref[...] = (part_ref[tile, :, part] + other_ref[tile, :, part].astype(F32)).astype(BF16)
        column += out_ref.shape[1]
        if column == width:
            tile, column = tile + 1, 0


def collect_kernel(dims, key_gain_ref, value_gain_ref, *rest):
    count_chip, count_ka, share = dims
    parts, outs = rest[:count_chip], rest[count_chip:]
    kv_at = pl.ds(pl.multiple_of(places()[1] // share * HEAD_DIM, HEAD_DIM), HEAD_DIM)
    gain = jnp.concatenate([key_gain_ref[:, kv_at], value_gain_ref[:, kv_at]], axis=1)
    for step in range(count_ka):
        rows = pl.ds(step * TILE, TILE)
        total = parts[0][rows, :]
        for number in range(1, count_chip):
            total = total + parts[number][rows, :].astype(F32)
        if share == 1:
            total = total * gain
        outs[step][:TILE, :] = total.astype(outs[step].dtype)
    spare = pl.ds(count_ka * TILE, SPARE)
    total = parts[0][spare, :]
    for number in range(1, count_chip):
        total = total + parts[number][spare, :].astype(F32)
    packed = pack_gains(jnp.sum(total, axis=0, keepdims=True))
    for step in range(count_ka):
        outs[step][TILE:, :] = packed.astype(outs[step].dtype)


def turn_kernel(*refs):
    half = len(refs) // 2
    for source, target in zip(refs[:half], refs[half:]):
        for head in range(source.shape[1] // HEAD_DIM):
            part = pl.ds(head * HEAD_DIM, HEAD_DIM)
            target[:, part] = source[:, part].T


def place_kernel(dims, *rest):
    count_ka, heads_dev, pieces = dims
    dq_parts, rest = rest[:len(pieces)], rest[len(pieces):]
    dq_out, rest = rest[0], rest[1:]
    turned, sems = rest[:-1], rest[-1]
    copies, used = [], 0
    for number, ((step, offset, late), piece) in enumerate(zip(pieces, dq_parts)):
        source = lax.rem(places()[1] - step + count_ka, count_ka)
        column = (source * heads_dev + offset) * HEAD_DIM
        columns = pl.ds(pl.multiple_of(column, HEAD_DIM), piece.shape[1])
        if late:
            turn_kernel(piece, turned[used])
            piece, used = turned[used], used + 1
        copies.append(pltpu.make_async_copy(piece, dq_out.at[:, columns], sems.at[number]))
        copies[-1].start()
    for copy in copies:
        copy.wait()


def finish_kernel(dims, key_gain_ref, value_gain_ref, *rest):
    count_ka, share = dims
    pieces, rest = rest[:count_ka], rest[count_ka:]
    dk_out, dv_out, gains_out, sums = rest
    _, place_ka = places()
    sums[...] = jnp.zeros_like(sums)
    for step in range(count_ka):
        source = lax.rem(place_ka + step, count_ka)
        sums[source // share] += pieces[step][...].astype(F32)
    for head in range(count_ka // share):
        part = pl.ds(head * HEAD_DIM, HEAD_DIM)
        key_total = sums[head, :TILE, :HEAD_DIM]
        value_total = sums[head, :TILE, HEAD_DIM:]
        if share > 1:
            key_total = key_total * key_gain_ref[:, part]
            value_total = value_total * value_gain_ref[:, part]
        dk_out[:, part] = key_total.astype(BF16)
        dv_out[:, part] = value_total.astype(BF16)
        gains = jnp.sum(sums[head, TILE:, :], axis=0, keepdims=True)
        gains_out[0:1, part] = gains[:, :HEAD_DIM]
        gains_out[1:2, part] = gains[:, HEAD_DIM:]


def in_vmem(count):
    return [pl.BlockSpec(memory_space=VMEM)] * count


def in_smem(count):
    return [pl.BlockSpec(memory_space=SMEM)] * count


def anywhere(count):
    return [pl.BlockSpec(memory_space=pl.ANY)] * count


def params(mib):
    return pltpu.CompilerParams(vmem_limit_bytes=mib * 1024 * 1024)


def shards(
    queries,
    key_rows,
    values,
    attn_out,
    grad_out,
    log_sums,
    key_gain,
    value_gain,
    doc_ids,
    tile_mask,
    block_order,
):
    count_pb = lax.axis_size("pb")
    count_ka = lax.axis_size("ka")
    rows_dev = key_rows.shape[0]
    query_rows = queries.shape[0]
    heads = log_sums.shape[0]
    feat_width = queries.shape[1]
    kv_heads = key_rows.shape[1] // HEAD_DIM
    heads_dev = heads // count_ka
    share = count_ka // kv_heads
    assert rows_dev == TILE and share * kv_heads == count_ka and count_pb & (count_pb - 1) == 0
    width = heads_dev * HEAD_DIM
    key_gain = key_gain.reshape(1, -1)
    value_gain = value_gain.reshape(1, -1)

    spare = extra_rows(heads_dev)
    count_chip = count_pb // 2

    def swap(array, number):
        return lax.ppermute(array, "pb", [(at, at ^ number) for at in range(count_pb)])

    def turn(array, step):
        return lax.ppermute(array, "ka", [(at, (at + step) % count_ka) for at in range(count_ka)])

    sends = pl.pallas_call(
        functools.partial(prepare_kernel, (count_ka, heads, heads_dev, share)),
        in_specs=in_vmem(2) + anywhere(2) + in_vmem(1),
        out_specs=in_vmem(count_ka),
        out_shape=[jax.ShapeDtypeStruct((TILE + spare, 2 * HEAD_DIM), BF16)] * count_ka,
        scratch_shapes=[VMEM((PARTS, TILE, feat_width // PARTS), BF16)] * 2
        + [VMEM((heads + 8, TILE), F32)] * 2
        + [pltpu.SemaphoreType.DMA((2, PARTS))],
        compiler_params=params(57),
        name="prepare",
    )(key_rows, values, attn_out, grad_out, log_sums)
    messages = [sends[0]] + [turn(sends[step], step) for step in range(1, count_ka)]

    later_queries, _ = lax.optimization_barrier((queries, sends[0]))
    own_queries = pl.pallas_call(
        functools.partial(own_heads_kernel, (count_ka, heads_dev)),
        in_specs=anywhere(2),
        out_specs=in_vmem(1)[0],
        out_shape=jax.ShapeDtypeStruct((2, count_ka, width, HEAD_DIM), BF16),
        scratch_shapes=[pltpu.SemaphoreType.DMA((2, heads_dev, count_ka))],
        compiler_params=params(57),
        cost_estimate=pl.CostEstimate(flops=0, bytes_accessed=8 * query_rows * width, transcendentals=0),
        name="own_heads",
    )(later_queries, grad_out)
    messages, own_queries = lax.optimization_barrier((messages, own_queries))
    own_block = jnp.concatenate([message[:TILE] for message in messages], axis=0)
    own_stats = jnp.concatenate([message[TILE:] for message in messages], axis=0)
    blocks = [own_block] + [swap(own_block, 2 * number) for number in range(1, count_chip)]
    other_stats = swap(own_stats, 1)
    later_order, _ = lax.optimization_barrier((block_order, own_block))
    other_queries = swap(own_queries, 1)

    key_tiles = count_chip * count_ka
    sum_shape = jax.ShapeDtypeStruct((key_tiles, TILE, HEAD_DIM), F32)
    key_shape = jax.ShapeDtypeStruct((key_tiles, TILE, HEAD_DIM), BF16)
    kv_shape = (query_rows + SPARE, 2 * HEAD_DIM)
    half = count_ka // 2
    rest_steps = tuple(step for step in range(1, count_ka) if step != half) + (0,)
    stages = ((1, (half,)), (0, (half,)), (1, rest_steps), (0, rest_steps))
    tables = pl.pallas_call(
        functools.partial(plan_kernel, (count_chip, count_ka, stages)),
        in_specs=in_smem(3),
        out_specs=in_smem(len(stages)),
        out_shape=[
            jax.ShapeDtypeStruct((ENTRY * (2 + len(steps) * key_tiles),), jnp.int32)
            for _, steps in stages
        ],
        cost_estimate=pl.CostEstimate(flops=0, bytes_accessed=1 << 22, transcendentals=0),
        name="plan",
    )(later_order, doc_ids, tile_mask)

    def attend(stage, outs, scratch, *operands):
        steps = stages[stage][1]
        dims = (count_chip, count_ka, heads_dev, share, stage, steps)
        pairs = len(steps) * key_tiles
        return pl.pallas_call(
            functools.partial(attention_kernel, dims),
            in_specs=in_smem(1) + in_vmem(len(operands)),
            out_specs=in_vmem(len(outs)),
            out_shape=outs,
            scratch_shapes=scratch + [
                VMEM((len(steps), head_rows(heads_dev), 2 * TILE), F32),
                VMEM((2, TILE, width), BF16),
                VMEM((2, TILE, width), BF16),
                VMEM((len(steps), HEAD_DIM, width), F32),
            ],
            compiler_params=params(14 + key_tiles // 2),
            cost_estimate=pl.CostEstimate(
                flops=10 * pairs * TILE * TILE * width if stage < 3 else 0,
                bytes_accessed=1 << 20 if stage < 3 else 0,
                transcendentals=0,
            ),
            name=("attention_other_first", "attention_own_first", "attention_other", "attention_own")[stage],
        )(tables[stage], *operands)

    def part_shape(stage, dtype):
        return jax.ShapeDtypeStruct((len(stages[stage][1]), HEAD_DIM, width), dtype)

    def add(part, other, cuts):
        return pl.pallas_call(
            add_kernel,
            in_specs=in_vmem(2),
            out_specs=in_vmem(part.shape[0] * cuts),
            out_shape=[jax.ShapeDtypeStruct((HEAD_DIM, width // cuts), BF16)] * (part.shape[0] * cuts),
            compiler_params=params(4 * part.shape[0]),
            name="add_queries",
        )(part, other)

    dq_other, *state = attend(
        0, [part_shape(0, BF16)] + [key_shape] * 3 + [sum_shape] * 2,
        [], key_gain, value_gain, other_queries, other_stats, *blocks,
    )
    keys, sums = state[:3], state[3:]
    dq_back = swap(dq_other, 1)
    dq_own, *sums = attend(
        1, [part_shape(1, F32)] + [sum_shape] * 2, [], own_queries, own_stats, *keys, *sums
    )
    dq_parts = [None] * count_ka
    dq_first = add(dq_own, dq_back, 2)
    dq_halves = [turn(part, half) for part in dq_first]
    rest_stats, _ = lax.optimization_barrier((other_stats, dq_first[0]))
    dq_other, *sums = attend(
        2, [part_shape(2, BF16)] + [sum_shape] * 2, [], other_queries, rest_stats, *keys, *sums
    )
    dq_other, dq_halves[0] = lax.optimization_barrier((dq_other, dq_halves[0]))
    dq_back = swap(dq_other, 1)
    dq_own, *kv_own = attend(
        3,
        [part_shape(3, F32), jax.ShapeDtypeStruct(kv_shape, F32)]
        + [jax.ShapeDtypeStruct(kv_shape, BF16)] * (count_chip - 1),
        [VMEM(sum_shape.shape, F32)] * 2,
        own_queries, own_stats, *blocks, *keys, *sums,
    )
    for step, tile in zip(rest_steps, add(dq_own, dq_back, 1)):
        dq_parts[step] = turn(tile, step) if step else tile
    kv_own[2], dq_halves[1] = lax.optimization_barrier((kv_own[2], dq_halves[1]))
    kv_parts = [kv_own[0]] + [swap(kv_own[number], 2 * number) for number in range(1, count_chip)]
    piece_type = BF16 if share == 1 else F32
    piece_shape = (TILE + SPARE, 2 * HEAD_DIM)
    totals = pl.pallas_call(
        functools.partial(collect_kernel, (count_chip, count_ka, share)),
        in_specs=in_vmem(2 + count_chip),
        out_specs=in_vmem(count_ka),
        out_shape=[jax.ShapeDtypeStruct(piece_shape, piece_type)] * count_ka,
        compiler_params=params(24),
        name="collect",
    )(key_gain, value_gain, *kv_parts)
    first_turns = [dq_parts[step] for step in rest_steps if step]
    totals, first_turns = lax.optimization_barrier((totals, first_turns))
    for step, tile in zip([step for step in rest_steps if step], first_turns):
        dq_parts[step] = tile
    pieces = [totals[0]] + [turn(totals[step], -step) for step in range(1, count_ka)]

    grad_keys, grad_values, gains = pl.pallas_call(
        functools.partial(finish_kernel, (count_ka, share)),
        in_specs=in_vmem(2 + count_ka),
        out_specs=in_vmem(3),
        out_shape=[
            jax.ShapeDtypeStruct(key_rows.shape, BF16),
            jax.ShapeDtypeStruct(key_rows.shape, BF16),
            jax.ShapeDtypeStruct((2, key_rows.shape[1]), F32),
        ],
        scratch_shapes=[VMEM((kv_heads, TILE + SPARE, 2 * HEAD_DIM), F32)],
        compiler_params=params(16),
        name="finish",
    )(key_gain, value_gain, *pieces)
    gains = gains + swap(gains, 1)
    first = [dq_parts[0], *dq_halves]
    turned = pl.pallas_call(
        turn_kernel,
        in_specs=in_vmem(len(first)),
        out_specs=in_vmem(len(first)),
        out_shape=[jax.ShapeDtypeStruct(part.shape, BF16) for part in first],
        compiler_params=params(8),
        cost_estimate=pl.CostEstimate(flops=0, bytes_accessed=1 << 22, transcendentals=0),
        name="turn_queries",
    )(*first)
    late = [step for step in rest_steps if step]
    where = ((0, 0, False), (half, 0, False), (half, heads_dev // 2, False))
    where += tuple((step, 0, True) for step in late)
    grad_queries = pl.pallas_call(
        functools.partial(place_kernel, (count_ka, heads_dev, where)),
        in_specs=in_vmem(len(where)),
        out_specs=pl.BlockSpec(memory_space=pl.ANY),
        out_shape=jax.ShapeDtypeStruct((rows_dev, feat_width), BF16),
        scratch_shapes=[VMEM((TILE, width), BF16)] * len(late) + [pltpu.SemaphoreType.DMA((len(where),))],
        compiler_params=params(16),
        cost_estimate=pl.CostEstimate(flops=0, bytes_accessed=4 * rows_dev * feat_width, transcendentals=0),
        name="place_queries",
    )(*turned, *[dq_parts[step] for step in late])
    return grad_queries, grad_keys, grad_values, gains[0], gains[1]


def solution(mesh):
    placed = (
        P("pb", None),
        P(("pb", "ka"), None),
        P(("pb", "ka"), None),
        P(("pb", "ka"), None),
        P("pb", None),
        P(None, ("pb", "ka")),
        P(),
        P(),
        P(),
        P(),
        P(),
    )
    return jax.shard_map(
        shards,
        mesh=mesh,
        in_specs=placed,
        out_specs=(P(("pb", "ka"), None), P(("pb", "ka"), None), P(("pb", "ka"), None), P(), P()),
        check_vma=False,
    )
```

time: 83.9 us -> 88.7 us (1.057)
  starting transfers between devices: 24.7 us -> 28.9 us
  Pallas kernels: 27.6 us -> 29.8 us
  waiting for transfers between devices: 27.8 us -> 26.5 us
    ppermute x9 -> x10, waiting for transfers between devices: 14.4 us -> 9.98 us  [turn(): lax.ppermute(array, 'ka', [(at, (at + step) % count_ka) for at in range(c...]
    ppermute x9 -> x10, starting transfers between devices: 16 us -> 19.8 us  [turn(): lax.ppermute(array, 'ka', [(at, (at + step) % count_ka) for at in range(c...]
    pallas_call x3 -> x4, Pallas kernels: 13.8 us -> 17.3 us  [attend(): pl.pallas_call(functools.partial(attention_kernel, dims), in_specs=in_sme...]
    ppermute x10 -> x11, waiting for transfers between devices: 13.4 us -> 16.5 us  [swap(): lax.ppermute(array, 'pb', [(at, at ^ number) for at in range(count_pb)])]
    pallas_call x3 -> x4, Pallas kernels: 5.8 us -> 4.7 us  [the longest x1 3.49 us: shards(): pl.pallas_call(functools.partial(own_heads_kernel, (count_ka, heads_dev))...]
    ppermute x10 -> x11, starting transfers between devices: 8.73 us -> 9.15 us  [swap(): lax.ppermute(array, 'pb', [(at, at ^ number) for at in range(count_pb)])]
  transfers between devices with their start and end apart: 19 -> 21, of which waited for: 7 -> 11; matrix products, arithmetic and copies ran while one was open for 0% -> 0% of each run, Pallas kernels for 24% -> 28%
where the time goes in v2:
time: 88.7 us; the launch traced here: 87.4 us
  Pallas kernels  29.8 us (34%)
  starting transfers between devices  28.9 us (33%)
  waiting for transfers between devices  26.5 us (30%)
  local copies, waits for them, and re-layouts  1.3 us (1%)
    ppermute x10, starting transfers between devices, turn(): lax.ppermute(array, 'ka', [(at, (at + step) % count_ka) for at in range(c...  19.8 us
    pallas_call x4, Pallas kernels, attend(): pl.pallas_call(functools.partial(attention_kernel, dims), in_specs=in_sme...  17.3 us
    ppermute x11, waiting for transfers between devices, swap(): lax.ppermute(array, 'pb', [(at, at ^ number) for at in range(count_pb)])  16.5 us
    ppermute x10, waiting for transfers between devices, turn(): lax.ppermute(array, 'ka', [(at, (at + step) % count_ka) for at in range(c...  9.98 us
    ppermute x11, starting transfers between devices, swap(): lax.ppermute(array, 'pb', [(at, at ^ number) for at in range(count_pb)])  9.15 us
    pallas_call x1, Pallas kernels, shards(): pl.pallas_call(functools.partial(prepare_kernel, (count_ka, heads, heads_...  3.69 us
    pallas_call x1, Pallas kernels, shards(): pl.pallas_call(functools.partial(own_heads_kernel, (count_ka, heads_dev))...  3.49 us
    pallas_call x1, Pallas kernels, shards(): pl.pallas_call(functools.partial(plan_kernel, (count_chip, count_ka, stag...  2.91 us
  transfers between devices with their start and end apart: 21, of which 11 were waited for; matrix products, arithmetic and copies ran while one was open for 0% of the time, Pallas kernels for 28%

profile of v2, /device:TPU:0, one launch (start us, length us, event | category | flops | bytes accessed | tf_op | source)
XLA Modules:
  0.0 87.4 jit_solution(686763625291605530)
XLA Ops:
  0.6 3.7 %prepare.1 = (bf16[160,256]{1,0:T(8,128)(2,1)}, bf16[160,256]{1,0:T(8,128)(2,1)}, bf16[160,256]{1,0:T(8,128)(2,1)}, bf16[160,256]{1,0:T(8,128)(2,1)}) custom-call(bf16[128,512]{1,0:T(8,128)(2,1)} %key_ref.1, bf16[128,512]{1,0:T(8,128)(2,1)} %value_ref.1, bf16[128,4096]{1,0:T(8,128)(2,1)} %attn_ref.1, bf16[512,4096]{1,0:T(8,128)(2,1)} %grads_ref.3, ...), custom_call_target="tpu_custom_call" | custom-call | tf_op jit(solution)/shard_map/prepare/pallas_call | solution.py:403
  4.3 3.1 %collective-permute-start = (bf16[160,256]{1,0:T(8,128)(2,1)}, bf16[160,256]{1,0:T(8,128)(2,1)S(1)}, u32[]{:S(2)}, u32[]{:S(2)}) collective-permute-start(bf16[160,256]{1,0:T(8,128)(2,1)} %get-tuple-element.64), channel_id=1, source_target_pairs={{0,1},{1,2},{2,3},{3,0},{4,5},{5,6},{6,7},{7,4},{8,9},{9,10},{10,1... | collective-permute-start | bytes 245768 | tf_op jit(solution)/shard_map/ppermute | solution.py:401
  7.4 2.6 %collective-permute-start.1 = (bf16[160,256]{1,0:T(8,128)(2,1)}, bf16[160,256]{1,0:T(8,128)(2,1)S(1)}, u32[]{:S(2)}, u32[]{:S(2)}) collective-permute-start(bf16[160,256]{1,0:T(8,128)(2,1)} %get-tuple-element.65), channel_id=1, source_target_pairs={{0,2},{1,3},{2,0},{3,1},{4,6},{5,7},{6,4},{7,5},{8,10},{9,11},{10,... | collective-permute-start | bytes 245768 | tf_op jit(solution)/shard_map/ppermute | solution.py:401
  10.0 1.3 %collective-permute-start.2 = (bf16[160,256]{1,0:T(8,128)(2,1)}, bf16[160,256]{1,0:T(8,128)(2,1)S(1)}, u32[]{:S(2)}, u32[]{:S(2)}) collective-permute-start(bf16[160,256]{1,0:T(8,128)(2,1)} %get-tuple-element.66), channel_id=1, source_target_pairs={{0,3},{1,0},{2,1},{3,2},{4,7},{5,4},{6,5},{7,6},{8,11},{9,8},{10,9... | collective-permute-start | bytes 245768 | tf_op jit(solution)/shard_map/ppermute | solution.py:401
  11.4 3.5 %own_heads.1.rest_0_ = bf16[2,4,1024,128]{3,2,1,0:T(8,128)(2,1)} custom-call(bf16[512,4096]{1,0:T(8,128)(2,1)} %queries_ref, bf16[512,4096]{1,0:T(8,128)(2,1)} %grads_ref.3), custom_call_target="tpu_custom_call" | custom-call | bytes 4194304 | tf_op jit(solution)/shard_map/own_heads/pallas_call | solution.py:417
  14.9 0.0 collective-permute-done
  14.9 0.8 collective-permute-done.1
  15.7 0.2 collective-permute-done.2
  15.9 0.0 collective-permute-start.6
  15.9 0.0 copy-done.7
  16.0 2.5 %collective-permute-start.5 = (bf16[512,256]{1,0:T(8,128)(2,1)S(1)}, bf16[512,256]{1,0:T(8,128)(2,1)S(1)}, u32[]{:S(2)}, u32[]{:S(2)}) collective-permute-start(bf16[512,256]{1,0:T(8,128)(2,1)S(1)} %pad_maximum_fusion.rest_4_.rest_2_), channel_id=1, source_target_pairs={{0,24},{4,28},{8,16},{12,20},{16,8},{20,12},{24,0},{28,4},{1,25},{... | collective-permute-start | bytes 786440 | tf_op jit(solution)/shard_map/ppermute | solution.py:398
  18.5 0.5 collective-permute-start.4
  19.0 0.5 collective-permute-start.3
  19.6 0.1 collective-permute-start.7
  19.7 2.9 %plan.1 = (s32[72]{0:T(128)}, s32[72]{0:T(128)}, s32[200]{0:T(256)}, s32[200]{0:T(256)}) custom-call(s32[32]{0:T(128)} %order_ref, s32[32]{0:T(128)} %doc_ref.1, s32[32,32]{1,0:T(8,128)} %mask_ref.1), custom_call_target="tpu_custom_call" | custom-call | bytes 4194304 | tf_op jit(solution)/shard_map/plan/pallas_call | solution.py:442
  22.6 0.0 collective-permute-done.7.rest_3_.rest_1_
  22.6 3.5 %collective-permute-done.5.rest_7_.rest_5_ = bf16[512,256]{1,0:T(8,128)(2,1)S(1)} collective-permute-done((bf16[512,256]{1,0:T(8,128)(2,1)S(1)}, bf16[512,256]{1,0:T(8,128)(2,1)S(1)}, u32[]{:S(2)}, u32[]{:S(2)}) %collective-permute-start.5) | collective-permute-done | bytes 262176 | tf_op jit(solution)/shard_map/ppermute | solution.py:398
  26.1 5.2 %collective-permute-done.4.rest_6_.rest_4_ = bf16[512,256]{1,0:T(8,128)(2,1)S(1)} collective-permute-done((bf16[512,256]{1,0:T(8,128)(2,1)S(1)}, bf16[512,256]{1,0:T(8,128)(2,1)S(1)}, u32[]{:S(2)}, u32[]{:S(2)}) %collective-permute-start.4) | collective-permute-done | bytes 262176 | tf_op jit(solution)/shard_map/ppermute | solution.py:398
  31.3 0.1 collective-permute-done.3.rest_5_.rest_3_
  31.4 0.0 collective-permute-done.6.rest_2_.rest_0_
  31.4 0.0 copy-done.1
  31.4 0.0 copy-done.2
  31.4 0.0 copy-start.6
  31.4 0.6 copy-done.6
  32.1 1.0 %attention_other_first.1 = (bf16[1,128,1024]{2,1,0:T(8,128)(2,1)S(1)}, bf16[16,128,128]{2,1,0:T(8,128)(2,1)S(1)}, bf16[16,128,128]{2,1,0:T(8,128)(2,1)S(1)}, bf1...) custom-call(s32[72]{0:T(128)S(1)} %copy-done.6, f32[1,512]{1,0:T(1,128)S(1)} %bitcast.4, ...), custom_call_target="tpu_custom_call" | custom-call | flops 2684354560 | bytes 1048576 | tf_op jit(solution)/shard_map/attention_other_first/pallas_call | solution.py:458
  33.1 1.9 %collective-permute-start.8 = (bf16[1,128,1024]{2,1,0:T(8,128)(2,1)S(1)}, bf16[1,128,1024]{2,1,0:T(8,128)(2,1)S(1)}, u32[]{:S(2)}, u32[]{:S(2)}) collective-permute-start(bf16[1,128,1024]{2,1,0:T(8,128)(2,1)S(1)} %get-tuple-element.84), channel_id=1, source_target_pairs={{0,4},{4,0},{8,12},{12,8},{16,20},{20,16},{24,28},{28,24},{1,5},{5... | collective-permute-start | bytes 786440 | tf_op jit(solution)/shard_map/ppermute | solution.py:398
  35.0 0.0 copy-done
  35.0 0.0 copy-done.5
  35.0 2.7 %attention_own_first.1 = (f32[1,128,1024]{2,1,0:T(8,128)S(1)}, f32[16,128,128]{2,1,0:T(8,128)S(1)}, f32[16,128,128]{2,1,0:T(8,128)S(1)}) custom-call(s32[72]{0:T(128)S(1)} %copy-done.5, bf16[2,4,1024,128]{3,2,1,0:T(8,128)(2,1)S(1)} %copy-done, bf16[128,256]{1,0:T(8,128)(2,1)S(1)} %pad_maximum_fusion.1.rest_1_, ...), custom_call_target="tpu_custom_call" | custom-call | flops 2684354560 | bytes 1048576 | tf_op jit(solution)/shard_map/attention_own_first/pallas_call | solution.py:458
  37.7 0.0 collective-permute-done.8.other_ref
  37.8 0.6 collective-permute-start.9
  38.4 0.0 copy-done.4
  38.4 5.6 %attention_other.1 = (bf16[3,128,1024]{2,1,0:T(8,128)(2,1)S(1)}, f32[16,128,128]{2,1,0:T(8,128)S(1)}, f32[16,128,128]{2,1,0:T(8,128)S(1)}) custom-call(s32[200]{0:T(256)S(1)} %copy-done.4, bf16[2,4,1024,128]{3,2,1,0:T(8,128)(2,1)S(1)} %collective-permute-done.6.rest_2_.rest_0_, bf16[128,256]{1,0:T(8,128)(2,1)S(1)} %collective-permute-done.7.rest_3_.rest_1_, ...), custom_call_target="tpu_custom_call" | custom-call | flops 8053063680 | bytes 1048576 | tf_op jit(solution)/shard_map/attention_other/pallas_call | solution.py:458
  44.1 0.0 collective-permute-done.9.refs_1_
  44.1 0.1 collective-permute-start.10
  44.1 3.0 %collective-permute-start.11 = (bf16[128,512]{1,0:T(8,128)(2,1)S(1)}, bf16[128,512]{1,0:T(8,128)(2,1)S(1)}, u32[]{:S(2)}, u32[]{:S(2)}) collective-permute-start(bf16[128,512]{1,0:T(8,128)(2,1)S(1)} %get-tuple-element.97), channel_id=1, source_target_pairs={{0,2},{1,3},{2,0},{3,1},{4,6},{5,7},{6,4},{7,5},{8,10},{9,11},{10,... | collective-permute-start | bytes 393224 | tf_op jit(solution)/shard_map/ppermute | solution.py:401
  47.2 0.0 copy-done.3
  47.2 7.9 %attention_own.1 = (f32[3,128,1024]{2,1,0:T(8,128)S(1)}, f32[528,256]{1,0:T(8,128)S(1)}, bf16[528,256]{1,0:T(8,128)(2,1)S(1)}, bf16[528,256]{1,0:T(8,128)(2,1)S(1)}, bf16[528,256]{1,0:T(8,128)(2,1)S(1)}) custom-call(s32[200]{0:T(256)S(1)} %copy-done.3, bf16[2,4,1024,128]{3,2,1,0:T(8,128)(2,1)S(1)} %copy-done, ...), custom_call_target="tpu_custom_call" | custom-call | tf_op jit(solution)/shard_map/attention_own/pallas_call | solution.py:458
  55.1 0.1 collective-permute-start.12
  55.2 0.1 collective-permute-start.14
  55.3 0.0 collective-permute-done.11.refs_2_
  55.3 3.4 %collective-permute-start.13 = (bf16[528,256]{1,0:T(8,128)(2,1)S(1)}, bf16[528,256]{1,0:T(8,128)(2,1)S(1)}, u32[]{:S(2)}, u32[]{:S(2)}) collective-permute-start(bf16[528,256]{1,0:T(8,128)(2,1)S(1)} %get-tuple-element.104), channel_id=1, source_target_pairs={{0,16},{4,20},{8,24},{12,28},{16,0},{20,4},{24,8},{28,12},{1,17},{... | collective-permute-start | bytes 811016 | tf_op jit(solution)/shard_map/ppermute | solution.py:398
  58.7 0.0 collective-permute-done.10.other_ref
  58.7 0.1 add_queries.3
  58.8 3.6 %collective-permute-start.15 = (bf16[128,1024]{1,0:T(8,128)(2,1)S(1)}, bf16[128,1024]{1,0:T(8,128)(2,1)S(1)}, u32[]{:S(2)}, u32[]{:S(2)}) collective-permute-start(bf16[128,1024]{1,0:T(8,128)(2,1)S(1)} %get-tuple-element.110), channel_id=1, source_target_pairs={{0,1},{1,2},{2,3},{3,0},{4,5},{5,6},{6,7},{7,4},{8,9},{9,10},{10,1... | collective-permute-start | bytes 786440 | tf_op jit(solution)/shard_map/ppermute | solution.py:401
  62.4 1.3 %collective-permute-start.16 = (bf16[128,1024]{1,0:T(8,128)(2,1)S(1)}, bf16[128,1024]{1,0:T(8,128)(2,1)S(1)}, u32[]{:S(2)}, u32[]{:S(2)}) collective-permute-start(bf16[128,1024]{1,0:T(8,128)(2,1)S(1)} %get-tuple-element.111), channel_id=1, source_target_pairs={{0,3},{1,0},{2,1},{3,2},{4,7},{5,4},{6,5},{7,6},{8,11},{9,8},{10,9... | collective-permute-start | bytes 786440 | tf_op jit(solution)/shard_map/ppermute | solution.py:401
  63.7 0.1 collective-permute-done.12.rest_1_
  63.8 3.1 %collective-permute-done.14.rest_3_ = bf16[528,256]{1,0:T(8,128)(2,1)S(1)} collective-permute-done((bf16[528,256]{1,0:T(8,128)(2,1)S(1)}, bf16[528,256]{1,0:T(8,128)(2,1)S(1)}, u32[]{:S(2)}, u32[]{:S(2)}) %collective-permute-start.14) | collective-permute-done | bytes 270368 | tf_op jit(solution)/shard_map/ppermute | solution.py:398
  66.9 4.5 %collective-permute-done.13.rest_2_ = bf16[528,256]{1,0:T(8,128)(2,1)S(1)} collective-permute-done((bf16[528,256]{1,0:T(8,128)(2,1)S(1)}, bf16[528,256]{1,0:T(8,128)(2,1)S(1)}, u32[]{:S(2)}, u32[]{:S(2)}) %collective-permute-start.13) | collective-permute-done | bytes 270368 | tf_op jit(solution)/shard_map/ppermute | solution.py:398
  71.4 0.2 collect.1
  71.6 0.0 collective-permute-done.15.rest_3_
  71.6 2.5 %collective-permute-done.16.rest_4_ = bf16[128,1024]{1,0:T(8,128)(2,1)S(1)} collective-permute-done((bf16[128,1024]{1,0:T(8,128)(2,1)S(1)}, bf16[128,1024]{1,0:T(8,128)(2,1)S(1)}, u32[]{:S(2)}, u32[]{:S(2)}) %collective-permute-start.16) | collective-permute-done | bytes 262176 | tf_op jit(solution)/shard_map/ppermute | solution.py:401
  74.1 3.3 %collective-permute-start.17 = (bf16[144,256]{1,0:T(8,128)(2,1)S(1)}, bf16[144,256]{1,0:T(8,128)(2,1)S(1)}, u32[]{:S(2)}, u32[]{:S(2)}) collective-permute-start(bf16[144,256]{1,0:T(8,128)(2,1)S(1)} %get-tuple-element.115), channel_id=1, source_target_pairs={{0,3},{1,0},{2,1},{3,2},{4,7},{5,4},{6,5},{7,6},{8,11},{9,8},{10,9... | collective-permute-start | bytes 221192 | tf_op jit(solution)/shard_map/ppermute | solution.py:401
  77.4 0.3 collective-permute-start.18
  77.7 0.6 collective-permute-start.19
  78.3 1.6 %collective-permute-done.17.rest_1_ = bf16[144,256]{1,0:T(8,128)(2,1)S(1)} collective-permute-done((bf16[144,256]{1,0:T(8,128)(2,1)S(1)}, bf16[144,256]{1,0:T(8,128)(2,1)S(1)}, u32[]{:S(2)}, u32[]{:S(2)}) %collective-permute-start.17) | collective-permute-done | bytes 73760 | tf_op jit(solution)/shard_map/ppermute | solution.py:401
  79.9 4.8 %collective-permute-done.18.rest_2_ = bf16[144,256]{1,0:T(8,128)(2,1)S(1)} collective-permute-done((bf16[144,256]{1,0:T(8,128)(2,1)S(1)}, bf16[144,256]{1,0:T(8,128)(2,1)S(1)}, u32[]{:S(2)}, u32[]{:S(2)}) %collective-permute-start.18) | collective-permute-done | bytes 73760 | tf_op jit(solution)/shard_map/ppermute | solution.py:401
  84.7 0.0 collective-permute-done.19.rest_3_
  84.7 0.8 finish.1
  85.5 0.0 collective-permute-start.20
  85.5 0.2 turn_queries.1
  85.7 1.0 %place_queries.1 = bf16[128,4096]{1,0:T(8,128)(2,1)} custom-call(bf16[128,1024]{1,0:T(8,128)(2,1)S(1)} %get-tuple-element.99.rest_0_, bf16[128,512]{1,0:T(8,128)(2,1)S(1)} %get-tuple-element.100.rest_1_, bf16[128,512]{1,0:T(8,128)(2,1)S(1)} %get-tuple-element.101.rest_2_, bf16[128,1024]{1,0:T(8,128)(2,1)S(1)} %collective-permute-done.15.rest_3_, ...), custom_call_target="tpu_custom_call" | custom-call | bytes 2097152 | tf_op jit(solution)/shard_map/place_queries/pallas_call | solution.py:563
  86.8 0.0 collective-permute-done.20
  86.8 0.6 fusion
  (19 shorter events, 0.1 us)
Async XLA Ops:
  4.3 10.5 %collective-permute-start = (bf16[160,256]{1,0:T(8,128)(2,1)}, bf16[160,256]{1,0:T(8,128)(2,1)S(1)}, u32[]{:S(2)}, u32[]{:S(2)}) collective-permute-start(bf16[160,256]{1,0:T(8,128)(2,1)} %get-tuple-element.64), channel_id=1, source_target_pairs={{0,1},{1,2},{2,3},{3,0},{4,5},{5,6},{6,7},{7,4},{8,9},{9,10},{10,1... | collective-permute-start | bytes 245768 | tf_op jit(solution)/shard_map/ppermute | solution.py:401
  7.4 8.3 %collective-permute-start.1 = (bf16[160,256]{1,0:T(8,128)(2,1)}, bf16[160,256]{1,0:T(8,128)(2,1)S(1)}, u32[]{:S(2)}, u32[]{:S(2)}) collective-permute-start(bf16[160,256]{1,0:T(8,128)(2,1)} %get-tuple-element.65), channel_id=1, source_target_pairs={{0,2},{1,3},{2,0},{3,1},{4,6},{5,7},{6,4},{7,5},{8,10},{9,11},{10,... | collective-permute-start | bytes 245768 | tf_op jit(solution)/shard_map/ppermute | solution.py:401
  10.0 5.9 %collective-permute-start.2 = (bf16[160,256]{1,0:T(8,128)(2,1)}, bf16[160,256]{1,0:T(8,128)(2,1)S(1)}, u32[]{:S(2)}, u32[]{:S(2)}) collective-permute-start(bf16[160,256]{1,0:T(8,128)(2,1)} %get-tuple-element.66), channel_id=1, source_target_pairs={{0,3},{1,0},{2,1},{3,2},{4,7},{5,4},{6,5},{7,6},{8,11},{9,8},{10,9... | collective-permute-start | bytes 245768 | tf_op jit(solution)/shard_map/ppermute | solution.py:401
  11.4 4.6 %copy-start.7 = (bf16[160,256]{1,0:T(8,128)(2,1)S(1)}, bf16[160,256]{1,0:T(8,128)(2,1)}, u32[]{:S(2)}) copy-start(bf16[160,256]{1,0:T(8,128)(2,1)} %get-tuple-element.68) | copy-start | bytes 245764
  11.4 20.0 %copy-start.1 = (f32[512]{0:T(512)S(1)}, f32[512]{0:T(512)}, u32[]{:S(2)}) copy-start(f32[512]{0:T(512)} %param.17) | copy-start | bytes 6148
  11.4 20.0 %copy-start.2 = (f32[512]{0:T(512)S(1)}, f32[512]{0:T(512)}, u32[]{:S(2)}) copy-start(f32[512]{0:T(512)} %param.18) | copy-start | bytes 6148
  15.9 15.5 %collective-permute-start.6 = (bf16[2,4,1024,128]{3,2,1,0:T(8,128)(2,1)}, bf16[2,4,1024,128]{3,2,1,0:T(8,128)(2,1)S(1)}, u32[]{:S(2)}, u32[]{:S(2)}) collective-permute-start(bf16[2,4,1024,128]{3,2,1,0:T(8,128)(2,1)} %own_heads.1.rest_0_), channel_id=1, source_target_pairs={{0,4},{4,0},{8,12},{12,8},{16,20},{20,16},{24,28},{28,24},{1,5},{5... | collective-permute-start | bytes 6291464 | tf_op jit(solution)/shard_map/ppermute | solution.py:398
  16.0 10.1 %collective-permute-start.5 = (bf16[512,256]{1,0:T(8,128)(2,1)S(1)}, bf16[512,256]{1,0:T(8,128)(2,1)S(1)}, u32[]{:S(2)}, u32[]{:S(2)}) collective-permute-start(bf16[512,256]{1,0:T(8,128)(2,1)S(1)} %pad_maximum_fusion.rest_4_.rest_2_), channel_id=1, source_target_pairs={{0,24},{4,28},{8,16},{12,20},{16,8},{20,12},{24,0},{28,4},{1,25},{... | collective-permute-start | bytes 786440 | tf_op jit(solution)/shard_map/ppermute | solution.py:398
  18.5 12.8 %collective-permute-start.4 = (bf16[512,256]{1,0:T(8,128)(2,1)S(1)}, bf16[512,256]{1,0:T(8,128)(2,1)S(1)}, u32[]{:S(2)}, u32[]{:S(2)}) collective-permute-start(bf16[512,256]{1,0:T(8,128)(2,1)S(1)} %pad_maximum_fusion.rest_4_.rest_2_), channel_id=1, source_target_pairs={{0,16},{4,20},{8,24},{12,28},{16,0},{20,4},{24,8},{28,12},{1,17},{... | collective-permute-start | bytes 786440 | tf_op jit(solution)/shard_map/ppermute | solution.py:398
  19.0 12.4 %collective-permute-start.3 = (bf16[512,256]{1,0:T(8,128)(2,1)S(1)}, bf16[512,256]{1,0:T(8,128)(2,1)S(1)}, u32[]{:S(2)}, u32[]{:S(2)}) collective-permute-start(bf16[512,256]{1,0:T(8,128)(2,1)S(1)} %pad_maximum_fusion.rest_4_.rest_2_), channel_id=1, source_target_pairs={{0,8},{4,12},{8,0},{12,4},{16,24},{20,28},{24,16},{28,20},{1,9},{5... | collective-permute-start | bytes 786440 | tf_op jit(solution)/shard_map/ppermute | solution.py:398
  19.6 3.0 %collective-permute-start.7 = (bf16[128,256]{1,0:T(8,128)(2,1)S(1)}, bf16[128,256]{1,0:T(8,128)(2,1)S(1)}, u32[]{:S(2)}, u32[]{:S(2)}) collective-permute-start(bf16[128,256]{1,0:T(8,128)(2,1)S(1)} %pad_maximum_fusion.1.rest_1_), channel_id=1, source_target_pairs={{0,4},{4,0},{8,12},{12,8},{16,20},{20,16},{24,28},{28,24},{1,5},{5... | collective-permute-start | bytes 196616 | tf_op jit(solution)/shard_map/ppermute | solution.py:398
  31.4 0.7 copy-start.6
  32.1 3.0 %copy-start = (bf16[2,4,1024,128]{3,2,1,0:T(8,128)(2,1)S(1)}, bf16[2,4,1024,128]{3,2,1,0:T(8,128)(2,1)}, u32[]{:S(2)}) copy-start(bf16[2,4,1024,128]{3,2,1,0:T(8,128)(2,1)} %own_heads.1.rest_0_) | copy-start | bytes 6291460
  32.1 3.0 %copy-start.5 = (s32[72]{0:T(128)S(1)}, s32[72]{0:T(128)}, u32[]{:S(2)}) copy-start(s32[72]{0:T(128)} %get-tuple-element.80.table_ref) | copy-start | bytes 868
  33.1 4.6 %collective-permute-start.8 = (bf16[1,128,1024]{2,1,0:T(8,128)(2,1)S(1)}, bf16[1,128,1024]{2,1,0:T(8,128)(2,1)S(1)}, u32[]{:S(2)}, u32[]{:S(2)}) collective-permute-start(bf16[1,128,1024]{2,1,0:T(8,128)(2,1)S(1)} %get-tuple-element.84), channel_id=1, source_target_pairs={{0,4},{4,0},{8,12},{12,8},{16,20},{20,16},{24,28},{28,24},{1,5},{5... | collective-permute-start | bytes 786440 | tf_op jit(solution)/shard_map/ppermute | solution.py:398
  35.0 3.4 %copy-start.4 = (s32[200]{0:T(256)S(1)}, s32[200]{0:T(256)}, u32[]{:S(2)}) copy-start(s32[200]{0:T(256)} %get-tuple-element.79.table_ref) | copy-start | bytes 2404
  37.8 6.3 %collective-permute-start.9 = (bf16[128,512]{1,0:T(8,128)(2,1)S(1)}, bf16[128,512]{1,0:T(8,128)(2,1)S(1)}, u32[]{:S(2)}, u32[]{:S(2)}) collective-permute-start(bf16[128,512]{1,0:T(8,128)(2,1)S(1)} %get-tuple-element.85), channel_id=1, source_target_pairs={{0,2},{1,3},{2,0},{3,1},{4,6},{5,7},{6,4},{7,5},{8,10},{9,11},{10,... | collective-permute-start | bytes 393224 | tf_op jit(solution)/shard_map/ppermute | solution.py:401
  38.4 8.8 %copy-start.3 = (s32[200]{0:T(256)S(1)}, s32[200]{0:T(256)}, u32[]{:S(2)}) copy-start(s32[200]{0:T(256)} %get-tuple-element.73.table_ref) | copy-start | bytes 2404
  44.1 14.6 %collective-permute-start.10 = (bf16[3,128,1024]{2,1,0:T(8,128)(2,1)S(1)}, bf16[3,128,1024]{2,1,0:T(8,128)(2,1)S(1)}, u32[]{:S(2)}, u32[]{:S(2)}) collective-permute-start(bf16[3,128,1024]{2,1,0:T(8,128)(2,1)S(1)} %get-tuple-element.93), channel_id=1, source_target_pairs={{0,4},{4,0},{8,12},{12,8},{16,20},{20,16},{24,28},{28,24},{1,5},{5... | collective-permute-start | bytes 2359304 | tf_op jit(solution)/shard_map/ppermute | solution.py:398
  44.1 11.1 %collective-permute-start.11 = (bf16[128,512]{1,0:T(8,128)(2,1)S(1)}, bf16[128,512]{1,0:T(8,128)(2,1)S(1)}, u32[]{:S(2)}, u32[]{:S(2)}) collective-permute-start(bf16[128,512]{1,0:T(8,128)(2,1)S(1)} %get-tuple-element.97), channel_id=1, source_target_pairs={{0,2},{1,3},{2,0},{3,1},{4,6},{5,7},{6,4},{7,5},{8,10},{9,11},{10,... | collective-permute-start | bytes 393224 | tf_op jit(solution)/shard_map/ppermute | solution.py:401
  55.1 8.7 %collective-permute-start.12 = (bf16[528,256]{1,0:T(8,128)(2,1)S(1)}, bf16[528,256]{1,0:T(8,128)(2,1)S(1)}, u32[]{:S(2)}, u32[]{:S(2)}) collective-permute-start(bf16[528,256]{1,0:T(8,128)(2,1)S(1)} %get-tuple-element.103), channel_id=1, source_target_pairs={{0,8},{4,12},{8,0},{12,4},{16,24},{20,28},{24,16},{28,20},{1,9},{5... | collective-permute-start | bytes 811016 | tf_op jit(solution)/shard_map/ppermute | solution.py:398
  55.2 11.7 %collective-permute-start.14 = (bf16[528,256]{1,0:T(8,128)(2,1)S(1)}, bf16[528,256]{1,0:T(8,128)(2,1)S(1)}, u32[]{:S(2)}, u32[]{:S(2)}) collective-permute-start(bf16[528,256]{1,0:T(8,128)(2,1)S(1)} %get-tuple-element.105), channel_id=1, source_target_pairs={{0,24},{4,28},{8,16},{12,20},{16,8},{20,12},{24,0},{28,4},{1,25},{... | collective-permute-start | bytes 811016 | tf_op jit(solution)/shard_map/ppermute | solution.py:398
  55.3 16.1 %collective-permute-start.13 = (bf16[528,256]{1,0:T(8,128)(2,1)S(1)}, bf16[528,256]{1,0:T(8,128)(2,1)S(1)}, u32[]{:S(2)}, u32[]{:S(2)}) collective-permute-start(bf16[528,256]{1,0:T(8,128)(2,1)S(1)} %get-tuple-element.104), channel_id=1, source_target_pairs={{0,16},{4,20},{8,24},{12,28},{16,0},{20,4},{24,8},{28,12},{1,17},{... | collective-permute-start | bytes 811016 | tf_op jit(solution)/shard_map/ppermute | solution.py:398
  58.8 12.8 %collective-permute-start.15 = (bf16[128,1024]{1,0:T(8,128)(2,1)S(1)}, bf16[128,1024]{1,0:T(8,128)(2,1)S(1)}, u32[]{:S(2)}, u32[]{:S(2)}) collective-permute-start(bf16[128,1024]{1,0:T(8,128)(2,1)S(1)} %get-tuple-element.110), channel_id=1, source_target_pairs={{0,1},{1,2},{2,3},{3,0},{4,5},{5,6},{6,7},{7,4},{8,9},{9,10},{10,1... | collective-permute-start | bytes 786440 | tf_op jit(solution)/shard_map/ppermute | solution.py:401
  62.4 11.7 %collective-permute-start.16 = (bf16[128,1024]{1,0:T(8,128)(2,1)S(1)}, bf16[128,1024]{1,0:T(8,128)(2,1)S(1)}, u32[]{:S(2)}, u32[]{:S(2)}) collective-permute-start(bf16[128,1024]{1,0:T(8,128)(2,1)S(1)} %get-tuple-element.111), channel_id=1, source_target_pairs={{0,3},{1,0},{2,1},{3,2},{4,7},{5,4},{6,5},{7,6},{8,11},{9,8},{10,9... | collective-permute-start | bytes 786440 | tf_op jit(solution)/shard_map/ppermute | solution.py:401
  74.1 5.8 %collective-permute-start.17 = (bf16[144,256]{1,0:T(8,128)(2,1)S(1)}, bf16[144,256]{1,0:T(8,128)(2,1)S(1)}, u32[]{:S(2)}, u32[]{:S(2)}) collective-permute-start(bf16[144,256]{1,0:T(8,128)(2,1)S(1)} %get-tuple-element.115), channel_id=1, source_target_pairs={{0,3},{1,0},{2,1},{3,2},{4,7},{5,4},{6,5},{7,6},{8,11},{9,8},{10,9... | collective-permute-start | bytes 221192 | tf_op jit(solution)/shard_map/ppermute | solution.py:401
  77.4 7.3 %collective-permute-start.18 = (bf16[144,256]{1,0:T(8,128)(2,1)S(1)}, bf16[144,256]{1,0:T(8,128)(2,1)S(1)}, u32[]{:S(2)}, u32[]{:S(2)}) collective-permute-start(bf16[144,256]{1,0:T(8,128)(2,1)S(1)} %get-tuple-element.116), channel_id=1, source_target_pairs={{0,2},{1,3},{2,0},{3,1},{4,6},{5,7},{6,4},{7,5},{8,10},{9,11},{10,... | collective-permute-start | bytes 221192 | tf_op jit(solution)/shard_map/ppermute | solution.py:401
  77.7 7.0 %collective-permute-start.19 = (bf16[144,256]{1,0:T(8,128)(2,1)S(1)}, bf16[144,256]{1,0:T(8,128)(2,1)S(1)}, u32[]{:S(2)}, u32[]{:S(2)}) collective-permute-start(bf16[144,256]{1,0:T(8,128)(2,1)S(1)} %get-tuple-element.117), channel_id=1, source_target_pairs={{0,1},{1,2},{2,3},{3,0},{4,5},{5,6},{6,7},{7,4},{8,9},{9,10},{10,1... | collective-permute-start | bytes 221192 | tf_op jit(solution)/shard_map/ppermute | solution.py:401
  85.5 1.2 %collective-permute-start.20 = (f32[2,512]{1,0:T(2,128)S(1)}, f32[2,512]{1,0:T(2,128)S(1)}, u32[]{:S(2)}, u32[]{:S(2)}) collective-permute-start(f32[2,512]{1,0:T(2,128)S(1)} %get-tuple-element.120), channel_id=1, source_target_pairs={{0,4},{4,0},{8,12},{12,8},{16,20},{20,16},{24,28},{28,24},{1,5},{5... | collective-permute-start | bytes 12296 | tf_op jit(solution)/shard_map/ppermute | solution.py:398

commit v3 on v2

--- a/solution.py
+++ b/solution.py
@@ -149,15 +149,15 @@
     if stage == 0:
         (key_gain_ref, value_gain_ref), rest = rest[:2], rest[2:]
     (heads_ref, stats_ref), rest = rest[:2], rest[2:]
-    if stage in (0, 3):
+    if stage in (0, 2):
         blocks, rest = rest[:count_chip], rest[count_chip:]
     if stage == 0:
         (dq_out, keys, values, keys_t, key_sum, value_sum), rest = rest[:6], rest[6:]
     else:
         (keys, values, keys_t, key_start, value_start), rest = rest[:5], rest[5:]
         dq_out, rest = rest[0], rest[1:]
-        if stage == 3:
-            kv_outs, rest = rest[:count_chip], rest[count_chip:]
+        if stage == 2:
+            (kv_own, kv_all), rest = rest[:2], rest[2:]
         (key_sum, value_sum), rest = rest[:2], rest[2:]
     lse_delta, weights_low, dscores_low, dq_sum = rest
     _, place_ka = places()
@@ -234,9 +234,10 @@
     lax.fori_loop(0, table_ref[0], unit_step, 0)
     for number in range(len(steps)):
         dq_out[number] = (dq_sum[number] * score_scale).astype(dq_out.dtype)
-    if stage != 3:
+    if stage != 2:
         return
 
+    place_chip = places()[0] // 2
     key_gains = jnp.zeros((8, HEAD_DIM), F32)
     value_gains = jnp.zeros((8, HEAD_DIM), F32)
     for number in range(count_chip):
@@ -245,8 +246,10 @@
             local = number * count_ka + step
             key_total = key_sum[local] * score_scale
             value_total = value_sum[local]
-            kv_outs[number][part, :HEAD_DIM] = key_total.astype(kv_outs[number].dtype)
-            kv_outs[number][part, HEAD_DIM:] = value_total.astype(kv_outs[number].dtype)
+            both = jnp.concatenate([key_total, value_total], axis=1)
+            kv_all[place_chip ^ number, part, :] = both.astype(BF16)
+            if number == 0:
+                kv_own[part, :] = both
             key_raw = blocks[number][part, :HEAD_DIM].astype(F32)
             value_raw = blocks[number][part, HEAD_DIM:].astype(F32)
             key_gains += jnp.sum((key_total * key_raw).reshape(TILE // 8, 8, HEAD_DIM), axis=0)
@@ -254,8 +257,9 @@
     gains = jnp.concatenate([jnp.sum(key_gains, axis=0, keepdims=True),
                              jnp.sum(value_gains, axis=0, keepdims=True)], axis=1)
     packed = pack_gains(gains)
+    kv_own[count_ka * TILE:, :] = packed
     for number in range(count_chip):
-        kv_outs[number][count_ka * TILE:, :] = packed.astype(kv_outs[number].dtype)
+        kv_all[number, count_ka * TILE:, :] = packed.astype(BF16)
 
 
 def pack_gains(gains):
@@ -265,12 +269,13 @@
     return jnp.where(rows < 3, packed, 0.0)
 
 
-def add_kernel(part_ref, other_ref, *outs):
+def add_kernel(steps, part_ref, other_ref, *outs):
     width = part_ref.shape[2]
     tile, column = 0, 0
     for out_ref in outs:
         part = pl.ds(column, out_ref.shape[1])
-        out_ref[...] = (part_ref[tile, :, part] + other_ref[tile, :, part].astype(F32)).astype(BF16)
+        other = other_ref[steps[tile], :, part].astype(F32)
+        out_ref[...] = (part_ref[tile, :, part] + other).astype(BF16)
         column += out_ref.shape[1]
         if column == width:
             tile, column = tile + 1, 0
@@ -278,24 +283,26 @@
 
 def collect_kernel(dims, key_gain_ref, value_gain_ref, *rest):
     count_chip, count_ka, share = dims
-    parts, outs = rest[:count_chip], rest[count_chip:]
-    kv_at = pl.ds(pl.multiple_of(places()[1] // share * HEAD_DIM, HEAD_DIM), HEAD_DIM)
+    own_ref, parts_ref, out_ref = rest
+    place_pb, place_ka = places()
+    others = [(place_pb // 2) ^ number for number in range(1, count_chip)]
+    kv_at = pl.ds(pl.multiple_of(place_ka // share * HEAD_DIM, HEAD_DIM), HEAD_DIM)
     gain = jnp.concatenate([key_gain_ref[:, kv_at], value_gain_ref[:, kv_at]], axis=1)
     for step in range(count_ka):
         rows = pl.ds(step * TILE, TILE)
-        total = parts[0][rows, :]
-        for number in range(1, count_chip):
-            total = total + parts[number][rows, :].astype(F32)
+        total = own_ref[rows, :]
+        for other in others:
+            total = total + parts_ref[other, rows, :].astype(F32)
         if share == 1:
             total = total * gain
-        outs[step][:TILE, :] = total.astype(outs[step].dtype)
+        out_ref[lax.rem(place_ka - step + count_ka, count_ka), :TILE, :] = total.astype(out_ref.dtype)
     spare = pl.ds(count_ka * TILE, SPARE)
-    total = parts[0][spare, :]
-    for number in range(1, count_chip):
-        total = total + parts[number][spare, :].astype(F32)
+    total = own_ref[spare, :]
+    for other in others:
+        total = total + parts_ref[other, spare, :].astype(F32)
     packed = pack_gains(jnp.sum(total, axis=0, keepdims=True))
     for step in range(count_ka):
-        outs[step][TILE:, :] = packed.astype(outs[step].dtype)
+        out_ref[step, TILE:, :] = packed.astype(out_ref.dtype)
 
 
 def turn_kernel(*refs):
@@ -327,13 +334,12 @@
 
 def finish_kernel(dims, key_gain_ref, value_gain_ref, *rest):
     count_ka, share = dims
-    pieces, rest = rest[:count_ka], rest[count_ka:]
-    dk_out, dv_out, gains_out, sums = rest
-    _, place_ka = places()
-    sums[...] = jnp.zeros_like(sums)
-    for step in range(count_ka):
-        source = lax.rem(place_ka + step, count_ka)
-        sums[source // share] += pieces[step][...].astype(F32)
+    pieces, dk_out, dv_out, gains_out, sums = rest
+    for source in range(count_ka):
+        if source % share:
+            sums[source // share] += pieces[source].astype(F32)
+        else:
+            sums[source // share] = pieces[source].astype(F32)
     for head in range(count_ka // share):
         part = pl.ds(head * HEAD_DIM, HEAD_DIM)
         key_total = sums[head, :TILE, :HEAD_DIM]
@@ -425,20 +431,21 @@
         name="own_heads",
     )(later_queries, grad_out)
     messages, own_queries = lax.optimization_barrier((messages, own_queries))
+    other_queries = swap(own_queries, 1)
     own_block = jnp.concatenate([message[:TILE] for message in messages], axis=0)
     own_stats = jnp.concatenate([message[TILE:] for message in messages], axis=0)
     blocks = [own_block] + [swap(own_block, 2 * number) for number in range(1, count_chip)]
     other_stats = swap(own_stats, 1)
     later_order, _ = lax.optimization_barrier((block_order, own_block))
-    other_queries = swap(own_queries, 1)
 
     key_tiles = count_chip * count_ka
     sum_shape = jax.ShapeDtypeStruct((key_tiles, TILE, HEAD_DIM), F32)
     key_shape = jax.ShapeDtypeStruct((key_tiles, TILE, HEAD_DIM), BF16)
     kv_shape = (query_rows + SPARE, 2 * HEAD_DIM)
     half = count_ka // 2
-    rest_steps = tuple(step for step in range(1, count_ka) if step != half) + (0,)
-    stages = ((1, (half,)), (0, (half,)), (1, rest_steps), (0, rest_steps))
+    early = (half, 0)
+    late = tuple(step for step in range(1, count_ka) if step != half)
+    stages = ((1, tuple(range(count_ka))), (0, early), (0, late))
     tables = pl.pallas_call(
         functools.partial(plan_kernel, (count_chip, count_ka, stages)),
         in_specs=in_smem(3),
@@ -468,22 +475,23 @@
             ],
             compiler_params=params(14 + key_tiles // 2),
             cost_estimate=pl.CostEstimate(
-                flops=10 * pairs * TILE * TILE * width if stage < 3 else 0,
-                bytes_accessed=1 << 20 if stage < 3 else 0,
+                flops=10 * pairs * TILE * TILE * width if stage < 2 else 0,
+                bytes_accessed=1 << 20 if stage < 2 else 0,
                 transcendentals=0,
             ),
-            name=("attention_other_first", "attention_own_first", "attention_other", "attention_own")[stage],
+            name=("attention_other", "attention_own_first", "attention_own")[stage],
         )(tables[stage], *operands)
 
     def part_shape(stage, dtype):
         return jax.ShapeDtypeStruct((len(stages[stage][1]), HEAD_DIM, width), dtype)
 
-    def add(part, other, cuts):
+    def add(part, other, steps, cuts):
+        widths = [width // cut for cut in cuts for _ in range(cut)]
         return pl.pallas_call(
-            add_kernel,
+            functools.partial(add_kernel, steps),
             in_specs=in_vmem(2),
-            out_specs=in_vmem(part.shape[0] * cuts),
-            out_shape=[jax.ShapeDtypeStruct((HEAD_DIM, width // cuts), BF16)] * (part.shape[0] * cuts),
+            out_specs=in_vmem(len(widths)),
+            out_shape=[jax.ShapeDtypeStruct((HEAD_DIM, each), BF16) for each in widths],
             compiler_params=params(4 * part.shape[0]),
             name="add_queries",
         )(part, other)
@@ -498,44 +506,44 @@
         1, [part_shape(1, F32)] + [sum_shape] * 2, [], own_queries, own_stats, *keys, *sums
     )
     dq_parts = [None] * count_ka
-    dq_first = add(dq_own, dq_back, 2)
+    *dq_first, dq_parts[0] = add(dq_own, dq_back, early, (2, 1))
     dq_halves = [turn(part, half) for part in dq_first]
-    rest_stats, _ = lax.optimization_barrier((other_stats, dq_first[0]))
-    dq_other, *sums = attend(
-        2, [part_shape(2, BF16)] + [sum_shape] * 2, [], other_queries, rest_stats, *keys, *sums
+    late_stats, _ = lax.optimization_barrier((own_stats, dq_first[0]))
+    dq_own, kv_own, kv_all = attend(
+        2,
+        [
+            part_shape(2, F32),
+            jax.ShapeDtypeStruct(kv_shape, F32),
+            jax.ShapeDtypeStruct((count_chip, *kv_shape), BF16),
+        ],
+        [VMEM(sum_shape.shape, F32)] * 2,
+        own_queries, late_stats, *blocks, *keys, *sums,
     )
-    dq_other, dq_halves[0] = lax.optimization_barrier((dq_other, dq_halves[0]))
-    dq_back = swap(dq_other, 1)
-    dq_own, *kv_own = attend(
-        3,
-        [part_shape(3, F32), jax.ShapeDtypeStruct(kv_shape, F32)]
-        + [jax.ShapeDtypeStruct(kv_shape, BF16)] * (count_chip - 1),
-        [VMEM(sum_shape.shape, F32)] * 2,
-        own_queries, own_stats, *blocks, *keys, *sums,
-    )
-    for step, tile in zip(rest_steps, add(dq_own, dq_back, 1)):
-        dq_parts[step] = turn(tile, step) if step else tile
-    kv_own[2], dq_halves[1] = lax.optimization_barrier((kv_own[2], dq_halves[1]))
-    kv_parts = [kv_own[0]] + [swap(kv_own[number], 2 * number) for number in range(1, count_chip)]
+    for step, tile in zip(late, add(dq_own, dq_back, late, (1,) * len(late))):
+        dq_parts[step] = turn(tile, step)
+    kv_all, dq_halves[0] = lax.optimization_barrier((kv_all, dq_halves[0]))
+    cores = [list(range(core, count_pb, 2)) for core in range(2)]
+    kv_parts = lax.all_to_all(kv_all, "pb", 0, 0, axis_index_groups=cores)
+
     piece_type = BF16 if share == 1 else F32
-    piece_shape = (TILE + SPARE, 2 * HEAD_DIM)
+    piece_shape = (count_ka, TILE + SPARE, 2 * HEAD_DIM)
     totals = pl.pallas_call(
         functools.partial(collect_kernel, (count_chip, count_ka, share)),
-        in_specs=in_vmem(2 + count_chip),
-        out_specs=in_vmem(count_ka),
-        out_shape=[jax.ShapeDtypeStruct(piece_shape, piece_type)] * count_ka,
+        in_specs=in_vmem(4),
+        out_specs=in_vmem(1)[0],
+        out_shape=jax.ShapeDtypeStruct(piece_shape, piece_type),
         compiler_params=params(24),
         name="collect",
-    )(key_gain, value_gain, *kv_parts)
-    first_turns = [dq_parts[step] for step in rest_steps if step]
+    )(key_gain, value_gain, kv_own, kv_parts)
+    first_turns = [dq_parts[step] for step in late]
     totals, first_turns = lax.optimization_barrier((totals, first_turns))
-    for step, tile in zip([step for step in rest_steps if step], first_turns):
+    for step, tile in zip(late, first_turns):
         dq_parts[step] = tile
-    pieces = [totals[0]] + [turn(totals[step], -step) for step in range(1, count_ka)]
+    pieces = lax.all_to_all(totals, "ka", 0, 0)
 
     grad_keys, grad_values, gains = pl.pallas_call(
         functools.partial(finish_kernel, (count_ka, share)),
-        in_specs=in_vmem(2 + count_ka),
+        in_specs=in_vmem(3),
         out_specs=in_vmem(3),
         out_shape=[
             jax.ShapeDtypeStruct(key_rows.shape, BF16),
@@ -545,7 +553,7 @@
         scratch_shapes=[VMEM((kv_heads, TILE + SPARE, 2 * HEAD_DIM), F32)],
         compiler_params=params(16),
         name="finish",
-    )(key_gain, value_gain, *pieces)
+    )(key_gain, value_gain, pieces)
     gains = gains + swap(gains, 1)
     first = [dq_parts[0], *dq_halves]
     turned = pl.pallas_call(
@@ -557,7 +565,6 @@
         cost_estimate=pl.CostEstimate(flops=0, bytes_accessed=1 << 22, transcendentals=0),
         name="turn_queries",
     )(*first)
-    late = [step for step in rest_steps if step]
     where = ((0, 0, False), (half, 0, False), (half, heads_dev // 2, False))
     where += tuple((step, 0, True) for step in late)
     grad_queries = pl.pallas_call(

time: 88.7 us -> 99.5 us (1.12)
  starting transfers between devices: 28.9 us -> 38 us
  local copies, waits for them, and re-layouts: 1.3 us -> 6.13 us
  Pallas kernels: 29.8 us -> 27.1 us
    all_to_all x0 -> x2, starting transfers between devices: none -> 19.1 us  [the longest x1 14.9 us: shards(): kv_parts = lax.all_to_all(kv_all, 'pb', 0, 0, axis_index_groups=cores)]
    all_to_all x0 -> x2, waiting for transfers between devices: none -> 14.3 us  [the longest x1 8.69 us: shards(): pieces = lax.all_to_all(totals, 'ka', 0, 0)]
    ppermute x10 -> x7, waiting for transfers between devices: 9.98 us -> 2.12 us  [turn(): lax.ppermute(array, 'ka', [(at, (at + step) % count_ka) for at in range(c...]
    ppermute x11 -> x7, waiting for transfers between devices: 16.5 us -> 9.44 us  [swap(): lax.ppermute(array, 'pb', [(at, at ^ number) for at in range(count_pb)])]
    ppermute x11 -> x7, starting transfers between devices: 9.15 us -> 3.7 us  [swap(): lax.ppermute(array, 'pb', [(at, at ^ number) for at in range(count_pb)])]
    unnamed x16 -> x36, local copies, waits for them, and re-layouts: 0.68 us -> 5.51 us
    ppermute x10 -> x7, starting transfers between devices: 19.8 us -> 15.3 us  [turn(): lax.ppermute(array, 'ka', [(at, (at + step) % count_ka) for at in range(c...]
    pallas_call x4 -> x3, Pallas kernels: 17.3 us -> 13 us  [attend(): pl.pallas_call(functools.partial(attention_kernel, dims), in_specs=in_sme...]
  transfers between devices with their start and end apart: 21 -> 16, of which waited for: 11 -> 10; matrix products, arithmetic and copies ran while one was open for 0% -> 0% of each run, Pallas kernels for 28% -> 15%
where the time goes in v3:
time: 99.5 us; the launch traced here: 98 us
  starting transfers between devices  38 us (38%)
  Pallas kernels  27.1 us (27%)
  waiting for transfers between devices  25.8 us (26%)
  local copies, waits for them, and re-layouts  6.13 us (6%)
    ppermute x7, starting transfers between devices, turn(): lax.ppermute(array, 'ka', [(at, (at + step) % count_ka) for at in range(c...  15.3 us
    all_to_all x1, starting transfers between devices, shards(): kv_parts = lax.all_to_all(kv_all, 'pb', 0, 0, axis_index_groups=cores)  14.9 us
    pallas_call x3, Pallas kernels, attend(): pl.pallas_call(functools.partial(attention_kernel, dims), in_specs=in_sme...  13 us
    ppermute x7, waiting for transfers between devices, swap(): lax.ppermute(array, 'pb', [(at, at ^ number) for at in range(count_pb)])  9.44 us
    all_to_all x1, waiting for transfers between devices, shards(): pieces = lax.all_to_all(totals, 'ka', 0, 0)  8.69 us
    all_to_all x1, waiting for transfers between devices, shards(): kv_parts = lax.all_to_all(kv_all, 'pb', 0, 0, axis_index_groups=cores)  5.58 us
    unnamed x36, local copies, waits for them, and re-layouts  5.51 us
    all_to_all x1, starting transfers between devices, shards(): pieces = lax.all_to_all(totals, 'ka', 0, 0)  4.12 us
  transfers between devices with their start and end apart: 16, of which 10 were waited for; matrix products, arithmetic and copies ran while one was open for 0% of the time, Pallas kernels for 15%

profile of v3, /device:TPU:0, one launch (start us, length us, event | category | flops | bytes accessed | tf_op | source)
XLA Modules:
  0.0 98.0 jit_solution(1917097586977982103)
XLA Ops:
  0.6 3.7 %prepare.1 = (bf16[160,256]{1,0:T(8,128)(2,1)}, bf16[160,256]{1,0:T(8,128)(2,1)}, bf16[160,256]{1,0:T(8,128)(2,1)}, bf16[160,256]{1,0:T(8,128)(2,1)}) custom-call(bf16[128,512]{1,0:T(8,128)(2,1)} %key_ref.1, bf16[128,512]{1,0:T(8,128)(2,1)} %value_ref.1, bf16[128,4096]{1,0:T(8,128)(2,1)} %attn_ref.1, bf16[512,4096]{1,0:T(8,128)(2,1)} %grads_ref.3, ...), custom_call_target="tpu_custom_call" | custom-call | tf_op jit(solution)/shard_map/prepare/pallas_call | solution.py:409
  4.3 3.1 %collective-permute-start = (bf16[160,256]{1,0:T(8,128)(2,1)}, bf16[160,256]{1,0:T(8,128)(2,1)S(1)}, u32[]{:S(2)}, u32[]{:S(2)}) collective-permute-start(bf16[160,256]{1,0:T(8,128)(2,1)} %get-tuple-element.49), channel_id=1, source_target_pairs={{0,1},{1,2},{2,3},{3,0},{4,5},{5,6},{6,7},{7,4},{8,9},{9,10},{10,1... | collective-permute-start | bytes 245768 | tf_op jit(solution)/shard_map/ppermute | solution.py:407
  7.4 2.6 %collective-permute-start.1 = (bf16[160,256]{1,0:T(8,128)(2,1)}, bf16[160,256]{1,0:T(8,128)(2,1)S(1)}, u32[]{:S(2)}, u32[]{:S(2)}) collective-permute-start(bf16[160,256]{1,0:T(8,128)(2,1)} %get-tuple-element.50), channel_id=1, source_target_pairs={{0,2},{1,3},{2,0},{3,1},{4,6},{5,7},{6,4},{7,5},{8,10},{9,11},{10,... | collective-permute-start | bytes 245768 | tf_op jit(solution)/shard_map/ppermute | solution.py:407
  10.0 1.3 %collective-permute-start.2 = (bf16[160,256]{1,0:T(8,128)(2,1)}, bf16[160,256]{1,0:T(8,128)(2,1)S(1)}, u32[]{:S(2)}, u32[]{:S(2)}) collective-permute-start(bf16[160,256]{1,0:T(8,128)(2,1)} %get-tuple-element.51), channel_id=1, source_target_pairs={{0,3},{1,0},{2,1},{3,2},{4,7},{5,4},{6,5},{7,6},{8,11},{9,8},{10,9... | collective-permute-start | bytes 245768 | tf_op jit(solution)/shard_map/ppermute | solution.py:407
  11.3 3.5 %own_heads.1.rest_0_ = bf16[2,4,1024,128]{3,2,1,0:T(8,128)(2,1)} custom-call(bf16[512,4096]{1,0:T(8,128)(2,1)} %queries_ref, bf16[512,4096]{1,0:T(8,128)(2,1)} %grads_ref.3), custom_call_target="tpu_custom_call" | custom-call | bytes 4194304 | tf_op jit(solution)/shard_map/own_heads/pallas_call | solution.py:423
  14.9 0.0 collective-permute-done
  14.9 0.8 collective-permute-done.1
  15.7 0.2 collective-permute-done.2
  15.9 0.0 collective-permute-start.3
  15.9 0.0 copy-done.17
  16.0 2.5 %collective-permute-start.7 = (bf16[512,256]{1,0:T(8,128)(2,1)S(1)}, bf16[512,256]{1,0:T(8,128)(2,1)S(1)}, u32[]{:S(2)}, u32[]{:S(2)}) collective-permute-start(bf16[512,256]{1,0:T(8,128)(2,1)S(1)} %pad_maximum_fusion.rest_4_.rest_2_), channel_id=1, source_target_pairs={{0,24},{4,28},{8,16},{12,20},{16,8},{20,12},{24,0},{28,4},{1,25},{... | collective-permute-start | bytes 786440 | tf_op jit(solution)/shard_map/ppermute | solution.py:404
  18.5 0.5 collective-permute-start.6
  19.0 0.5 collective-permute-start.5
  19.6 0.1 collective-permute-start.4
  19.7 3.1 %plan.1 = (s32[264]{0:T(512)}, s32[136]{0:T(256)}, s32[136]{0:T(256)}) custom-call(s32[32]{0:T(128)} %order_ref, s32[32]{0:T(128)} %doc_ref.1, s32[32,32]{1,0:T(8,128)} %mask_ref.1), custom_call_target="tpu_custom_call" | custom-call | bytes 4194304 | tf_op jit(solution)/shard_map/plan/pallas_call | solution.py:449
  22.7 0.0 collective-permute-done.4.rest_3_
  22.7 3.4 %collective-permute-done.7.rest_7_.rest_5_ = bf16[512,256]{1,0:T(8,128)(2,1)S(1)} collective-permute-done((bf16[512,256]{1,0:T(8,128)(2,1)S(1)}, bf16[512,256]{1,0:T(8,128)(2,1)S(1)}, u32[]{:S(2)}, u32[]{:S(2)}) %collective-permute-start.7) | collective-permute-done | bytes 262176 | tf_op jit(solution)/shard_map/ppermute | solution.py:404
  26.1 5.2 %collective-permute-done.6.rest_6_.rest_4_ = bf16[512,256]{1,0:T(8,128)(2,1)S(1)} collective-permute-done((bf16[512,256]{1,0:T(8,128)(2,1)S(1)}, bf16[512,256]{1,0:T(8,128)(2,1)S(1)}, u32[]{:S(2)}, u32[]{:S(2)}) %collective-permute-start.6) | collective-permute-done | bytes 262176 | tf_op jit(solution)/shard_map/ppermute | solution.py:404
  31.3 0.1 collective-permute-done.5.rest_5_.rest_3_
  31.4 0.0 collective-permute-done.3.rest_2_
  31.4 0.0 copy-done.11
  31.4 0.0 copy-done.12
  31.4 0.0 copy-start.15
  31.4 0.7 copy-done.15
  32.1 8.1 %attention_other.1 = (bf16[4,128,1024]{2,1,0:T(8,128)(2,1)S(1)}, bf16[16,128,128]{2,1,0:T(8,128)(2,1)S(1)}, bf16[16,128,128]{2,1,0:T(8,128)(2,1)S(1)}, bf16[16,1...) custom-call(s32[264]{0:T(512)S(1)} %copy-done.15, f32[1,512]{1,0:T(1,128)S(1)} %bitcast.4, ...), custom_call_target="tpu_custom_call" | custom-call | flops 10737418240 | bytes 1048576 | tf_op jit(solution)/shard_map/attention_other/pallas_call | solution.py:465
  40.3 0.0 copy-done.3
  40.3 0.0 copy-done.5
  40.3 0.1 collective-permute-start.8
  40.4 0.0 copy-done
  40.4 0.0 copy-done.16
  40.4 1.8 %attention_own_first.1 = (f32[2,128,1024]{2,1,0:T(8,128)S(1)}, f32[16,128,128]{2,1,0:T(8,128)S(1)}, f32[16,128,128]{2,1,0:T(8,128)S(1)}) custom-call(s32[136]{0:T(256)S(1)} %copy-done.16, bf16[2,4,1024,128]{3,2,1,0:T(8,128)(2,1)S(1)} %copy-done, bf16[128,256]{1,0:T(8,128)(2,1)S(1)} %pad_maximum_fusion.1.rest_1_, ...), custom_call_target="tpu_custom_call" | custom-call | flops 5368709120 | bytes 1048576 | tf_op jit(solution)/shard_map/attention_own_first/pallas_call | solution.py:465
  42.2 0.0 copy-start.4
  42.2 0.0 copy-start.6
  42.2 0.0 copy-start.13
  42.2 0.8 collective-permute-done.8.other_ref
  43.0 0.1 add_queries.2
  43.1 0.7 copy-done.7
  43.9 0.6 copy-done.14
  44.5 1.5 %collective-permute-start.9 = (bf16[128,512]{1,0:T(8,128)(2,1)S(1)}, bf16[128,512]{1,0:T(8,128)(2,1)S(1)}, u32[]{:S(2)}, u32[]{:S(2)}) collective-permute-start(bf16[128,512]{1,0:T(8,128)(2,1)S(1)} %get-tuple-element.70), channel_id=1, source_target_pairs={{0,2},{1,3},{2,0},{3,1},{4,6},{5,7},{6,4},{7,5},{8,10},{9,11},{10,... | collective-permute-start | bytes 393224 | tf_op jit(solution)/shard_map/ppermute | solution.py:407
  46.0 0.0 copy-done.13
  46.0 3.1 %attention_own.1 = (f32[2,128,1024]{2,1,0:T(8,128)S(1)}, f32[528,256]{1,0:T(8,128)S(1)}, bf16[4,528,256]{2,1,0:T(8,128)(2,1)}) custom-call(s32[136]{0:T(256)S(1)} %copy-done.13, bf16[2,4,1024,128]{3,2,1,0:T(8,128)(2,1)S(1)} %copy-done, bf16[128,256]{1,0:T(8,128)(2,1)S(1)} %pad_maximum_fusion.1.rest_1_, bf16[512,256]{1,0:T(8,128)(2,1)S(1)} %pad_maximum_fusion.rest_4_.rest_2_, ...), custom_call_target="tpu_custom_call" | custom-call | tf_op jit(solution)/shard_map/attention_own/pallas_call | solution.py:465
  49.1 0.8 copy-done.1
  49.9 0.4 collective-permute-done.9.refs_1_
  50.4 0.7 copy-done.9
  51.0 14.9 %all-to-all-start = ((bf16[4,528,256]{2,1,0:T(8,128)(2,1)}), bf16[4,528,256]{2,1,0:T(8,128)(2,1)S(1)}, u32[]{:S(2)}, u32[]{:S(2)}) async-start(bf16[4,528,256]{2,1,0:T(8,128)(2,1)} %get-tuple-element.81), calls=%async_computation | async-start | bytes 2162688 | tf_op jit(solution)/shard_map/all_to_all | solution.py:526
  66.0 0.9 add_queries.3
  66.8 2.3 %collective-permute-start.11 = (bf16[128,1024]{1,0:T(8,128)(2,1)}, bf16[128,1024]{1,0:T(8,128)(2,1)S(1)}, u32[]{:S(2)}, u32[]{:S(2)}) collective-permute-start(bf16[128,1024]{1,0:T(8,128)(2,1)} %get-tuple-element.83), channel_id=1, source_target_pairs={{0,1},{1,2},{2,3},{3,0},{4,5},{5,6},{6,7},{7,4},{8,9},{9,10},{10,1... | collective-permute-start | bytes 786440 | tf_op jit(solution)/shard_map/ppermute | solution.py:407
  69.1 1.5 %collective-permute-start.12 = (bf16[128,1024]{1,0:T(8,128)(2,1)}, bf16[128,1024]{1,0:T(8,128)(2,1)S(1)}, u32[]{:S(2)}, u32[]{:S(2)}) collective-permute-start(bf16[128,1024]{1,0:T(8,128)(2,1)} %get-tuple-element.84), channel_id=1, source_target_pairs={{0,3},{1,0},{2,1},{3,2},{4,7},{5,4},{6,5},{7,6},{8,11},{9,8},{10,9... | collective-permute-start | bytes 786440 | tf_op jit(solution)/shard_map/ppermute | solution.py:407
  70.6 5.6 %all-to-all-done.rest_1_ = bf16[4,528,256]{2,1,0:T(8,128)(2,1)S(1)} async-done(((bf16[4,528,256]{2,1,0:T(8,128)(2,1)}), bf16[4,528,256]{2,1,0:T(8,128)(2,1)S(1)}, u32[]{:S(2)}, u32[]{:S(2)}) %all-to-all-start) | async-done | bytes 1081376 | tf_op jit(solution)/shard_map/all_to_all | solution.py:526
  76.2 1.0 %copy-done.2 = f32[528,256]{1,0:T(8,128)S(1)} copy-done((f32[528,256]{1,0:T(8,128)S(1)}, f32[528,256]{1,0:T(8,128)}, u32[]{:S(2)}) %copy-start.2) | copy-done | bytes 540696
  77.3 0.9 collect.1
  78.1 0.0 collective-permute-done.11.rest_3_
  78.1 0.0 collective-permute-done.12.rest_4_
  78.1 4.1 %all-to-all-start.1 = ((bf16[4,144,256]{2,1,0:T(8,128)(2,1)}), bf16[4,144,256]{2,1,0:T(8,128)(2,1)S(1)}, u32[]{:S(2)}, u32[]{:S(2)}) async-start(bf16[4,144,256]{2,1,0:T(8,128)(2,1)} %collect.1), calls=%async_computation.1 | async-start | bytes 589824 | tf_op jit(solution)/shard_map/all_to_all | solution.py:542
  82.3 2.9 %collective-permute-start.10 = (bf16[128,512]{1,0:T(8,128)(2,1)}, bf16[128,512]{1,0:T(8,128)(2,1)S(1)}, u32[]{:S(2)}, u32[]{:S(2)}) collective-permute-start(bf16[128,512]{1,0:T(8,128)(2,1)} %copy-done.14), channel_id=1, source_target_pairs={{0,2},{1,3},{2,0},{3,1},{4,6},{5,7},{6,4},{7,5},{8,10},{9,11},{10,... | collective-permute-start | bytes 393224 | tf_op jit(solution)/shard_map/ppermute | solution.py:407
  85.2 8.7 %all-to-all-done.1.rest_0_ = bf16[4,144,256]{2,1,0:T(8,128)(2,1)S(1)} async-done(((bf16[4,144,256]{2,1,0:T(8,128)(2,1)}), bf16[4,144,256]{2,1,0:T(8,128)(2,1)S(1)}, u32[]{:S(2)}, u32[]{:S(2)}) %all-to-all-start.1) | async-done | bytes 294944 | tf_op jit(solution)/shard_map/all_to_all | solution.py:542
  93.9 0.7 finish.1
  94.6 0.0 collective-permute-start.13
  94.6 0.7 collective-permute-done.10.refs_2_
  95.3 0.9 copy-done.10
  96.2 0.2 turn_queries.1
  96.4 1.0 %place_queries.1 = bf16[128,4096]{1,0:T(8,128)(2,1)} custom-call(bf16[128,1024]{1,0:T(8,128)(2,1)S(1)} %get-tuple-element.77.rest_0_, bf16[128,512]{1,0:T(8,128)(2,1)S(1)} %get-tuple-element.78.rest_1_, bf16[128,512]{1,0:T(8,128)(2,1)S(1)} %get-tuple-element.79.rest_2_, bf16[128,1024]{1,0:T(8,128)(2,1)S(1)} %collective-permute-done.11.rest_3_, ...), custom_call_target="tpu_custom_call" | custom-call | bytes 2097152 | tf_op jit(solution)/shard_map/place_queries/pallas_call | solution.py:570
  97.4 0.0 collective-permute-done.13
  97.5 0.6 fusion
  (28 shorter events, 0.1 us)
Async XLA Ops:
  4.3 10.5 %collective-permute-start = (bf16[160,256]{1,0:T(8,128)(2,1)}, bf16[160,256]{1,0:T(8,128)(2,1)S(1)}, u32[]{:S(2)}, u32[]{:S(2)}) collective-permute-start(bf16[160,256]{1,0:T(8,128)(2,1)} %get-tuple-element.49), channel_id=1, source_target_pairs={{0,1},{1,2},{2,3},{3,0},{4,5},{5,6},{6,7},{7,4},{8,9},{9,10},{10,1... | collective-permute-start | bytes 245768 | tf_op jit(solution)/shard_map/ppermute | solution.py:407
  7.4 8.3 %collective-permute-start.1 = (bf16[160,256]{1,0:T(8,128)(2,1)}, bf16[160,256]{1,0:T(8,128)(2,1)S(1)}, u32[]{:S(2)}, u32[]{:S(2)}) collective-permute-start(bf16[160,256]{1,0:T(8,128)(2,1)} %get-tuple-element.50), channel_id=1, source_target_pairs={{0,2},{1,3},{2,0},{3,1},{4,6},{5,7},{6,4},{7,5},{8,10},{9,11},{10,... | collective-permute-start | bytes 245768 | tf_op jit(solution)/shard_map/ppermute | solution.py:407
  10.0 5.9 %collective-permute-start.2 = (bf16[160,256]{1,0:T(8,128)(2,1)}, bf16[160,256]{1,0:T(8,128)(2,1)S(1)}, u32[]{:S(2)}, u32[]{:S(2)}) collective-permute-start(bf16[160,256]{1,0:T(8,128)(2,1)} %get-tuple-element.51), channel_id=1, source_target_pairs={{0,3},{1,0},{2,1},{3,2},{4,7},{5,4},{6,5},{7,6},{8,11},{9,8},{10,9... | collective-permute-start | bytes 245768 | tf_op jit(solution)/shard_map/ppermute | solution.py:407
  11.3 4.6 %copy-start.17 = (bf16[160,256]{1,0:T(8,128)(2,1)S(1)}, bf16[160,256]{1,0:T(8,128)(2,1)}, u32[]{:S(2)}) copy-start(bf16[160,256]{1,0:T(8,128)(2,1)} %get-tuple-element.53) | copy-start | bytes 245764
  11.3 20.1 %copy-start.11 = (f32[512]{0:T(512)S(1)}, f32[512]{0:T(512)}, u32[]{:S(2)}) copy-start(f32[512]{0:T(512)} %param.17) | copy-start | bytes 6148
  11.3 20.1 %copy-start.12 = (f32[512]{0:T(512)S(1)}, f32[512]{0:T(512)}, u32[]{:S(2)}) copy-start(f32[512]{0:T(512)} %param.18) | copy-start | bytes 6148
  15.9 15.5 %collective-permute-start.3 = (bf16[2,4,1024,128]{3,2,1,0:T(8,128)(2,1)}, bf16[2,4,1024,128]{3,2,1,0:T(8,128)(2,1)}, u32[]{:S(2)}, u32[]{:S(2)}) collective-permute-start(bf16[2,4,1024,128]{3,2,1,0:T(8,128)(2,1)} %own_heads.1.rest_0_), channel_id=1, source_target_pairs={{0,4},{4,0},{8,12},{12,8},{16,20},{20,16},{24,28},{28,24},{1,5},{5... | collective-permute-start | bytes 6291464 | tf_op jit(solution)/shard_map/ppermute | solution.py:404
  16.0 10.1 %collective-permute-start.7 = (bf16[512,256]{1,0:T(8,128)(2,1)S(1)}, bf16[512,256]{1,0:T(8,128)(2,1)S(1)}, u32[]{:S(2)}, u32[]{:S(2)}) collective-permute-start(bf16[512,256]{1,0:T(8,128)(2,1)S(1)} %pad_maximum_fusion.rest_4_.rest_2_), channel_id=1, source_target_pairs={{0,24},{4,28},{8,16},{12,20},{16,8},{20,12},{24,0},{28,4},{1,25},{... | collective-permute-start | bytes 786440 | tf_op jit(solution)/shard_map/ppermute | solution.py:404
  18.5 12.8 %collective-permute-start.6 = (bf16[512,256]{1,0:T(8,128)(2,1)S(1)}, bf16[512,256]{1,0:T(8,128)(2,1)S(1)}, u32[]{:S(2)}, u32[]{:S(2)}) collective-permute-start(bf16[512,256]{1,0:T(8,128)(2,1)S(1)} %pad_maximum_fusion.rest_4_.rest_2_), channel_id=1, source_target_pairs={{0,16},{4,20},{8,24},{12,28},{16,0},{20,4},{24,8},{28,12},{1,17},{... | collective-permute-start | bytes 786440 | tf_op jit(solution)/shard_map/ppermute | solution.py:404
  19.0 12.4 %collective-permute-start.5 = (bf16[512,256]{1,0:T(8,128)(2,1)S(1)}, bf16[512,256]{1,0:T(8,128)(2,1)S(1)}, u32[]{:S(2)}, u32[]{:S(2)}) collective-permute-start(bf16[512,256]{1,0:T(8,128)(2,1)S(1)} %pad_maximum_fusion.rest_4_.rest_2_), channel_id=1, source_target_pairs={{0,8},{4,12},{8,0},{12,4},{16,24},{20,28},{24,16},{28,20},{1,9},{5... | collective-permute-start | bytes 786440 | tf_op jit(solution)/shard_map/ppermute | solution.py:404
  19.6 3.1 %collective-permute-start.4 = (bf16[128,256]{1,0:T(8,128)(2,1)S(1)}, bf16[128,256]{1,0:T(8,128)(2,1)S(1)}, u32[]{:S(2)}, u32[]{:S(2)}) collective-permute-start(bf16[128,256]{1,0:T(8,128)(2,1)S(1)} %pad_maximum_fusion.1.rest_1_), channel_id=1, source_target_pairs={{0,4},{4,0},{8,12},{12,8},{16,20},{20,16},{24,28},{28,24},{1,5},{5... | collective-permute-start | bytes 196616 | tf_op jit(solution)/shard_map/ppermute | solution.py:404
  31.3 9.0 %copy-start.3 = (bf16[512,256]{1,0:T(8,128)(2,1)}, bf16[512,256]{1,0:T(8,128)(2,1)S(1)}, u32[]{:S(2)}) copy-start(bf16[512,256]{1,0:T(8,128)(2,1)S(1)} %collective-permute-done.6.rest_6_.rest_4_) | copy-start | bytes 786436
  31.4 8.9 %copy-start.5 = (bf16[512,256]{1,0:T(8,128)(2,1)}, bf16[512,256]{1,0:T(8,128)(2,1)S(1)}, u32[]{:S(2)}) copy-start(bf16[512,256]{1,0:T(8,128)(2,1)S(1)} %collective-permute-done.5.rest_5_.rest_3_) | copy-start | bytes 786436
  31.4 0.7 copy-start.15
  32.1 8.2 %copy-start = (bf16[2,4,1024,128]{3,2,1,0:T(8,128)(2,1)S(1)}, bf16[2,4,1024,128]{3,2,1,0:T(8,128)(2,1)}, u32[]{:S(2)}) copy-start(bf16[2,4,1024,128]{3,2,1,0:T(8,128)(2,1)} %own_heads.1.rest_0_) | copy-start | bytes 6291460
  32.1 8.2 %copy-start.16 = (s32[136]{0:T(256)S(1)}, s32[136]{0:T(256)}, u32[]{:S(2)}) copy-start(s32[136]{0:T(256)} %get-tuple-element.58.table_ref) | copy-start | bytes 1636
  40.3 2.7 %collective-permute-start.8 = (bf16[4,128,1024]{2,1,0:T(8,128)(2,1)S(1)}, bf16[4,128,1024]{2,1,0:T(8,128)(2,1)S(1)}, u32[]{:S(2)}, u32[]{:S(2)}) collective-permute-start(bf16[4,128,1024]{2,1,0:T(8,128)(2,1)S(1)} %get-tuple-element.67), channel_id=1, source_target_pairs={{0,4},{4,0},{8,12},{12,8},{16,20},{20,16},{24,28},{28,24},{1,5},{5... | collective-permute-start | bytes 3145736 | tf_op jit(solution)/shard_map/ppermute | solution.py:404
  42.2 3.8 %copy-start.4 = (bf16[512,256]{1,0:T(8,128)(2,1)S(1)}, bf16[512,256]{1,0:T(8,128)(2,1)}, u32[]{:S(2)}) copy-start(bf16[512,256]{1,0:T(8,128)(2,1)} %copy-done.3) | copy-start | bytes 786436
  42.2 3.8 %copy-start.6 = (bf16[512,256]{1,0:T(8,128)(2,1)S(1)}, bf16[512,256]{1,0:T(8,128)(2,1)}, u32[]{:S(2)}) copy-start(bf16[512,256]{1,0:T(8,128)(2,1)} %copy-done.5) | copy-start | bytes 786436
  42.2 3.8 %copy-start.13 = (s32[136]{0:T(256)S(1)}, s32[136]{0:T(256)}, u32[]{:S(2)}) copy-start(s32[136]{0:T(256)} %get-tuple-element.69.table_ref) | copy-start | bytes 1636
  43.1 0.7 copy-start.7
  43.8 0.6 copy-start.14
  44.5 5.9 %collective-permute-start.9 = (bf16[128,512]{1,0:T(8,128)(2,1)S(1)}, bf16[128,512]{1,0:T(8,128)(2,1)S(1)}, u32[]{:S(2)}, u32[]{:S(2)}) collective-permute-start(bf16[128,512]{1,0:T(8,128)(2,1)S(1)} %get-tuple-element.70), channel_id=1, source_target_pairs={{0,2},{1,3},{2,0},{3,1},{4,6},{5,7},{6,4},{7,5},{8,10},{9,11},{10,... | collective-permute-start | bytes 393224 | tf_op jit(solution)/shard_map/ppermute | solution.py:407
  49.1 0.8 copy-start.1
  50.4 0.7 copy-start.9
  51.0 25.2 %all-to-all-start = ((bf16[4,528,256]{2,1,0:T(8,128)(2,1)}), bf16[4,528,256]{2,1,0:T(8,128)(2,1)S(1)}, u32[]{:S(2)}, u32[]{:S(2)}) async-start(bf16[4,528,256]{2,1,0:T(8,128)(2,1)} %get-tuple-element.81), calls=%async_computation | async-start | bytes 2162688 | tf_op jit(solution)/shard_map/all_to_all | solution.py:526
  66.0 29.3 %copy-start.8 = (bf16[128,1024]{1,0:T(8,128)(2,1)S(1)}, bf16[128,1024]{1,0:T(8,128)(2,1)}, u32[]{:S(2)}) copy-start(bf16[128,1024]{1,0:T(8,128)(2,1)} %copy-done.7) | copy-start | bytes 786436
  66.8 11.3 %collective-permute-start.11 = (bf16[128,1024]{1,0:T(8,128)(2,1)}, bf16[128,1024]{1,0:T(8,128)(2,1)S(1)}, u32[]{:S(2)}, u32[]{:S(2)}) collective-permute-start(bf16[128,1024]{1,0:T(8,128)(2,1)} %get-tuple-element.83), channel_id=1, source_target_pairs={{0,1},{1,2},{2,3},{3,0},{4,5},{5,6},{6,7},{7,4},{8,9},{9,10},{10,1... | collective-permute-start | bytes 786440 | tf_op jit(solution)/shard_map/ppermute | solution.py:407
  69.1 9.0 %collective-permute-start.12 = (bf16[128,1024]{1,0:T(8,128)(2,1)}, bf16[128,1024]{1,0:T(8,128)(2,1)S(1)}, u32[]{:S(2)}, u32[]{:S(2)}) collective-permute-start(bf16[128,1024]{1,0:T(8,128)(2,1)} %get-tuple-element.84), channel_id=1, source_target_pairs={{0,3},{1,0},{2,1},{3,2},{4,7},{5,4},{6,5},{7,6},{8,11},{9,8},{10,9... | collective-permute-start | bytes 786440 | tf_op jit(solution)/shard_map/ppermute | solution.py:407
  76.2 1.0 %copy-start.2 = (f32[528,256]{1,0:T(8,128)S(1)}, f32[528,256]{1,0:T(8,128)}, u32[]{:S(2)}) copy-start(f32[528,256]{1,0:T(8,128)} %copy-done.1) | copy-start | bytes 1622020
  78.1 15.7 %all-to-all-start.1 = ((bf16[4,144,256]{2,1,0:T(8,128)(2,1)}), bf16[4,144,256]{2,1,0:T(8,128)(2,1)S(1)}, u32[]{:S(2)}, u32[]{:S(2)}) async-start(bf16[4,144,256]{2,1,0:T(8,128)(2,1)} %collect.1), calls=%async_computation.1 | async-start | bytes 589824 | tf_op jit(solution)/shard_map/all_to_all | solution.py:542
  82.3 13.0 %collective-permute-start.10 = (bf16[128,512]{1,0:T(8,128)(2,1)}, bf16[128,512]{1,0:T(8,128)(2,1)S(1)}, u32[]{:S(2)}, u32[]{:S(2)}) collective-permute-start(bf16[128,512]{1,0:T(8,128)(2,1)} %copy-done.14), channel_id=1, source_target_pairs={{0,2},{1,3},{2,0},{3,1},{4,6},{5,7},{6,4},{7,5},{8,10},{9,11},{10,... | collective-permute-start | bytes 393224 | tf_op jit(solution)/shard_map/ppermute | solution.py:407
  94.6 2.8 %collective-permute-start.13 = (f32[2,512]{1,0:T(2,128)S(1)}, f32[2,512]{1,0:T(2,128)S(1)}, u32[]{:S(2)}, u32[]{:S(2)}) collective-permute-start(f32[2,512]{1,0:T(2,128)S(1)} %get-tuple-element.90), channel_id=1, source_target_pairs={{0,4},{4,0},{8,12},{12,8},{16,20},{20,16},{24,28},{28,24},{1,5},{5... | collective-permute-start | bytes 12296 | tf_op jit(solution)/shard_map/ppermute | solution.py:404
  95.3 0.9 copy-start.10

commit v4 on v2

v4 whole, which is shorter than its diff:
```python
import functools

import jax
import jax.numpy as jnp
from jax import lax
from jax.experimental import pallas as pl
from jax.experimental.pallas import tpu as pltpu
from jax.sharding import PartitionSpec as P

HEAD_DIM = 128
TILE = 128
SPARE = 16
LOG2E = 1.4426950408889634
ENTRY = 4
PARTS = 4
STAT_TERMS = 2
EARLY = 1
HIDING = 3
LAST_DIMS = (((1,), (1,)), ((), ()))
VMEM = pltpu.VMEM
SMEM = pltpu.SMEM
F32 = jnp.float32
BF16 = jnp.bfloat16


def split_float(x, count):
    terms = []
    for _ in range(count):
        terms.append(x.astype(BF16).astype(F32))
        x = x - terms[-1]
    return terms


def head_rows(heads_dev):
    return -(-heads_dev // 8) * 8


def extra_rows(heads_dev):
    return STAT_TERMS * head_rows(heads_dev)


def prepare_kernel(dims, key_ref, value_ref, attn_ref, grads_ref, lse_ref, *rest):
    count_ka, heads, heads_dev, share = dims
    outs, (attn, grad, lse_pad, delta_pad, sems) = rest[:count_ka], rest[count_ka:]
    _, place_ka = places()
    rows8 = head_rows(heads_dev)
    part_heads = heads // PARTS
    rows = pl.ds(pl.multiple_of(place_ka * TILE, TILE), TILE)
    copies = []
    for part in range(PARTS):
        columns = pl.ds(part * part_heads * HEAD_DIM, part_heads * HEAD_DIM)
        copies.append((
            pltpu.make_async_copy(attn_ref.at[:, columns], attn.at[part], sems.at[0, part]),
            pltpu.make_async_copy(grads_ref.at[rows, columns], grad.at[part], sems.at[1, part]),
        ))
        for copy in copies[-1]:
            copy.start()
    for step in range(count_ka):
        target = lax.rem(place_ka + step, count_ka)
        kv_at = pl.ds(pl.multiple_of(target // share * HEAD_DIM, HEAD_DIM), HEAD_DIM)
        outs[step][:TILE, :HEAD_DIM] = key_ref[:, kv_at]
        outs[step][:TILE, HEAD_DIM:] = value_ref[:, kv_at]
    lanes = lax.broadcasted_iota(jnp.int32, (TILE, TILE), 1)
    columns = jnp.zeros((TILE, TILE), F32)
    for part in range(PARTS):
        for copy in copies[part]:
            copy.wait()
        for head in range(part_heads):
            at = pl.ds(head * HEAD_DIM, HEAD_DIM)
            products = grad[part, :, at].astype(F32) * attn[part, :, at].astype(F32)
            total = jnp.sum(products, axis=1, keepdims=True)
            columns = jnp.where(lanes == part * part_heads + head, total, columns)
    delta_pad[...] = jnp.zeros_like(delta_pad)
    lse_pad[...] = jnp.zeros_like(lse_pad)
    delta_pad[:heads, :] = columns.T[:heads, :]
    lse_pad[:heads, :] = lse_ref[...]
    for step in range(count_ka):
        target = lax.rem(place_ka + step, count_ka)
        head_at = pl.ds(target * heads_dev, rows8)
        both = jnp.concatenate([lse_pad[head_at, :], delta_pad[head_at, :]], axis=1)
        outs[step][TILE:, :] = jnp.concatenate(split_float(both, STAT_TERMS), axis=0).astype(BF16)


def own_heads_kernel(queries_ref, grads_ref, out_ref, sems):
    _, place_ka = places()
    width = out_ref.shape[2]
    columns = pl.ds(pl.multiple_of(place_ka * width, HEAD_DIM), width)
    copies = [
        pltpu.make_async_copy(ref.at[:, columns], out_ref.at[number], sems.at[number])
        for number, ref in enumerate((queries_ref, grads_ref))
    ]
    for copy in copies:
        copy.start()
    for copy in copies:
        copy.wait()


def places():
    return lax.axis_index("pb"), lax.axis_index("ka")


def plan_kernel(dims, order_ref, doc_ref, mask_ref, other_ref, own_ref):
    count_chip, count_ka, order = dims
    place_pb, place_ka = places()

    def walk(table, query_pb, key_pb, steps, units):
        def query_step(turn_q, units):
            step_q = jnp.int32(order[0])
            for number, step in enumerate(order):
                step_q = jnp.where(turn_q == number, step, step_q)
            tile_at = lax.rem(place_ka + step_q, count_ka)
            seq_q = order_ref[query_pb * count_ka + tile_at]
            doc_q = doc_ref[seq_q]

            def collect(number, units):
                for step in range(count_ka):
                    stored = (key_pb ^ (2 * number)) * count_ka + lax.rem(
                        place_ka - step + count_ka, count_ka
                    )
                    seq_k = order_ref[stored]
                    live = (mask_ref[seq_q, seq_k] == 1) & (doc_ref[seq_k] == doc_q) & (seq_q >= seq_k)
                    if table is not None:
                        base = ENTRY * (units + 1)
                        table[base] = turn_q
                        table[base + 1] = tile_at
                        table[base + 2] = number * count_ka + step
                        table[base + 3] = jnp.where(seq_q == seq_k, 0, -TILE)
                    units = units + live.astype(jnp.int32)
                return units

            return lax.fori_loop(0, count_chip, collect, units)

        return lax.fori_loop(*steps, query_step, units)

    def close(table, units):
        base = ENTRY * (units + 1)
        table[base] = 0
        table[base + 1] = 0
        table[base + 2] = 0
        table[base + 3] = TILE
        return (units + 1) // 2

    none = jnp.int32(0)
    other = close(other_ref, walk(other_ref, place_pb ^ 1, place_pb, (0, count_ka), none))
    early = walk(own_ref, place_pb, place_pb, (0, EARLY), none)
    total = close(own_ref, walk(own_ref, place_pb, place_pb, (EARLY, count_ka), early))
    partner = (walk(None, place_pb, place_pb ^ 1, (0, count_ka), none) + 1) // 2
    first = jnp.minimum(jnp.maximum(partner - other, (early + 1) // 2), total)
    other_ref[0] = other
    own_ref[0] = first
    own_ref[1] = jnp.minimum(first + HIDING, total)
    own_ref[2] = total


def attention_kernel(dims, *rest):
    count_chip, count_ka, heads_dev, share, stage = dims
    if stage == 0:
        (other_table, own_table, key_gain_ref, value_gain_ref), rest = rest[:4], rest[4:]
        (other_heads, other_stats), rest = rest[:2], rest[2:]
    else:
        own_table, rest = rest[0], rest[1:]
    (own_heads, own_stats), rest = rest[:2], rest[2:]
    if stage != 1:
        blocks, rest = rest[:count_chip], rest[count_chip:]
    if stage == 0:
        (dq_out, dq_sum, keys, values, keys_t, key_sum, value_sum), rest = rest[:7], rest[7:]
    else:
        (keys, values, keys_t, dq_start, key_start, value_start), rest = rest[:6], rest[6:]
        dq_sum, rest = rest[0], rest[1:]
        if stage == 2:
            kv_outs, rest = rest[:count_chip], rest[count_chip:]
        (key_sum, value_sum), rest = rest[:2], rest[2:]
    own_lse, weights_low, dscores_low = rest[:3]
    _, place_ka = places()
    rows8 = head_rows(heads_dev)
    spare = extra_rows(heads_dev)
    score_scale = HEAD_DIM ** -0.5

    if stage == 0:
        kv_at = pl.ds(pl.multiple_of(place_ka // share * HEAD_DIM, HEAD_DIM), HEAD_DIM)
        key_gain = key_gain_ref[:, kv_at]
        value_gain = value_gain_ref[:, kv_at]
        for number in range(count_chip):
            for step in range(count_ka):
                part = pl.ds(step * TILE, TILE)
                local = number * count_ka + step
                key_tile = (blocks[number][part, :HEAD_DIM].astype(F32) * key_gain).astype(BF16)
                value_tile = (blocks[number][part, HEAD_DIM:].astype(F32) * value_gain).astype(BF16)
                keys[local] = key_tile
                values[local] = value_tile
                keys_t[local] = key_tile.T
        key_sum[...] = jnp.zeros_like(key_sum)
        value_sum[...] = jnp.zeros_like(value_sum)
        dq_sum[...] = jnp.zeros_like(dq_sum)
    else:
        key_sum[...] = key_start[...]
        value_sum[...] = value_start[...]
        dq_sum[...] = dq_start[...]

    reach = (lax.broadcasted_iota(jnp.int32, (TILE, TILE), 1)
             - lax.broadcasted_iota(jnp.int32, (TILE, TILE), 0))
    reach = jnp.concatenate([reach, reach], axis=1)

    def run(table, heads_ref, stats_ref, lse_delta, dq_to, first, last):
        for slot in range(count_ka):
            packed = stats_ref[pl.ds(slot * spare, spare), :].astype(F32)
            terms = [packed[term * rows8:(term + 1) * rows8] for term in range(STAT_TERMS)]
            lse_delta[slot] = sum(terms[1:], terms[0])

        def heads_of(kind, tile_at, heads):
            rows = pl.ds(pl.multiple_of(tile_at * TILE, TILE), TILE)
            return jnp.concatenate(
                [heads_ref[kind, rows, pl.ds(head * HEAD_DIM, HEAD_DIM)] for head in heads], axis=0
            )

        def unit_step(at, carry):
            terms = []
            for lane in range(2):
                base = ENTRY * (2 * at + lane + 1)
                turn_q, tile_at, key_at = table[base], table[base + 1], table[base + 2]
                slot = lax.rem(place_ka - tile_at + count_ka, count_ka)
                allowed = reach >= table[base + 3]
                for head in range(0, heads_dev, 2):
                    part = pl.ds(head * HEAD_DIM, 2 * HEAD_DIM)
                    both = (head, head + 1)
                    scores = lax.dot_general(
                        keys[key_at], heads_of(0, tile_at, both), LAST_DIMS, preferred_element_type=F32
                    )
                    dweights = lax.dot_general(
                        values[key_at], heads_of(1, tile_at, both), LAST_DIMS, preferred_element_type=F32
                    )
                    lse_row, delta_row = [
                        jnp.concatenate(
                            [lse_delta[slot, number:number + 1, lanes] for number in both], axis=1
                        )
                        for lanes in (slice(0, TILE), slice(TILE, 2 * TILE))
                    ]
                    weights = jnp.exp2(scores * (score_scale * LOG2E) - lse_row * LOG2E)
                    weights = jnp.where(allowed, weights, 0.0)
                    weights_low[lane, :, part] = weights.astype(BF16)
                    dscores_low[lane, :, part] = (weights * (dweights - delta_row)).astype(BF16)
                every = range(heads_dev)
                terms.append((
                    turn_q,
                    key_at,
                    jnp.dot(weights_low[lane], heads_of(1, tile_at, every), preferred_element_type=F32),
                    jnp.dot(dscores_low[lane], heads_of(0, tile_at, every), preferred_element_type=F32),
                    jnp.dot(keys_t[key_at], dscores_low[lane], preferred_element_type=F32),
                ))
            for turn_q, key_at, value_term, key_term, dq_term in terms:
                value_sum[key_at] += value_term
                key_sum[key_at] += key_term
                dq_to[turn_q] += dq_term
            return carry

        lax.fori_loop(first, last, unit_step, 0)

    if stage == 0:
        other_lse, dq_other = rest[3:]
        dq_other[...] = jnp.zeros_like(dq_other)
        run(other_table, other_heads, other_stats, other_lse, dq_other, 0, other_table[0])
        for turn_q in range(count_ka):
            dq_out[turn_q] = (dq_other[turn_q] * score_scale).astype(BF16)
    first = own_table[stage - 1] if stage else 0
    run(own_table, own_heads, own_stats, own_lse, dq_sum, first, own_table[stage])
    if stage != 2:
        return

    key_gains = jnp.zeros((8, HEAD_DIM), F32)
    value_gains = jnp.zeros((8, HEAD_DIM), F32)
    for number in range(count_chip):
        for step in range(count_ka):
            part = pl.ds(step * TILE, TILE)
            local = number * count_ka + step
            key_total = key_sum[local] * score_scale
            value_total = value_sum[local]
            kv_outs[number][part, :HEAD_DIM] = key_total.astype(kv_outs[number].dtype)
            kv_outs[number][part, HEAD_DIM:] = value_total.astype(kv_outs[number].dtype)
            key_raw = blocks[number][part, :HEAD_DIM].astype(F32)
            value_raw = blocks[number][part, HEAD_DIM:].astype(F32)
            key_gains += jnp.sum((key_total * key_raw).reshape(TILE // 8, 8, HEAD_DIM), axis=0)
            value_gains += jnp.sum((value_total * value_raw).reshape(TILE // 8, 8, HEAD_DIM), axis=0)
    gains = jnp.concatenate([jnp.sum(key_gains, axis=0, keepdims=True),
                             jnp.sum(value_gains, axis=0, keepdims=True)], axis=1)
    packed = pack_gains(gains)
    for number in range(count_chip):
        kv_outs[number][count_ka * TILE:, :] = packed.astype(kv_outs[number].dtype)


def pack_gains(gains):
    rows = lax.broadcasted_iota(jnp.int32, (SPARE, gains.shape[1]), 0)
    high, middle, low = split_float(gains, 3)
    packed = jnp.where(rows == 0, high, jnp.where(rows == 1, middle, low))
    return jnp.where(rows < 3, packed, 0.0)


def add_kernel(first, part_ref, other_ref, *outs):
    for tile, out_ref in enumerate(outs, first):
        own = part_ref[tile] * HEAD_DIM ** -0.5
        out_ref[...] = (own + other_ref[tile].astype(F32)).astype(BF16)


def collect_kernel(dims, key_gain_ref, value_gain_ref, *rest):
    count_chip, count_ka, share = dims
    parts, outs = rest[:count_chip], rest[count_chip:]
    kv_at = pl.ds(pl.multiple_of(places()[1] // share * HEAD_DIM, HEAD_DIM), HEAD_DIM)
    gain = jnp.concatenate([key_gain_ref[:, kv_at], value_gain_ref[:, kv_at]], axis=1)
    for step in range(count_ka):
        rows = pl.ds(step * TILE, TILE)
        total = parts[0][rows, :]
        for number in range(1, count_chip):
            total = total + parts[number][rows, :].astype(F32)
        if share == 1:
            total = total * gain
        outs[step][:TILE, :] = total.astype(outs[step].dtype)
    spare = pl.ds(count_ka * TILE, SPARE)
    total = parts[0][spare, :]
    for number in range(1, count_chip):
        total = total + parts[number][spare, :].astype(F32)
    packed = pack_gains(jnp.sum(total, axis=0, keepdims=True))
    for step in range(count_ka):
        outs[step][TILE:, :] = packed.astype(outs[step].dtype)


def turn_kernel(*refs):
    half = len(refs) // 2
    for source, target in zip(refs[:half], refs[half:]):
        for head in range(source.shape[1] // HEAD_DIM):
            part = pl.ds(head * HEAD_DIM, HEAD_DIM)
            target[:, part] = source[:, part].T


def place_kernel(dims, gains_ref, other_ref, *rest):
    count_ka, heads_dev, pieces = dims
    dq_parts, rest = rest[:len(pieces)], rest[len(pieces):]
    dq_out, key_gain_out, value_gain_out, *turned, sems = rest
    width = heads_dev * HEAD_DIM
    copies, used = [], 0
    for number, ((step, late), piece) in enumerate(zip(pieces, dq_parts)):
        source = lax.rem(places()[1] - step + count_ka, count_ka)
        columns = pl.ds(pl.multiple_of(source * width, HEAD_DIM), width)
        if late:
            turn_kernel(piece, turned[used])
            piece, used = turned[used], used + 1
        copies.append(pltpu.make_async_copy(piece, dq_out.at[:, columns], sems.at[number]))
        copies[-1].start()
    key_gain_out[...] = gains_ref[0:1, :] + other_ref[0:1, :]
    value_gain_out[...] = gains_ref[1:2, :] + other_ref[1:2, :]
    for copy in copies:
        copy.wait()


def finish_kernel(dims, key_gain_ref, value_gain_ref, *rest):
    count_ka, share = dims
    pieces, rest = rest[:count_ka], rest[count_ka:]
    dk_out, dv_out, gains_out, sums = rest
    _, place_ka = places()
    sums[...] = jnp.zeros_like(sums)
    for step in range(count_ka):
        source = lax.rem(place_ka + step, count_ka)
        sums[source // share] += pieces[step][...].astype(F32)
    for head in range(count_ka // share):
        part = pl.ds(head * HEAD_DIM, HEAD_DIM)
        key_total = sums[head, :TILE, :HEAD_DIM]
        value_total = sums[head, :TILE, HEAD_DIM:]
        if share > 1:
            key_total = key_total * key_gain_ref[:, part]
            value_total = value_total * value_gain_ref[:, part]
        dk_out[:, part] = key_total.astype(BF16)
        dv_out[:, part] = value_total.astype(BF16)
        gains = jnp.sum(sums[head, TILE:, :], axis=0, keepdims=True)
        gains_out[0:1, part] = gains[:, :HEAD_DIM]
        gains_out[1:2, part] = gains[:, HEAD_DIM:]


def in_vmem(count):
    return [pl.BlockSpec(memory_space=VMEM)] * count


def in_smem(count):
    return [pl.BlockSpec(memory_space=SMEM)] * count


def anywhere(count):
    return [pl.BlockSpec(memory_space=pl.ANY)] * count


def params(mib):
    return pltpu.CompilerParams(vmem_limit_bytes=mib * 1024 * 1024)


def shards(
    queries,
    key_rows,
    values,
    attn_out,
    grad_out,
    log_sums,
    key_gain,
    value_gain,
    doc_ids,
    tile_mask,
    block_order,
):
    count_pb = lax.axis_size("pb")
    count_ka = lax.axis_size("ka")
    rows_dev = key_rows.shape[0]
    query_rows = queries.shape[0]
    heads = log_sums.shape[0]
    feat_width = queries.shape[1]
    kv_heads = key_rows.shape[1] // HEAD_DIM
    heads_dev = heads // count_ka
    share = count_ka // kv_heads
    assert rows_dev == TILE and share * kv_heads == count_ka and count_pb & (count_pb - 1) == 0
    width = heads_dev * HEAD_DIM
    key_gain = key_gain.reshape(1, -1)
    value_gain = value_gain.reshape(1, -1)

    spare = extra_rows(heads_dev)
    count_chip = count_pb // 2

    def swap(array, number):
        return lax.ppermute(array, "pb", [(at, at ^ number) for at in range(count_pb)])

    def turn(array, step):
        return lax.ppermute(array, "ka", [(at, (at + step) % count_ka) for at in range(count_ka)])

    sends = pl.pallas_call(
        functools.partial(prepare_kernel, (count_ka, heads, heads_dev, share)),
        in_specs=in_vmem(2) + anywhere(2) + in_vmem(1),
        out_specs=in_vmem(count_ka),
        out_shape=[jax.ShapeDtypeStruct((TILE + spare, 2 * HEAD_DIM), BF16)] * count_ka,
        scratch_shapes=[VMEM((PARTS, TILE, feat_width // PARTS), BF16)] * 2
        + [VMEM((heads + 8, TILE), F32)] * 2
        + [pltpu.SemaphoreType.DMA((2, PARTS))],
        compiler_params=params(57),
        name="prepare",
    )(key_rows, values, attn_out, grad_out, log_sums)
    messages = [sends[0]] + [turn(sends[step], step) for step in range(1, count_ka)]

    later_queries, _ = lax.optimization_barrier((queries, sends[0]))
    own_queries = pl.pallas_call(
        own_heads_kernel,
        in_specs=anywhere(2),
        out_specs=in_vmem(1)[0],
        out_shape=jax.ShapeDtypeStruct((2, query_rows, width), BF16),
        scratch_shapes=[pltpu.SemaphoreType.DMA((2,))],
        compiler_params=params(48),
        cost_estimate=pl.CostEstimate(flops=0, bytes_accessed=8 * query_rows * width, transcendentals=0),
        name="own_heads",
    )(later_queries, grad_out)
    messages, own_queries = lax.optimization_barrier((messages, own_queries))
    other_queries = swap(own_queries, 1)
    own_block = jnp.concatenate([message[:TILE] for message in messages], axis=0)
    own_stats = jnp.concatenate([message[TILE:] for message in messages], axis=0)
    blocks = [own_block] + [swap(own_block, 2 * number) for number in range(1, count_chip)]
    other_stats = swap(own_stats, 1)
    later_order, _ = lax.optimization_barrier((block_order, own_block))

    key_tiles = count_chip * count_ka
    sum_shape = jax.ShapeDtypeStruct((key_tiles, TILE, HEAD_DIM), F32)
    key_shape = jax.ShapeDtypeStruct((key_tiles, TILE, HEAD_DIM), BF16)
    kv_shape = (query_rows + SPARE, 2 * HEAD_DIM)
    half = count_ka // 2
    late = tuple(step for step in range(count_ka) if step != half)
    order = (half,) + late
    table_shape = jax.ShapeDtypeStruct((ENTRY * (2 + count_ka * key_tiles),), jnp.int32)
    other_table, own_table = pl.pallas_call(
        functools.partial(plan_kernel, (count_chip, count_ka, order)),
        in_specs=in_smem(3),
        out_specs=in_smem(2),
        out_shape=[table_shape] * 2,
        cost_estimate=pl.CostEstimate(flops=0, bytes_accessed=1 << 22, transcendentals=0),
        name="plan",
    )(later_order, doc_ids, tile_mask)

    def attend(stage, tables, outs, scratch, *operands):
        return pl.pallas_call(
            functools.partial(attention_kernel, (count_chip, count_ka, heads_dev, share, stage)),
            in_specs=in_smem(len(tables)) + in_vmem(len(operands)),
            out_specs=in_vmem(len(outs)),
            out_shape=outs,
            scratch_shapes=scratch[0] + [
                VMEM((count_ka, head_rows(heads_dev), 2 * TILE), F32),
                VMEM((2, TILE, width), BF16),
                VMEM((2, TILE, width), BF16),
            ] + scratch[1],
            compiler_params=params(20 + key_tiles // 2),
            cost_estimate=pl.CostEstimate(
                flops=5 * count_ka * key_tiles * TILE * TILE * width if stage < 2 else 0,
                bytes_accessed=1 << 20 if stage < 2 else 0,
                transcendentals=0,
            ),
            name=("attention_first", "attention_second", "attention_third")[stage],
        )(*tables, *operands)

    dq_shape = (count_ka, HEAD_DIM, width)
    dq_sums = jax.ShapeDtypeStruct(dq_shape, F32)

    def add(part, other, first, count):
        return pl.pallas_call(
            functools.partial(add_kernel, first),
            in_specs=in_vmem(2),
            out_specs=in_vmem(count),
            out_shape=[jax.ShapeDtypeStruct((HEAD_DIM, width), BF16)] * count,
            compiler_params=params(4 * count_ka),
            name="add_queries",
        )(part, other)

    dq_other, dq_own, *state = attend(
        0, (other_table, own_table),
        [jax.ShapeDtypeStruct(dq_shape, BF16), dq_sums] + [key_shape] * 3 + [sum_shape] * 2,
        ([], [VMEM((count_ka, head_rows(heads_dev), 2 * TILE), F32), VMEM(dq_shape, F32)]),
        key_gain, value_gain, other_queries, other_stats, own_queries, own_stats, *blocks,
    )
    keys, sums = state[:3], state[3:]
    dq_back = swap(dq_other, 1)
    dq_own, *sums = attend(
        1, (own_table,), [dq_sums] + [sum_shape] * 2, ([], []), own_queries, own_stats, *keys, dq_own, *sums
    )
    dq_parts = [None] * count_ka
    dq_first, = add(dq_own, dq_back, 0, 1)
    dq_parts[half] = turn(dq_first, half)
    late_stats, _ = lax.optimization_barrier((own_stats, dq_first))
    dq_own, *kv_own = attend(
        2, (own_table,),
        [dq_sums, jax.ShapeDtypeStruct(kv_shape, F32)]
        + [jax.ShapeDtypeStruct(kv_shape, BF16)] * (count_chip - 1),
        ([VMEM(sum_shape.shape, F32)] * 2, []),
        own_queries, late_stats, *blocks, *keys, dq_own, *sums,
    )
    dq_own, dq_parts[half] = lax.optimization_barrier((dq_own, dq_parts[half]))
    for step, tile in zip(late, add(dq_own, dq_back, EARLY, len(late))):
        dq_parts[step] = turn(tile, step) if step else tile
    kv_parts = [kv_own[0]] + [swap(kv_own[number], 2 * number) for number in range(1, count_chip)]

    piece_type = BF16 if share == 1 else F32
    piece_shape = (TILE + SPARE, 2 * HEAD_DIM)
    totals = pl.pallas_call(
        functools.partial(collect_kernel, (count_chip, count_ka, share)),
        in_specs=in_vmem(2 + count_chip),
        out_specs=in_vmem(count_ka),
        out_shape=[jax.ShapeDtypeStruct(piece_shape, piece_type)] * count_ka,
        compiler_params=params(24),
        name="collect",
    )(key_gain, value_gain, *kv_parts)
    pieces = [totals[0]] + [turn(totals[step], -step) for step in range(1, count_ka)]

    grad_keys, grad_values, gains = pl.pallas_call(
        functools.partial(finish_kernel, (count_ka, share)),
        in_specs=in_vmem(2 + count_ka),
        out_specs=in_vmem(3),
        out_shape=[
            jax.ShapeDtypeStruct(key_rows.shape, BF16),
            jax.ShapeDtypeStruct(key_rows.shape, BF16),
            jax.ShapeDtypeStruct((2, key_rows.shape[1]), F32),
        ],
        scratch_shapes=[VMEM((kv_heads, TILE + SPARE, 2 * HEAD_DIM), F32)],
        compiler_params=params(16),
        name="finish",
    )(key_gain, value_gain, *pieces)
    first = [dq_parts[0], dq_parts[half]]
    turned = pl.pallas_call(
        turn_kernel,
        in_specs=in_vmem(len(first)),
        out_specs=in_vmem(len(first)),
        out_shape=[jax.ShapeDtypeStruct(part.shape, BF16) for part in first],
        compiler_params=params(8),
        cost_estimate=pl.CostEstimate(flops=0, bytes_accessed=1 << 22, transcendentals=0),
        name="turn_queries",
    )(*first)
    later = [step for step in late if step]
    where = ((0, False), (half, False)) + tuple((step, True) for step in later)
    grad_queries, grad_key_gain, grad_value_gain = pl.pallas_call(
        functools.partial(place_kernel, (count_ka, heads_dev, where)),
        in_specs=in_vmem(2 + len(where)),
        out_specs=anywhere(1) + in_vmem(2),
        out_shape=[jax.ShapeDtypeStruct((rows_dev, feat_width), BF16)]
        + [jax.ShapeDtypeStruct(key_gain.shape, F32)] * 2,
        scratch_shapes=[VMEM((TILE, width), BF16)] * len(later) + [pltpu.SemaphoreType.DMA((len(where),))],
        compiler_params=params(16),
        cost_estimate=pl.CostEstimate(flops=0, bytes_accessed=4 * rows_dev * feat_width, transcendentals=0),
        name="place_queries",
    )(gains, swap(gains, 1), *turned, *[dq_parts[step] for step in later])
    return grad_queries, grad_keys, grad_values, grad_key_gain.reshape(-1), grad_value_gain.reshape(-1)


def solution(mesh):
    placed = (
        P("pb", None),
        P(("pb", "ka"), None),
        P(("pb", "ka"), None),
        P(("pb", "ka"), None),
        P("pb", None),
        P(None, ("pb", "ka")),
        P(),
        P(),
        P(),
        P(),
        P(),
    )
    return jax.shard_map(
        shards,
        mesh=mesh,
        in_specs=placed,
        out_specs=(P(("pb", "ka"), None), P(("pb", "ka"), None), P(("pb", "ka"), None), P(), P()),
        check_vma=False,
    )
```

time: 88.7 us -> 87.8 us (0.990)
  waiting for transfers between devices: 26.5 us -> 30.2 us
  Pallas kernels: 29.8 us -> 27.4 us
  starting transfers between devices: 28.9 us -> 26.8 us
    ppermute x10 -> x9, waiting for transfers between devices: 9.98 us -> 20.6 us  [turn(): lax.ppermute(array, 'ka', [(at, (at + step) % count_ka) for at in range(c...]
    ppermute x11 -> x10, waiting for transfers between devices: 16.5 us -> 9.6 us  [swap(): lax.ppermute(array, 'pb', [(at, at ^ number) for at in range(count_pb)])]
    pallas_call x8 -> x7, Pallas kernels: 23.9 us -> 20.9 us  [the longest x3 15.4 us: attend(): pl.pallas_call(functools.partial(attention_kernel, (count_chip, count_ka,...]
    ppermute x11 -> x10, starting transfers between devices: 9.15 us -> 7.27 us  [swap(): lax.ppermute(array, 'pb', [(at, at ^ number) for at in range(count_pb)])]
    ppermute x10 -> x9, starting transfers between devices: 19.8 us -> 19.5 us  [turn(): lax.ppermute(array, 'ka', [(at, (at + step) % count_ka) for at in range(c...]
  transfers between devices with their start and end apart: 21 -> 19, of which waited for: 11 -> 10; matrix products, arithmetic and copies ran while one was open for 0% -> 0% of each run, Pallas kernels for 28% -> 14%
where the time goes in v4:
time: 87.8 us; the launch traced here: 86.6 us
  waiting for transfers between devices  30.2 us (34%)
  Pallas kernels  27.4 us (31%)
  starting transfers between devices  26.8 us (31%)
  local copies, waits for them, and re-layouts  1.4 us (2%)
    ppermute x9, waiting for transfers between devices, turn(): lax.ppermute(array, 'ka', [(at, (at + step) % count_ka) for at in range(c...  20.6 us
    ppermute x9, starting transfers between devices, turn(): lax.ppermute(array, 'ka', [(at, (at + step) % count_ka) for at in range(c...  19.5 us
    pallas_call x3, Pallas kernels, attend(): pl.pallas_call(functools.partial(attention_kernel, (count_chip, count_ka,...  15.4 us
    ppermute x10, waiting for transfers between devices, swap(): lax.ppermute(array, 'pb', [(at, at ^ number) for at in range(count_pb)])  9.6 us
    ppermute x10, starting transfers between devices, swap(): lax.ppermute(array, 'pb', [(at, at ^ number) for at in range(count_pb)])  7.27 us
    pallas_call x1, Pallas kernels, shards(): pl.pallas_call(functools.partial(prepare_kernel, (count_ka, heads, heads_...  3.67 us
    pallas_call x1, Pallas kernels, shards(): pl.pallas_call(functools.partial(plan_kernel, (count_chip, count_ka, orde...  3.52 us
  transfers between devices with their start and end apart: 19, of which 10 were waited for; matrix products, arithmetic and copies ran while one was open for 0% of the time, Pallas kernels for 14%

profile of v4, /device:TPU:0, one launch (start us, length us, event | category | flops | bytes accessed | tf_op | source)
XLA Modules:
  0.0 86.6 jit_solution(3803746036386041668)
XLA Ops:
  0.6 3.7 %prepare.1 = (bf16[144,256]{1,0:T(8,128)(2,1)}, bf16[144,256]{1,0:T(8,128)(2,1)}, bf16[144,256]{1,0:T(8,128)(2,1)}, bf16[144,256]{1,0:T(8,128)(2,1)}) custom-call(bf16[128,512]{1,0:T(8,128)(2,1)} %key_ref.1, bf16[128,512]{1,0:T(8,128)(2,1)} %value_ref.1, bf16[128,4096]{1,0:T(8,128)(2,1)} %attn_ref.1, bf16[512,4096]{1,0:T(8,128)(2,1)} %grads_ref.3, ...), custom_call_target="tpu_custom_call" | custom-call | tf_op jit(solution)/shard_map/prepare/pallas_call | solution.py:428
  4.3 3.1 %collective-permute-start = (bf16[144,256]{1,0:T(8,128)(2,1)}, bf16[144,256]{1,0:T(8,128)(2,1)S(1)}, u32[]{:S(2)}, u32[]{:S(2)}) collective-permute-start(bf16[144,256]{1,0:T(8,128)(2,1)} %get-tuple-element.52), channel_id=1, source_target_pairs={{0,1},{1,2},{2,3},{3,0},{4,5},{5,6},{6,7},{7,4},{8,9},{9,10},{10,1... | collective-permute-start | bytes 221192 | tf_op jit(solution)/shard_map/ppermute | solution.py:426
  7.4 2.6 %collective-permute-start.1 = (bf16[144,256]{1,0:T(8,128)(2,1)}, bf16[144,256]{1,0:T(8,128)(2,1)S(1)}, u32[]{:S(2)}, u32[]{:S(2)}) collective-permute-start(bf16[144,256]{1,0:T(8,128)(2,1)} %get-tuple-element.53), channel_id=1, source_target_pairs={{0,2},{1,3},{2,0},{3,1},{4,6},{5,7},{6,4},{7,5},{8,10},{9,11},{10,... | collective-permute-start | bytes 221192 | tf_op jit(solution)/shard_map/ppermute | solution.py:426
  10.0 1.3 %collective-permute-start.2 = (bf16[144,256]{1,0:T(8,128)(2,1)}, bf16[144,256]{1,0:T(8,128)(2,1)S(1)}, u32[]{:S(2)}, u32[]{:S(2)}) collective-permute-start(bf16[144,256]{1,0:T(8,128)(2,1)} %get-tuple-element.54), channel_id=1, source_target_pairs={{0,3},{1,0},{2,1},{3,2},{4,7},{5,4},{6,5},{7,6},{8,11},{9,8},{10,9... | collective-permute-start | bytes 221192 | tf_op jit(solution)/shard_map/ppermute | solution.py:426
  11.3 0.0 copy-start.4
  11.3 0.0 copy-start
  11.3 0.0 copy-start.1
  11.3 1.6 %own_heads.1.rest_6_.rest_1_ = bf16[2,512,1024]{2,1,0:T(8,128)(2,1)S(1)} custom-call(bf16[512,4096]{1,0:T(8,128)(2,1)} %queries_ref, bf16[512,4096]{1,0:T(8,128)(2,1)} %grads_ref.3), custom_call_target="tpu_custom_call" | custom-call | bytes 4194304 | tf_op jit(solution)/shard_map/own_heads/pallas_call | solution.py:442
  12.9 0.0 collective-permute-done
  12.9 2.2 %collective-permute-done.1 = bf16[144,256]{1,0:T(8,128)(2,1)S(1)} collective-permute-done((bf16[144,256]{1,0:T(8,128)(2,1)}, bf16[144,256]{1,0:T(8,128)(2,1)S(1)}, u32[]{:S(2)}, u32[]{:S(2)}) %collective-permute-start.1) | collective-permute-done | bytes 73760 | tf_op jit(solution)/shard_map/ppermute | solution.py:426
  15.1 0.2 collective-permute-done.2
  15.4 0.0 collective-permute-start.3
  15.4 0.0 copy-done.4
  15.5 2.5 %collective-permute-start.7 = (bf16[512,256]{1,0:T(8,128)(2,1)S(1)}, bf16[512,256]{1,0:T(8,128)(2,1)S(1)}, u32[]{:S(2)}, u32[]{:S(2)}) collective-permute-start(bf16[512,256]{1,0:T(8,128)(2,1)S(1)} %pad_maximum_fusion.rest_8_.rest_3_), channel_id=1, source_target_pairs={{0,24},{4,28},{8,16},{12,20},{16,8},{20,12},{24,0},{28,4},{1,25},{... | collective-permute-start | bytes 786440 | tf_op jit(solution)/shard_map/ppermute | solution.py:423
  18.0 0.5 collective-permute-start.6
  18.5 0.5 collective-permute-start.5
  19.0 0.1 collective-permute-start.4
  19.1 3.5 %plan.1 = (s32[264]{0:T(512)}, s32[264]{0:T(512)}) custom-call(s32[32]{0:T(128)} %order_ref, s32[32]{0:T(128)} %doc_ref.1, s32[32,32]{1,0:T(8,128)} %mask_ref.1), custom_call_target="tpu_custom_call" | custom-call | bytes 4194304 | tf_op jit(solution)/shard_map/plan/pallas_call | solution.py:468
  22.6 0.0 collective-permute-done.4.rest_5_
  22.7 2.9 %collective-permute-done.7.rest_11_.rest_6_ = bf16[512,256]{1,0:T(8,128)(2,1)S(1)} collective-permute-done((bf16[512,256]{1,0:T(8,128)(2,1)S(1)}, bf16[512,256]{1,0:T(8,128)(2,1)S(1)}, u32[]{:S(2)}, u32[]{:S(2)}) %collective-permute-start.7) | collective-permute-done | bytes 262176 | tf_op jit(solution)/shard_map/ppermute | solution.py:423
  25.6 5.2 %collective-permute-done.6.rest_10_.rest_5_ = bf16[512,256]{1,0:T(8,128)(2,1)S(1)} collective-permute-done((bf16[512,256]{1,0:T(8,128)(2,1)S(1)}, bf16[512,256]{1,0:T(8,128)(2,1)S(1)}, u32[]{:S(2)}, u32[]{:S(2)}) %collective-permute-start.6) | collective-permute-done | bytes 262176 | tf_op jit(solution)/shard_map/ppermute | solution.py:423
  30.8 0.1 collective-permute-done.5.rest_9_.rest_4_
  30.9 0.0 collective-permute-done.3.rest_4_
  30.9 0.0 copy-done
  30.9 0.0 copy-done.1
  30.9 0.0 copy-start.2
  30.9 0.7 copy-done.2
  31.6 0.0 copy-start.3
  31.6 0.7 copy-done.3
  32.2 9.4 %attention_first.1 = (bf16[4,128,1024]{2,1,0:T(8,128)(2,1)S(1)}, f32[4,128,1024]{2,1,0:T(8,128)S(1)}, bf16[16,128,128]{2,1,0:T(8,128)(2,1)S(1)}, bf16[16,128,128...) custom-call(s32[264]{0:T(512)S(1)} %copy-done.3, ...), custom_call_target="tpu_custom_call" | custom-call | flops 5368709120 | bytes 1048576 | tf_op jit(solution)/shard_map/attention_first/pallas_call | solution.py:478
  41.7 0.1 collective-permute-start.8
  41.7 3.9 %attention_second.1 = (f32[4,128,1024]{2,1,0:T(8,128)S(1)}, f32[16,128,128]{2,1,0:T(8,128)S(1)}, f32[16,128,128]{2,1,0:T(8,128)S(1)}) custom-call(s32[264]{0:T(512)S(1)} %copy-done.2, bf16[2,512,1024]{2,1,0:T(8,128)(2,1)S(1)} %own_heads.1.rest_6_.rest_1_, bf16[64,256]{1,0:T(8,128)(2,1)S(1)} %pad_maximum_fusion.1.rest_7_.rest_2_, ...), custom_call_target="tpu_custom_call" | custom-call | flops 5368709120 | bytes 1048576 | tf_op jit(solution)/shard_map/attention_second/pallas_call | solution.py:478
  45.6 0.0 collective-permute-done.8.other_ref
  45.6 0.1 add_queries.2
  45.7 2.6 %collective-permute-start.16 = (bf16[128,1024]{1,0:T(8,128)(2,1)S(1)}, bf16[128,1024]{1,0:T(8,128)(2,1)S(1)}, u32[]{:S(2)}, u32[]{:S(2)}) collective-permute-start(bf16[128,1024]{1,0:T(8,128)(2,1)S(1)} %add_queries.2), channel_id=1, source_target_pairs={{0,2},{1,3},{2,0},{3,1},{4,6},{5,7},{6,4},{7,5},{8,10},{9,11},{10,... | collective-permute-start | bytes 786440 | tf_op jit(solution)/shard_map/ppermute | solution.py:426
  48.3 2.1 %attention_third.1 = (f32[4,128,1024]{2,1,0:T(8,128)S(1)}, f32[528,256]{1,0:T(8,128)S(1)}, bf16[528,256]{1,0:T(8,128)(2,1)S(1)}, bf16[528,256]{1,0:T(8,128)(2,1)S(1)}, bf16[528,256]{1,0:T(8,128)(2,1)S(1)}) custom-call(s32[264]{0:T(512)S(1)} %copy-done.2, bf16[2,512,1024]{2,1,0:T(8,128)(2,1)S(1)} %own_heads.1.rest_6_.rest_1_, ...), custom_call_target="tpu_custom_call" | custom-call | tf_op jit(solution)/shard_map/attention_third/pallas_call | solution.py:478
  50.4 1.5 %collective-permute-start.9 = (bf16[528,256]{1,0:T(8,128)(2,1)S(1)}, bf16[528,256]{1,0:T(8,128)(2,1)S(1)}, u32[]{:S(2)}, u32[]{:S(2)}) collective-permute-start(bf16[528,256]{1,0:T(8,128)(2,1)S(1)} %get-tuple-element.76), channel_id=1, source_target_pairs={{0,8},{4,12},{8,0},{12,4},{16,24},{20,28},{24,16},{28,20},{1,9},{5... | collective-permute-start | bytes 811016 | tf_op jit(solution)/shard_map/ppermute | solution.py:423
  52.0 0.2 collective-permute-start.10
  52.2 1.8 %collective-permute-start.11 = (bf16[528,256]{1,0:T(8,128)(2,1)S(1)}, bf16[528,256]{1,0:T(8,128)(2,1)S(1)}, u32[]{:S(2)}, u32[]{:S(2)}) collective-permute-start(bf16[528,256]{1,0:T(8,128)(2,1)S(1)} %get-tuple-element.78), channel_id=1, source_target_pairs={{0,24},{4,28},{8,16},{12,20},{16,8},{20,12},{24,0},{28,4},{1,25},{... | collective-permute-start | bytes 811016 | tf_op jit(solution)/shard_map/ppermute | solution.py:423
  54.0 7.0 %collective-permute-done.16.refs_1_ = bf16[128,1024]{1,0:T(8,128)(2,1)S(1)} collective-permute-done((bf16[128,1024]{1,0:T(8,128)(2,1)S(1)}, bf16[128,1024]{1,0:T(8,128)(2,1)S(1)}, u32[]{:S(2)}, u32[]{:S(2)}) %collective-permute-start.16) | collective-permute-done | bytes 262176 | tf_op jit(solution)/shard_map/ppermute | solution.py:426
  61.0 0.2 add_queries.3
  61.2 0.4 collective-permute-start.17
  61.7 3.4 %collective-permute-start.18 = (bf16[128,1024]{1,0:T(8,128)(2,1)S(1)}, bf16[128,1024]{1,0:T(8,128)(2,1)S(1)}, u32[]{:S(2)}, u32[]{:S(2)}) collective-permute-start(bf16[128,1024]{1,0:T(8,128)(2,1)S(1)} %get-tuple-element.91), channel_id=1, source_target_pairs={{0,3},{1,0},{2,1},{3,2},{4,7},{5,4},{6,5},{7,6},{8,11},{9,8},{10,9... | collective-permute-start | bytes 786440 | tf_op jit(solution)/shard_map/ppermute | solution.py:426
  65.1 0.0 collective-permute-done.9.rest_1_
  65.1 0.4 collective-permute-done.10.rest_2_
  65.5 0.0 collective-permute-done.11.rest_3_
  65.5 0.2 collect.1
  65.7 5.3 %collective-permute-start.12 = (bf16[144,256]{1,0:T(8,128)(2,1)S(1)}, bf16[144,256]{1,0:T(8,128)(2,1)S(1)}, u32[]{:S(2)}, u32[]{:S(2)}) collective-permute-start(bf16[144,256]{1,0:T(8,128)(2,1)S(1)} %get-tuple-element.80), channel_id=1, source_target_pairs={{0,3},{1,0},{2,1},{3,2},{4,7},{5,4},{6,5},{7,6},{8,11},{9,8},{10,9... | collective-permute-start | bytes 221192 | tf_op jit(solution)/shard_map/ppermute | solution.py:426
  71.0 0.0 collective-permute-start.13
  71.0 0.8 collective-permute-start.14
  71.7 4.9 %collective-permute-done.12.rest_1_ = bf16[144,256]{1,0:T(8,128)(2,1)S(1)} collective-permute-done((bf16[144,256]{1,0:T(8,128)(2,1)S(1)}, bf16[144,256]{1,0:T(8,128)(2,1)S(1)}, u32[]{:S(2)}, u32[]{:S(2)}) %collective-permute-start.12) | collective-permute-done | bytes 73760 | tf_op jit(solution)/shard_map/ppermute | solution.py:426
  76.6 6.4 %collective-permute-done.13.rest_2_ = bf16[144,256]{1,0:T(8,128)(2,1)S(1)} collective-permute-done((bf16[144,256]{1,0:T(8,128)(2,1)S(1)}, bf16[144,256]{1,0:T(8,128)(2,1)S(1)}, u32[]{:S(2)}, u32[]{:S(2)}) %collective-permute-start.13) | collective-permute-done | bytes 73760 | tf_op jit(solution)/shard_map/ppermute | solution.py:426
  82.9 0.0 collective-permute-done.14.rest_3_
  82.9 0.8 finish.1
  83.8 0.0 collective-permute-start.15
  83.8 0.2 turn_queries.1
  84.0 1.0 %collective-permute-done.15.other_ref = f32[2,512]{1,0:T(2,128)S(1)} collective-permute-done((f32[2,512]{1,0:T(2,128)S(1)}, f32[2,512]{1,0:T(2,128)S(1)}, u32[]{:S(2)}, u32[]{:S(2)}) %collective-permute-start.15) | collective-permute-done | bytes 4128 | tf_op jit(solution)/shard_map/ppermute | solution.py:423
  84.9 0.0 collective-permute-done.17.rest_2_
  85.0 0.0 collective-permute-done.18.rest_3_
  85.0 1.7 %place_queries.1 = (bf16[128,4096]{1,0:T(8,128)(2,1)}, f32[1,512]{1,0:T(1,128)}, f32[1,512]{1,0:T(1,128)}) custom-call(f32[2,512]{1,0:T(2,128)S(1)} %get-tuple-element.83.gains_ref, f32[2,512]{1,0:T(2,128)S(1)} %collective-permute-done.15.other_ref, bf16[128,1024]{1,0:T(8,128)(2,1)S(1)} %get-tuple-element.88.rest_0_, ...), custom_call_target="tpu_custom_call" | custom-call | bytes 2097152 | tf_op jit(solution)/shard_map/place_queries/pallas_call | solution.py:574
  (10 shorter events, 0.1 us)
Async XLA Ops:
  4.3 8.6 %collective-permute-start = (bf16[144,256]{1,0:T(8,128)(2,1)}, bf16[144,256]{1,0:T(8,128)(2,1)S(1)}, u32[]{:S(2)}, u32[]{:S(2)}) collective-permute-start(bf16[144,256]{1,0:T(8,128)(2,1)} %get-tuple-element.52), channel_id=1, source_target_pairs={{0,1},{1,2},{2,3},{3,0},{4,5},{5,6},{6,7},{7,4},{8,9},{9,10},{10,1... | collective-permute-start | bytes 221192 | tf_op jit(solution)/shard_map/ppermute | solution.py:426
  7.4 7.8 %collective-permute-start.1 = (bf16[144,256]{1,0:T(8,128)(2,1)}, bf16[144,256]{1,0:T(8,128)(2,1)S(1)}, u32[]{:S(2)}, u32[]{:S(2)}) collective-permute-start(bf16[144,256]{1,0:T(8,128)(2,1)} %get-tuple-element.53), channel_id=1, source_target_pairs={{0,2},{1,3},{2,0},{3,1},{4,6},{5,7},{6,4},{7,5},{8,10},{9,11},{10,... | collective-permute-start | bytes 221192 | tf_op jit(solution)/shard_map/ppermute | solution.py:426
  10.0 5.4 %collective-permute-start.2 = (bf16[144,256]{1,0:T(8,128)(2,1)}, bf16[144,256]{1,0:T(8,128)(2,1)S(1)}, u32[]{:S(2)}, u32[]{:S(2)}) collective-permute-start(bf16[144,256]{1,0:T(8,128)(2,1)} %get-tuple-element.54), channel_id=1, source_target_pairs={{0,3},{1,0},{2,1},{3,2},{4,7},{5,4},{6,5},{7,6},{8,11},{9,8},{10,9... | collective-permute-start | bytes 221192 | tf_op jit(solution)/shard_map/ppermute | solution.py:426
  11.3 4.0 %copy-start.4 = (bf16[144,256]{1,0:T(8,128)(2,1)S(1)}, bf16[144,256]{1,0:T(8,128)(2,1)}, u32[]{:S(2)}) copy-start(bf16[144,256]{1,0:T(8,128)(2,1)} %get-tuple-element.56) | copy-start | bytes 221188
  11.3 19.5 %copy-start = (f32[512]{0:T(512)S(1)}, f32[512]{0:T(512)}, u32[]{:S(2)}) copy-start(f32[512]{0:T(512)} %param.17) | copy-start | bytes 6148
  11.3 19.5 %copy-start.1 = (f32[512]{0:T(512)S(1)}, f32[512]{0:T(512)}, u32[]{:S(2)}) copy-start(f32[512]{0:T(512)} %param.18) | copy-start | bytes 6148
  15.4 15.5 %collective-permute-start.3 = (bf16[2,512,1024]{2,1,0:T(8,128)(2,1)S(1)}, bf16[2,512,1024]{2,1,0:T(8,128)(2,1)}, u32[]{:S(2)}, u32[]{:S(2)}) collective-permute-start(bf16[2,512,1024]{2,1,0:T(8,128)(2,1)S(1)} %own_heads.1.rest_6_.rest_1_), channel_id=1, source_target_pairs={{0,4},{4,0},{8,12},{12,8},{16,20},{20,16},{24,28},{28,24},{1,5},{5... | collective-permute-start | bytes 6291464 | tf_op jit(solution)/shard_map/ppermute | solution.py:423
  15.5 10.1 %collective-permute-start.7 = (bf16[512,256]{1,0:T(8,128)(2,1)S(1)}, bf16[512,256]{1,0:T(8,128)(2,1)S(1)}, u32[]{:S(2)}, u32[]{:S(2)}) collective-permute-start(bf16[512,256]{1,0:T(8,128)(2,1)S(1)} %pad_maximum_fusion.rest_8_.rest_3_), channel_id=1, source_target_pairs={{0,24},{4,28},{8,16},{12,20},{16,8},{20,12},{24,0},{28,4},{1,25},{... | collective-permute-start | bytes 786440 | tf_op jit(solution)/shard_map/ppermute | solution.py:423
  18.0 12.8 %collective-permute-start.6 = (bf16[512,256]{1,0:T(8,128)(2,1)S(1)}, bf16[512,256]{1,0:T(8,128)(2,1)S(1)}, u32[]{:S(2)}, u32[]{:S(2)}) collective-permute-start(bf16[512,256]{1,0:T(8,128)(2,1)S(1)} %pad_maximum_fusion.rest_8_.rest_3_), channel_id=1, source_target_pairs={{0,16},{4,20},{8,24},{12,28},{16,0},{20,4},{24,8},{28,12},{1,17},{... | collective-permute-start | bytes 786440 | tf_op jit(solution)/shard_map/ppermute | solution.py:423
  18.5 12.4 %collective-permute-start.5 = (bf16[512,256]{1,0:T(8,128)(2,1)S(1)}, bf16[512,256]{1,0:T(8,128)(2,1)S(1)}, u32[]{:S(2)}, u32[]{:S(2)}) collective-permute-start(bf16[512,256]{1,0:T(8,128)(2,1)S(1)} %pad_maximum_fusion.rest_8_.rest_3_), channel_id=1, source_target_pairs={{0,8},{4,12},{8,0},{12,4},{16,24},{20,28},{24,16},{28,20},{1,9},{5... | collective-permute-start | bytes 786440 | tf_op jit(solution)/shard_map/ppermute | solution.py:423
  19.0 3.6 %collective-permute-start.4 = (bf16[64,256]{1,0:T(8,128)(2,1)S(1)}, bf16[64,256]{1,0:T(8,128)(2,1)S(1)}, u32[]{:S(2)}, u32[]{:S(2)}) collective-permute-start(bf16[64,256]{1,0:T(8,128)(2,1)S(1)} %pad_maximum_fusion.1.rest_7_.rest_2_), channel_id=1, source_target_pairs={{0,4},{4,0},{8,12},{12,8},{16,20},{20,16},{24,28},{28,24},{1,5},{5... | collective-permute-start | bytes 98312 | tf_op jit(solution)/shard_map/ppermute | solution.py:423
  30.9 0.7 copy-start.2
  31.6 0.7 copy-start.3
  41.7 4.0 %collective-permute-start.8 = (bf16[4,128,1024]{2,1,0:T(8,128)(2,1)S(1)}, bf16[4,128,1024]{2,1,0:T(8,128)(2,1)S(1)}, u32[]{:S(2)}, u32[]{:S(2)}) collective-permute-start(bf16[4,128,1024]{2,1,0:T(8,128)(2,1)S(1)} %get-tuple-element.71), channel_id=1, source_target_pairs={{0,4},{4,0},{8,12},{12,8},{16,20},{20,16},{24,28},{28,24},{1,5},{5... | collective-permute-start | bytes 3145736 | tf_op jit(solution)/shard_map/ppermute | solution.py:423
  45.7 15.3 %collective-permute-start.16 = (bf16[128,1024]{1,0:T(8,128)(2,1)S(1)}, bf16[128,1024]{1,0:T(8,128)(2,1)S(1)}, u32[]{:S(2)}, u32[]{:S(2)}) collective-permute-start(bf16[128,1024]{1,0:T(8,128)(2,1)S(1)} %add_queries.2), channel_id=1, source_target_pairs={{0,2},{1,3},{2,0},{3,1},{4,6},{5,7},{6,4},{7,5},{8,10},{9,11},{10,... | collective-permute-start | bytes 786440 | tf_op jit(solution)/shard_map/ppermute | solution.py:426
  50.4 14.7 %collective-permute-start.9 = (bf16[528,256]{1,0:T(8,128)(2,1)S(1)}, bf16[528,256]{1,0:T(8,128)(2,1)S(1)}, u32[]{:S(2)}, u32[]{:S(2)}) collective-permute-start(bf16[528,256]{1,0:T(8,128)(2,1)S(1)} %get-tuple-element.76), channel_id=1, source_target_pairs={{0,8},{4,12},{8,0},{12,4},{16,24},{20,28},{24,16},{28,20},{1,9},{5... | collective-permute-start | bytes 811016 | tf_op jit(solution)/shard_map/ppermute | solution.py:423
  52.0 13.5 %collective-permute-start.10 = (bf16[528,256]{1,0:T(8,128)(2,1)S(1)}, bf16[528,256]{1,0:T(8,128)(2,1)S(1)}, u32[]{:S(2)}, u32[]{:S(2)}) collective-permute-start(bf16[528,256]{1,0:T(8,128)(2,1)S(1)} %get-tuple-element.77), channel_id=1, source_target_pairs={{0,16},{4,20},{8,24},{12,28},{16,0},{20,4},{24,8},{28,12},{1,17},{... | collective-permute-start | bytes 811016 | tf_op jit(solution)/shard_map/ppermute | solution.py:423
  52.2 13.3 %collective-permute-start.11 = (bf16[528,256]{1,0:T(8,128)(2,1)S(1)}, bf16[528,256]{1,0:T(8,128)(2,1)S(1)}, u32[]{:S(2)}, u32[]{:S(2)}) collective-permute-start(bf16[528,256]{1,0:T(8,128)(2,1)S(1)} %get-tuple-element.78), channel_id=1, source_target_pairs={{0,24},{4,28},{8,16},{12,20},{16,8},{20,12},{24,0},{28,4},{1,25},{... | collective-permute-start | bytes 811016 | tf_op jit(solution)/shard_map/ppermute | solution.py:423
  61.2 23.7 %collective-permute-start.17 = (bf16[128,1024]{1,0:T(8,128)(2,1)S(1)}, bf16[128,1024]{1,0:T(8,128)(2,1)S(1)}, u32[]{:S(2)}, u32[]{:S(2)}) collective-permute-start(bf16[128,1024]{1,0:T(8,128)(2,1)S(1)} %get-tuple-element.90), channel_id=1, source_target_pairs={{0,1},{1,2},{2,3},{3,0},{4,5},{5,6},{6,7},{7,4},{8,9},{9,10},{10,1... | collective-permute-start | bytes 786440 | tf_op jit(solution)/shard_map/ppermute | solution.py:426
  61.7 23.3 %collective-permute-start.18 = (bf16[128,1024]{1,0:T(8,128)(2,1)S(1)}, bf16[128,1024]{1,0:T(8,128)(2,1)S(1)}, u32[]{:S(2)}, u32[]{:S(2)}) collective-permute-start(bf16[128,1024]{1,0:T(8,128)(2,1)S(1)} %get-tuple-element.91), channel_id=1, source_target_pairs={{0,3},{1,0},{2,1},{3,2},{4,7},{5,4},{6,5},{7,6},{8,11},{9,8},{10,9... | collective-permute-start | bytes 786440 | tf_op jit(solution)/shard_map/ppermute | solution.py:426
  65.7 10.9 %collective-permute-start.12 = (bf16[144,256]{1,0:T(8,128)(2,1)S(1)}, bf16[144,256]{1,0:T(8,128)(2,1)S(1)}, u32[]{:S(2)}, u32[]{:S(2)}) collective-permute-start(bf16[144,256]{1,0:T(8,128)(2,1)S(1)} %get-tuple-element.80), channel_id=1, source_target_pairs={{0,3},{1,0},{2,1},{3,2},{4,7},{5,4},{6,5},{7,6},{8,11},{9,8},{10,9... | collective-permute-start | bytes 221192 | tf_op jit(solution)/shard_map/ppermute | solution.py:426
  71.0 12.0 %collective-permute-start.13 = (bf16[144,256]{1,0:T(8,128)(2,1)S(1)}, bf16[144,256]{1,0:T(8,128)(2,1)S(1)}, u32[]{:S(2)}, u32[]{:S(2)}) collective-permute-start(bf16[144,256]{1,0:T(8,128)(2,1)S(1)} %get-tuple-element.81), channel_id=1, source_target_pairs={{0,2},{1,3},{2,0},{3,1},{4,6},{5,7},{6,4},{7,5},{8,10},{9,11},{10,... | collective-permute-start | bytes 221192 | tf_op jit(solution)/shard_map/ppermute | solution.py:426
  71.0 12.0 %collective-permute-start.14 = (bf16[144,256]{1,0:T(8,128)(2,1)S(1)}, bf16[144,256]{1,0:T(8,128)(2,1)S(1)}, u32[]{:S(2)}, u32[]{:S(2)}) collective-permute-start(bf16[144,256]{1,0:T(8,128)(2,1)S(1)} %get-tuple-element.82), channel_id=1, source_target_pairs={{0,1},{1,2},{2,3},{3,0},{4,5},{5,6},{6,7},{7,4},{8,9},{9,10},{10,1... | collective-permute-start | bytes 221192 | tf_op jit(solution)/shard_map/ppermute | solution.py:426
  83.8 1.2 %collective-permute-start.15 = (f32[2,512]{1,0:T(2,128)S(1)}, f32[2,512]{1,0:T(2,128)S(1)}, u32[]{:S(2)}, u32[]{:S(2)}) collective-permute-start(f32[2,512]{1,0:T(2,128)S(1)} %get-tuple-element.83.gains_ref), channel_id=1, source_target_pairs={{0,4},{4,0},{8,12},{12,8},{16,20},{20,16},{24,28},{28,24},{1,5},{5... | collective-permute-start | bytes 12296 | tf_op jit(solution)/shard_map/ppermute | solution.py:423
